TPU v7x, 32 devices: a whole 2x2x4 slice. The times are simulated.
32 devices in a mesh: dp: 8 (over y, x, core), tensor: 4 (over z).
Axes of the slice: x: 2, y: 2, z: 4, core: 2. Of those that a mesh axis runs over, the one named last changes fastest.
Arguments:
- block_input: bfloat16 [2, 8192, 2048], P(None, ('dp', 'tensor')), may hold values from -6 to 6
- segment_ids: int32 [2, 8192], P(None, 'dp'), may hold values from 0 to 63, never falling along the last dimension, each value on 1 to 1024 neighbouring positions
- out_cotangent: bfloat16 [2, 8192, 2048], P(None, ('dp', 'tensor')), may hold values from -6 to 6
- norm1_gain: float32 [2048], replicated, may hold values from 0.5 to 1.5
- query_weight: bfloat16 [2048, 2048], P(None, 'tensor'), may hold values from -0.125 to 0.125
- key_weight: bfloat16 [2048, 2048], P(None, 'tensor'), may hold values from -0.125 to 0.125
- value_weight: bfloat16 [2048, 4096], P(None, 'tensor'), may hold values from -0.125 to 0.125
- gate_weight: bfloat16 [2048, 4096], P(None, 'tensor'), may hold values from -0.125 to 0.125
- decay_weight: bfloat16 [2048, 2, 16], P(None, None, 'tensor'), may hold values from -0.125 to 0.125
- conv_query: float32 [4, 2048], P(None, 'tensor'), may hold values from -2 to 2
- conv_key: float32 [4, 2048], P(None, 'tensor'), may hold values from -2 to 2
- conv_value: float32 [4, 4096], P(None, 'tensor'), may hold values from -2 to 2
- decay_log: float32 [16], P('tensor'), may hold values from -6 to 0
- decay_bias: float32 [16], P('tensor'), may hold values from -2 to 1
- output_gain: float32 [256], replicated, may hold values from 0.5 to 1.5
- output_weight: bfloat16 [4096, 2048], P('tensor'), may hold values from -0.1875 to 0.1875
- norm2_gain: float32 [2048], replicated, may hold values from 0.5 to 1.5
- ffn_gate: bfloat16 [2048, 5632], P(None, 'tensor'), may hold values from -0.125 to 0.125
- ffn_up: bfloat16 [2048, 5632], P(None, 'tensor'), may hold values from -0.125 to 0.125
- ffn_down: bfloat16 [5632, 2048], P('tensor'), may hold values from -0.109375 to 0.109375
Outputs:
- block_output: bfloat16 [2, 8192, 2048], P(None, ('dp', 'tensor'))
- input_grad: bfloat16 [2, 8192, 2048], P(None, ('dp', 'tensor'))
- grad_norm1_gain: float32 [2048], replicated
- grad_query_weight: float32 [2048, 2048], P(None, 'tensor')
- grad_key_weight: float32 [2048, 2048], P(None, 'tensor')
- grad_value_weight: float32 [2048, 4096], P(None, 'tensor')
- grad_gate_weight: float32 [2048, 4096], P(None, 'tensor')
- grad_decay_weight: float32 [2048, 2, 16], P(None, None, 'tensor')
- grad_conv_query: float32 [4, 2048], P(None, 'tensor')
- grad_conv_key: float32 [4, 2048], P(None, 'tensor')
- grad_conv_value: float32 [4, 4096], P(None, 'tensor')
- grad_decay_log: float32 [16], P('tensor')
- grad_decay_bias: float32 [16], P('tensor')
- grad_output_gain: float32 [256], replicated
- grad_output_weight: float32 [4096, 2048], P('tensor')
- grad_norm2_gain: float32 [2048], replicated
- grad_ffn_gate: float32 [2048, 5632], P(None, 'tensor')
- grad_ffn_up: float32 [2048, 5632], P(None, 'tensor')
- grad_ffn_down: float32 [5632, 2048], P('tensor')
Inputs may be any that keep to these rules, and one draw needn't show every extreme that they name: `segment_ids`: ids never fall along a row; each document takes 1 to 1024 consecutive positions and one takes exactly 1024.
All inputs are finite; a program needn't handle non-finite values.
Results may differ from a plain program's by a relative error of at most 0.015.
Values may be sent and summed in bfloat16 or wider, within the bound.
No kernel may reach another device: no remote copies, remote signals or barrier semaphores. Data moves between devices by JAX's collectives and lax.ppermute only.
A program may use at most 768 MiB of HBM per device.

v0:
```python
import jax
import jax.numpy as jnp
from jax import lax
from jax.sharding import PartitionSpec as P

SPAN = 64


def rms_norm(values, gain_vec):
    return values * lax.rsqrt(jnp.mean(values * values, axis=-1, keepdims=True) + 1e-05) * gain_vec


def unit_rows(values):
    return values * lax.rsqrt(jnp.sum(values * values, axis=-1, keepdims=True) + 1e-06)


def causal_conv(values, weights, segments):
    length = values.shape[0]
    summed = weights[0] * values
    for offset in range(1, weights.shape[0]):
        shifted = jnp.concatenate(
            [jnp.zeros((offset, values.shape[1]), jnp.float32), values[: length - offset]], axis=0
        )
        linked = jnp.concatenate(
            [
                jnp.zeros((offset,), jnp.float32),
                (segments[offset:] == segments[: length - offset]).astype(jnp.float32),
            ]
        )
        summed = summed + weights[offset] * shifted * linked[:, None]
    return jax.nn.silu(summed)


def delta_rule(query_rows, key_rows, value_rows, beta_gate, decays, segments):
    length, head_count, key_size = query_rows.shape
    value_size = value_rows.shape[2]
    blocks = length // SPAN
    position = jnp.arange(SPAN)
    on_or_below = position[:, None] >= position[None, :]
    strict = position[:, None] > position[None, :]
    identity = jnp.eye(SPAN, dtype=jnp.float32)
    highest = lax.Precision.HIGHEST

    def advance(state_pair, inputs):
        memory, previous = state_pair
        q_blk, k_blk, v_blk, b_blk, d_blk, s_blk = inputs
        cum_decay = jnp.cumsum(d_blk, axis=0)
        same_doc = s_blk[:, None] == s_blk[None, :]
        log_gaps = cum_decay[:, None, :] - cum_decay[None, :, :]
        within = jnp.transpose(
            jnp.exp(jnp.where((same_doc & on_or_below)[:, :, None], log_gaps, -1e30)), (2, 0, 1)
        )
        before = jnp.transpose(
            jnp.exp(jnp.where((same_doc & strict)[:, :, None], log_gaps, -1e30)), (2, 0, 1)
        )
        carried = (s_blk == previous).astype(jnp.float32)
        growth = jnp.exp(cum_decay) * carried[:, None]
        key_key = jnp.einsum("ihd,jhd->hij", k_blk, k_blk, precision=highest)
        query_key = jnp.einsum("ihd,jhd->hij", q_blk, k_blk, precision=highest)
        key_state = jnp.einsum("ihd,hde->hie", k_blk, memory, precision=highest)
        query_state = jnp.einsum("ihd,hde->hie", q_blk, memory, precision=highest)
        beta_col = jnp.transpose(b_blk)[:, :, None]
        growth_col = jnp.transpose(growth)[:, :, None]
        system = identity + beta_col * key_key * before
        target = beta_col * (jnp.transpose(v_blk, (1, 0, 2)) - growth_col * key_state)
        solved = lax.linalg.triangular_solve(system, target, left_side=True, lower=True)
        output = growth_col * query_state + jnp.einsum(
            "hij,hje->hie", query_key * within, solved, precision=highest
        )
        last_row = within[:, SPAN - 1, :]
        memory_next = growth[SPAN - 1][:, None, None] * memory + jnp.einsum(
            "jhd,hj,hje->hde", k_blk, last_row, solved, precision=highest
        )
        return ((memory_next, s_blk[SPAN - 1]), jnp.transpose(output, (1, 0, 2)))

    def to_blocks(array):
        return array.reshape((blocks, SPAN) + array.shape[1:])

    start_pair = (
        jnp.zeros((head_count, key_size, value_size), jnp.float32),
        jnp.array(-1, dtype=jnp.int32),
    )
    inputs = (
        to_blocks(query_rows),
        to_blocks(key_rows),
        to_blocks(value_rows),
        to_blocks(beta_gate),
        to_blocks(decays),
        to_blocks(segments),
    )
    unused, outputs = lax.scan(advance, start_pair, inputs)
    return outputs.reshape(length, head_count, value_size)


def mixer_core(
    projected, segments, conv_query, conv_key, conv_value, decay_log, decay_bias, output_gain
):
    length = projected.shape[0]
    head_count = decay_log.shape[0]
    qk_cols = conv_query.shape[1]
    v_cols = conv_value.shape[1]
    key_size = qk_cols // head_count
    value_size = v_cols // head_count
    query_rows = causal_conv(projected[:, :qk_cols], conv_query, segments).reshape(
        length, head_count, key_size
    )
    key_rows = causal_conv(projected[:, qk_cols : 2 * qk_cols], conv_key, segments).reshape(
        length, head_count, key_size
    )
    value_rows = causal_conv(
        projected[:, 2 * qk_cols : 2 * qk_cols + v_cols], conv_value, segments
    ).reshape(length, head_count, value_size)
    gating = projected[:, 2 * qk_cols + v_cols : 2 * qk_cols + 2 * v_cols].reshape(
        length, head_count, value_size
    )
    rate_col = 2 * qk_cols + 2 * v_cols
    rate_in = projected[:, rate_col : rate_col + head_count]
    beta_in = projected[:, rate_col + head_count : rate_col + 2 * head_count]
    query_rows = unit_rows(query_rows) * key_size ** (-0.5)
    key_rows = unit_rows(key_rows)
    beta_gate = jax.nn.sigmoid(beta_in)
    decays = -jnp.exp(decay_log) * jax.nn.softplus(rate_in + decay_bias)
    mixed_out = delta_rule(query_rows, key_rows, value_rows, beta_gate, decays, segments)
    mixed_out = rms_norm(mixed_out, output_gain) * jax.nn.silu(gating)
    return mixed_out.reshape(length, v_cols)


def contract_rows(left, right):
    return lax.dot_general(
        left, right, (((0,), (0,)), ((), ())), preferred_element_type=jnp.float32
    )


def contract_cols(left, right):
    return lax.dot_general(
        left, right, (((1,), (1,)), ((), ())), preferred_element_type=jnp.float32
    )


def body(
    block_input,
    segment_ids,
    out_cotangent,
    norm1_gain,
    query_weight,
    key_weight,
    value_weight,
    gate_weight,
    decay_weight,
    conv_query,
    conv_key,
    conv_value,
    decay_log,
    decay_bias,
    output_gain,
    output_weight,
    norm2_gain,
    ffn_gate,
    ffn_up,
    ffn_down,
):
    batch_count, slice_rows, width = block_input.shape
    head_count = decay_log.shape[0]
    qk_cols = query_weight.shape[1]
    v_cols = value_weight.shape[1]
    ffn_cols = ffn_gate.shape[1]
    proj_all = jnp.concatenate(
        [
            query_weight,
            key_weight,
            value_weight,
            gate_weight,
            decay_weight.reshape(width, 2 * head_count),
        ],
        axis=1,
    )
    ffn_both = jnp.concatenate([ffn_gate, ffn_up], axis=1)
    proj_cols = proj_all.shape[1]
    core_params = (conv_query, conv_key, conv_value, decay_log, decay_bias, output_gain)
    grad_proj = jnp.zeros((width, proj_cols), jnp.float32)
    grad_ffn = jnp.zeros((width, 2 * ffn_cols), jnp.float32)
    grad_down = jnp.zeros((ffn_cols, width), jnp.float32)
    grad_out = jnp.zeros((v_cols, width), jnp.float32)
    grad_core = tuple((jnp.zeros(param.shape, jnp.float32) for param in core_params))
    grad_first_gain = jnp.zeros((width,), jnp.float32)
    grad_second_gain = jnp.zeros((width,), jnp.float32)
    mixed_rows = []
    input_rows = []
    for batch_no in range(batch_count):
        x_rows = block_input[batch_no].astype(jnp.float32)
        seg_rows = segment_ids[batch_no]
        normed, first_back = jax.vjp(rms_norm, x_rows, norm1_gain)
        normed_full = lax.all_gather(normed.astype(jnp.bfloat16), "tensor", axis=0, tiled=True)
        projected = jnp.dot(normed_full, proj_all, preferred_element_type=jnp.float32)

        def core_call(proj_in, params_in):
            return mixer_core(
                proj_in,
                seg_rows,
                params_in[0],
                params_in[1],
                params_in[2],
                params_in[3],
                params_in[4],
                params_in[5],
            )

        mixed_out, core_back = jax.vjp(core_call, projected, core_params)
        mixed_low = mixed_out.astype(jnp.bfloat16)
        branch = lax.psum_scatter(
            jnp.dot(mixed_low, output_weight, preferred_element_type=jnp.float32),
            "tensor",
            scatter_dimension=0,
            tiled=True,
        )
        residual = x_rows + branch
        ffn_input, second_back = jax.vjp(rms_norm, residual, norm2_gain)
        ffn_full = lax.all_gather(ffn_input.astype(jnp.bfloat16), "tensor", axis=0, tiled=True)
        gate_up = jnp.dot(ffn_full, ffn_both, preferred_element_type=jnp.float32)
        gate_pre = gate_up[:, :ffn_cols]
        up_pre = gate_up[:, ffn_cols:]
        sig_gate = jax.nn.sigmoid(gate_pre)
        silu_gate = gate_pre * sig_gate
        hidden = (silu_gate * up_pre).astype(jnp.bfloat16)
        ffn_out = lax.psum_scatter(
            jnp.dot(hidden, ffn_down, preferred_element_type=jnp.float32).astype(jnp.bfloat16),
            "tensor",
            scatter_dimension=0,
            tiled=True,
        ).astype(jnp.float32)
        mixed_rows.append((residual + ffn_out).astype(jnp.bfloat16))
        rows_in = lax.all_gather(out_cotangent[batch_no], "tensor", axis=0, tiled=True)
        down_sum = contract_rows(hidden, rows_in)
        hidden_grad = contract_cols(rows_in, ffn_down)
        down_part, hidden_grad = (down_sum, hidden_grad)
        grad_down = grad_down + down_part
        gate_grad = hidden_grad * up_pre * sig_gate * (1.0 + gate_pre * (1.0 - sig_gate))
        up_grad = hidden_grad * silu_gate
        gate_up_grad = jnp.concatenate([gate_grad, up_grad], axis=1).astype(jnp.bfloat16)
        grad_ffn = grad_ffn + contract_rows(ffn_full, gate_up_grad)
        ffn_input_grad = lax.psum_scatter(
            contract_cols(gate_up_grad, ffn_both), "tensor", scatter_dimension=0, tiled=True
        )
        residual_part, second_gain_part = second_back(ffn_input_grad)
        grad_second_gain = grad_second_gain + second_gain_part
        residual_grad = out_cotangent[batch_no].astype(jnp.float32) + residual_part
        mixer_rows_in = lax.all_gather(
            residual_grad.astype(jnp.bfloat16), "tensor", axis=0, tiled=True
        )
        out_sum = contract_rows(mixed_low, mixer_rows_in)
        mixed_grad = contract_cols(mixer_rows_in, output_weight)
        out_part, mixed_grad = (out_sum, mixed_grad)
        grad_out = grad_out + out_part
        proj_grad, params_grad = core_back(mixed_grad)
        grad_core = tuple((total + part for total, part in zip(grad_core, params_grad)))
        proj_grad_low = proj_grad.astype(jnp.bfloat16)
        grad_proj = grad_proj + contract_rows(normed_full, proj_grad_low)
        normed_grad = lax.psum_scatter(
            contract_cols(proj_grad_low, proj_all).astype(jnp.bfloat16),
            "tensor",
            scatter_dimension=0,
            tiled=True,
        ).astype(jnp.float32)
        x_part, first_gain_part = first_back(normed_grad)
        grad_first_gain = grad_first_gain + first_gain_part
        input_rows.append((residual_grad + x_part).astype(jnp.bfloat16))
    summed_all = lax.psum(
        (
            grad_proj,
            grad_out,
            grad_core[0],
            grad_core[1],
            grad_core[2],
            grad_core[3],
            grad_core[4],
            grad_ffn,
            grad_down,
        ),
        "dp",
    )
    grad_proj, grad_out, grad_cq, grad_ck, grad_cv, grad_dlog, grad_dbias, grad_ffn, grad_down = (
        summed_all
    )
    gain_sums = lax.psum((grad_first_gain, grad_second_gain, grad_core[5]), ("dp", "tensor"))
    rate_col = 2 * qk_cols + 2 * v_cols
    return (
        jnp.stack(mixed_rows, axis=0),
        jnp.stack(input_rows, axis=0),
        gain_sums[0],
        grad_proj[:, :qk_cols],
        grad_proj[:, qk_cols : 2 * qk_cols],
        grad_proj[:, 2 * qk_cols : 2 * qk_cols + v_cols],
        grad_proj[:, 2 * qk_cols + v_cols : rate_col],
        grad_proj[:, rate_col:].reshape(width, 2, head_count),
        grad_cq,
        grad_ck,
        grad_cv,
        grad_dlog,
        grad_dbias,
        gain_sums[2],
        grad_out,
        gain_sums[1],
        grad_ffn[:, :ffn_cols],
        grad_ffn[:, ffn_cols:],
        grad_down,
    )


def solution(mesh):
    in_specs = (
        P(None, ("dp", "tensor"), None),
        P(None, "dp"),
        P(None, ("dp", "tensor"), None),
        P(),
        P(None, "tensor"),
        P(None, "tensor"),
        P(None, "tensor"),
        P(None, "tensor"),
        P(None, None, "tensor"),
        P(None, "tensor"),
        P(None, "tensor"),
        P(None, "tensor"),
        P("tensor"),
        P("tensor"),
        P(),
        P("tensor", None),
        P(),
        P(None, "tensor"),
        P(None, "tensor"),
        P("tensor", None),
    )
    out_specs = (
        P(None, ("dp", "tensor"), None),
        P(None, ("dp", "tensor"), None),
        P(),
        P(None, "tensor"),
        P(None, "tensor"),
        P(None, "tensor"),
        P(None, "tensor"),
        P(None, None, "tensor"),
        P(None, "tensor"),
        P(None, "tensor"),
        P(None, "tensor"),
        P("tensor"),
        P("tensor"),
        P(),
        P("tensor", None),
        P(),
        P(None, "tensor"),
        P(None, "tensor"),
        P("tensor", None),
    )
    return jax.shard_map(body, mesh=mesh, in_specs=in_specs, out_specs=out_specs, check_vma=False)
```

profile of v0, /device:TPU:0, one launch (start us, length us, event | category | flops | bytes accessed | tf_op | source)
XLA Modules:
  0.0 5990.7 jit_solution(17691132138725051429)
XLA Ops:
  28.8 66.9 %all-gather.15.cloned.1.call-done = bf16[1024,2048]{1,0:T(8,128)(2,1)} async-done(((bf16[256,2048]{1,0:T(8,128)(2,1)}), bf16[1024,2048]{1,0:T(8,128)(2,1)}) %all-gather.15.cloned.1.call-update) | async-done | bytes 4194320 | tf_op jit(solution)/shard_map/all_gather | solution.py:193
  95.7 27.6 fusion.461
  137.7 39.5 all-gather.11.cloned.1.call-done
  177.2 27.7 fusion.458
  258.6 20.3 fusion.356
  335.9 631.3 %while.177 = (s32[]{:T(128)}, f32[4,128,256]{2,1,0:T(8,128)S(1)}, s32[]{:T(128)}, f32[16,64,4,256]{3,1,2,0:T(8,128)}, pred[16,64,64,4]{2,3,1,0:T(4,128)(4,1)}, /...) while((s32[]{:T(128)}, f32[4,128,256]{2,1,0:T(8,128)S(1)}, ...), condition=%wide.region_15.18_spmd.clone, body=%wide.region_13.17_spmd.clone.sunk | while | flops 454787840 | bytes 9994402 | solution.py:91
  339.7 19.7 custom-call.31
  379.2 19.7 custom-call.31
  418.7 19.7 custom-call.31
  458.1 19.7 custom-call.31
  497.5 19.7 custom-call.31
  537.1 19.7 custom-call.31
  576.6 19.7 custom-call.31
  616.0 19.7 custom-call.31
  655.4 19.7 custom-call.31
  694.9 19.7 custom-call.31
  734.3 19.7 custom-call.31
  773.7 19.7 custom-call.31
  852.7 19.7 custom-call.31
  892.2 19.7 custom-call.31
  931.6 19.7 custom-call.31
  1103.5 596.8 %while.176 = (s32[]{:T(128)}, f32[4,128,256]{2,1,0:T(8,128)S(1)}, s32[]{:T(128)}, f32[16,64,4,256]{3,1,2,0:T(8,128)}, pred[16,64,64,4]{2,3,1,0:T(4,128)(4,1)}, /...) while((s32[]{:T(128)}, f32[4,128,256]{2,1,0:T(8,128)S(1)}, ...), condition=%wide.region_5.8_spmd.clone, body=%wide.region_3.7_spmd.clone.sunk | while | flops 454787840 | bytes 9995430 | solution.py:91
  1105.8 19.7 custom-call.30
  1180.3 19.7 custom-call.30
  1217.6 19.7 custom-call.30
  1254.9 19.7 custom-call.30
  1292.2 19.7 custom-call.30
  1329.5 19.7 custom-call.30
  1366.8 19.7 custom-call.30
  1404.1 19.7 custom-call.30
  1441.4 19.7 custom-call.30
  1478.7 19.7 custom-call.30
  1516.0 19.7 custom-call.30
  1553.3 19.7 custom-call.30
  1590.6 19.7 custom-call.30
  1627.9 19.7 custom-call.30
  1665.3 19.7 custom-call.30
  1734.5 142.7 %reduce-scatter.9.cloned.1.call-done = f32[256,2048]{1,0:T(8,128)} async-done(((f32[1024,2048]{1,0:T(8,128)}), f32[256,2048]{1,0:T(8,128)}) %reduce-scatter.9.cloned.1.call-update) | async-done | bytes 2097168 | tf_op jit(solution)/shard_map/reduce_scatter | solution.py:210
  1897.9 67.7 %all-gather.13.cloned.1.call-done = bf16[1024,2048]{1,0:T(8,128)(2,1)} async-done(((bf16[256,2048]{1,0:T(8,128)(2,1)}), bf16[1024,2048]{1,0:T(8,128)(2,1)}) %all-gather.13.cloned.1.call-update) | async-done | bytes 4194320 | tf_op jit(solution)/shard_map/all_gather | solution.py:218
  1984.2 62.1 %all-gather.23.cloned.1.call-done = bf16[1,1024,2048]{2,1,0:T(8,128)(2,1)} async-done(((bf16[1,256,2048]{2,1,0:T(8,128)(2,1)}), bf16[1,1024,2048]{2,1,0:T(8,128)(2,1)}) %all-gather.23.cloned.1.call-update) | async-done | bytes 4194320 | tf_op jit(solution)/shard_map/all_gather | solution.py:232
  2082.0 143.1 %reduce-scatter.17.cloned.1.call-done = f32[256,2048]{1,0:T(8,128)} async-done(((f32[1024,2048]{1,0:T(8,128)}), f32[256,2048]{1,0:T(8,128)}) %reduce-scatter.17.cloned.1.call-update) | async-done | bytes 2097168 | tf_op jit(solution)/shard_map/reduce_scatter | solution.py:241
  2230.4 80.9 %all-gather.17.cloned.1.call-done = bf16[1024,2048]{1,0:T(8,128)(2,1)} async-done(((bf16[256,2048]{1,0:T(8,128)(2,1)}), bf16[1024,2048]{1,0:T(8,128)(2,1)}) %all-gather.17.cloned.1.call-update) | async-done | bytes 4194320 | tf_op jit(solution)/shard_map/all_gather | solution.py:218
  2330.3 61.9 %all-gather.25.cloned.1.call-done = bf16[1,1024,2048]{2,1,0:T(8,128)(2,1)} async-done(((bf16[1,256,2048]{2,1,0:T(8,128)(2,1)}), bf16[1,1024,2048]{2,1,0:T(8,128)(2,1)}) %all-gather.25.cloned.1.call-update) | async-done | bytes 4194320 | tf_op jit(solution)/shard_map/all_gather | solution.py:232
  2439.4 131.6 %reduce-scatter.21.cloned.1.call-done = f32[256,2048]{1,0:T(8,128)} async-done(((f32[1024,2048]{1,0:T(8,128)}), f32[256,2048]{1,0:T(8,128)}) %reduce-scatter.21.cloned.1.call-update) | async-done | bytes 2097168 | tf_op jit(solution)/shard_map/reduce_scatter | solution.py:241
  2574.3 77.1 %reduce-scatter.15.cloned.1.call-done = bf16[256,2048]{1,0:T(8,128)(2,1)} async-done(((bf16[1024,2048]{1,0:T(8,128)(2,1)}), bf16[256,2048]{1,0:T(8,128)(2,1)}) %reduce-scatter.15.cloned.1.call-update) | async-done | bytes 1048592 | tf_op jit(solution)/shard_map/reduce_scatter | solution.py:225
  2691.9 46.4 all-gather.19.cloned.1.call-done
  2759.4 59.9 %all-gather.21.cloned.1.call-done = bf16[1024,2048]{1,0:T(8,128)(2,1)} async-done(((bf16[256,2048]{1,0:T(8,128)(2,1)}), bf16[1024,2048]{1,0:T(8,128)(2,1)}) %all-gather.21.cloned.1.call-update) | async-done | bytes 4194320 | tf_op jit(solution)/shard_map/all_gather | solution.py:247
  2877.1 865.1 %while.179 = (s32[]{:T(128)}, f32[4,128,256]{2,1,0:T(8,128)S(1)}, f32[16,64,4,128]{3,1,2,0:T(8,128)}, f32[16,64,4,128]{3,1,2,0:T(8,128)}, f32[16,64,4,256]{3,1,2...) while((s32[]{:T(128)}, f32[4,128,256]{2,1,0:T(8,128)S(1)}, ...), condition=%wide.region_49.54_spmd.clone, body=%wide.region_40.53_spmd.clone.sunk | while | flops 921653248 | bytes 16545573 | solution.py:91
  2883.3 19.7 custom-call.33
  2937.4 19.7 custom-call.33
  2991.4 19.7 custom-call.33
  3045.4 19.7 custom-call.33
  3099.5 19.7 custom-call.33
  3153.6 19.7 custom-call.33
  3207.6 19.7 custom-call.33
  3762.8 903.1 %while.178 = (s32[]{:T(128)}, f32[4,128,256]{2,1,0:T(8,128)S(1)}, f32[16,64,4,128]{3,1,2,0:T(8,128)S(1)}, f32[16,64,4,128]{3,1,2,0:T(8,128)}, f32[16,64,4,256]{3...) while((s32[]{:T(128)}, f32[4,128,256]{2,1,0:T(8,128)S(1)}, ...), condition=%wide.region_32.37_spmd.clone, body=%wide.region_23.36_spmd.clone.sunk | while | flops 921653248 | bytes 16523101 | solution.py:91
  4859.3 21.7 convolution_convert_fusion
  4906.0 21.7 convolution_convert_fusion.1
  4981.9 21.0 convolution_add_fusion.13
  5002.9 25.7 fusion.428
  5041.8 28.7 convolution_add_fusion.12
  5071.7 24.7 all-reduce.81
  5099.8 39.0 all-reduce.80
  5151.1 747.8 %all-reduce.85.cloned.1.call-done = (f32[2048,3080]{0,1:T(8,128)}, f32[1024,2048]{1,0:T(8,128)}, f32[2048,2816]{1,0:T(8,128)}, f32[1408,2048]{1,0:T(8,128)}) async-done(((f32[2048,3080]{0,1:T(8,128)}, f32[1024,2048]{1,0:T(8,128)}, f32[2048,2816]{1,0:T(8,128)}, f32[1408,2048]{1,0:T(8,128)}), (f32[2048,3080]{0,1:T(8,128)}, f32[1024,2048]{1,0:T(8,128)}, f32[2048,2816]{1,0:T(8,128)}, ...) | async-done | bytes 68222992 | tf_op jit(solution)/shard_map/psum | solution.py:267
  (3146 shorter events, 3232.8 us)
Async XLA Ops:
  7.2 88.5 %all-gather.15.cloned.1.call-start = ((), (), s32[]{:S(2)}) async-start(), calls=%async_computation.12 | async-start | bytes 5242880 | tf_op jit(solution)/shard_map/all_gather | solution.py:193
  12.0 165.1 %all-gather.11.cloned.1.call-start = ((), (), s32[]{:S(2)}) async-start(), calls=%async_computation.8 | async-start | bytes 5242880 | tf_op jit(solution)/shard_map/all_gather | solution.py:193
  12.8 1721.7 %reduce-scatter.13.cloned.1.call-start = ((), (), s32[]{:S(2)}) async-start(), calls=%async_computation.13 | async-start | bytes 10485760 | tf_op jit(solution)/shard_map/reduce_scatter | solution.py:210
  13.2 1003.0 %copy-start.154 = (f32[1,512]{1,0:T(1,128)}, f32[1,512]{1,0:T(1,128)S(1)}, u32[]{:S(2)}) copy-start(f32[1,512]{1,0:T(1,128)S(1)} %get-tuple-element.3814) | copy-start | bytes 6148
  13.2 1003.0 %copy-start.164 = (f32[1,512]{1,0:T(1,128)}, f32[1,512]{1,0:T(1,128)S(1)}, u32[]{:S(2)}) copy-start(f32[1,512]{1,0:T(1,128)S(1)} %get-tuple-element.3815) | copy-start | bytes 6148
  13.2 1003.0 %copy-start.166 = (f32[1,512]{1,0:T(1,128)}, f32[1,512]{1,0:T(1,128)S(1)}, u32[]{:S(2)}) copy-start(f32[1,512]{1,0:T(1,128)S(1)} %get-tuple-element.3817) | copy-start | bytes 6148
  13.3 1003.0 %copy-start.168 = (f32[1,512]{1,0:T(1,128)}, f32[1,512]{1,0:T(1,128)S(1)}, u32[]{:S(2)}) copy-start(f32[1,512]{1,0:T(1,128)S(1)} %get-tuple-element.3816) | copy-start | bytes 6148
  13.3 245.2 %copy-start.143 = (f32[1024]{0:T(1024)}, f32[1024]{0:T(1024)S(1)}, u32[]{:S(2)}) copy-start(f32[1024]{0:T(1024)S(1)} %pad_convert_fusion) | copy-start | bytes 12292
  13.4 245.1 %copy-start.135 = (f32[1024]{0:T(1024)}, f32[1024]{0:T(1024)S(1)}, u32[]{:S(2)}) copy-start(f32[1024]{0:T(1024)S(1)} %pad_convert_fusion.1) | copy-start | bytes 12292
  13.5 245.0 %copy-start.137 = (f32[1024]{0:T(1024)}, f32[1024]{0:T(1024)S(1)}, u32[]{:S(2)}) copy-start(f32[1024]{0:T(1024)S(1)} %fusion.417) | copy-start | bytes 12292
  13.6 1002.7 %copy-start.133 = (f32[1024]{0:T(1024)}, f32[1024]{0:T(1024)S(1)}, u32[]{:S(2)}) copy-start(f32[1024]{0:T(1024)S(1)} %fusion.416) | copy-start | bytes 12292
  13.6 279.4 %copy-start.235 = (f32[4]{0:T(128)}, f32[4]{0:T(128)S(1)}, u32[]{:S(2)}) copy-start(f32[4]{0:T(128)S(1)} %exponential_negate_fusion) | copy-start | bytes 52
  13.7 1002.6 %copy-start.141 = (f32[1024]{0:T(1024)}, f32[1024]{0:T(1024)S(1)}, u32[]{:S(2)}) copy-start(f32[1024]{0:T(1024)S(1)} %pad_convert_fusion.2) | copy-start | bytes 12292
  16.0 1000.3 %copy-start.139 = (f32[1024]{0:T(1024)}, f32[1024]{0:T(1024)S(1)}, u32[]{:S(2)}) copy-start(f32[1024]{0:T(1024)S(1)} %pad_convert_fusion.3) | copy-start | bytes 12292
  16.0 210.9 %copy-start.174 = (f32[1,512]{1,0:T(1,128)}, f32[1,512]{1,0:T(1,128)S(1)}, u32[]{:S(2)}) copy-start(f32[1,512]{1,0:T(1,128)S(1)} %get-tuple-element.3820) | copy-start | bytes 6148
  16.0 1000.3 %copy-start.156 = (f32[1,512]{1,0:T(1,128)}, f32[1,512]{1,0:T(1,128)S(1)}, u32[]{:S(2)}) copy-start(f32[1,512]{1,0:T(1,128)S(1)} %get-tuple-element.3818) | copy-start | bytes 6148
  16.0 1000.3 %copy-start.170 = (f32[1,512]{1,0:T(1,128)}, f32[1,512]{1,0:T(1,128)S(1)}, u32[]{:S(2)}) copy-start(f32[1,512]{1,0:T(1,128)S(1)} %get-tuple-element.3819) | copy-start | bytes 6148
  16.1 1000.3 %copy-start.172 = (f32[1,512]{1,0:T(1,128)}, f32[1,512]{1,0:T(1,128)S(1)}, u32[]{:S(2)}) copy-start(f32[1,512]{1,0:T(1,128)S(1)} %get-tuple-element.3821) | copy-start | bytes 6148
  16.1 242.5 %copy-start.145 = (f32[1,1024]{1,0:T(1,128)}, f32[1,1024]{1,0:T(1,128)S(1)}, u32[]{:S(2)}) copy-start(f32[1,1024]{1,0:T(1,128)S(1)} %get-tuple-element.3801) | copy-start | bytes 12292
  16.1 242.5 %copy-start.158 = (f32[1,1024]{1,0:T(1,128)}, f32[1,1024]{1,0:T(1,128)S(1)}, u32[]{:S(2)}) copy-start(f32[1,1024]{1,0:T(1,128)S(1)} %get-tuple-element.3802) | copy-start | bytes 12292
  16.1 242.5 %copy-start.160 = (f32[1,1024]{1,0:T(1,128)}, f32[1,1024]{1,0:T(1,128)S(1)}, u32[]{:S(2)}) copy-start(f32[1,1024]{1,0:T(1,128)S(1)} %get-tuple-element.3804) | copy-start | bytes 12292
  16.1 242.5 %copy-start.162 = (f32[1,1024]{1,0:T(1,128)}, f32[1,1024]{1,0:T(1,128)S(1)}, u32[]{:S(2)}) copy-start(f32[1,1024]{1,0:T(1,128)S(1)} %get-tuple-element.3803) | copy-start | bytes 12292
  234.9 23.5 copy-start.118
  979.0 23.3 copy-start.94
  983.0 33.3 copy-start.40
  994.5 67.3 %copy-start.124 = (f32[1024,4]{0,1:T(4,128)}, f32[1024,4]{0,1:T(4,128)S(1)}, u32[]{:S(2)}) copy-start(f32[1024,4]{0,1:T(4,128)S(1)} %get-tuple-element.3754) | copy-start | bytes 49156
  1016.2 861.1 %reduce-scatter.9.cloned.1.call-start = ((), (), s32[]{:S(2)}) async-start(), calls=%async_computation.9 | async-start | bytes 10485760 | tf_op jit(solution)/shard_map/reduce_scatter | solution.py:210
  1026.2 21.3 copy-start.120
  1734.4 142.8 %copy-start.2 = (bf16[2,256,2048]{2,1,0:T(8,128)(2,1)S(1)}, bf16[2,256,2048]{2,1,0:T(8,128)(2,1)}, u32[]{:S(2)}) copy-start(bf16[2,256,2048]{2,1,0:T(8,128)(2,1)} %param.35) | copy-start | bytes 6291460
  1734.4 148.3 %copy-start.102 = (f32[2048]{0:T(1024)S(1)}, f32[2048]{0:T(1024)}, u32[]{:S(2)}) copy-start(f32[2048]{0:T(1024)} %param.51) | copy-start | bytes 24580
  1734.5 231.1 %all-gather.13.cloned.1.call-start = ((), (), s32[]{:S(2)}) async-start(), calls=%async_computation.10 | async-start | bytes 5242880 | tf_op jit(solution)/shard_map/all_gather | solution.py:218
  1881.4 770.0 %copy-start.180 = (f32[256]{0:T(256)}, f32[256]{0:T(256)S(1)}, u32[]{:S(2)}) copy-start(f32[256]{0:T(256)S(1)} %fusion.419) | copy-start | bytes 3076
  1884.0 162.4 %all-gather.23.cloned.1.call-start = ((), (), s32[]{:S(2)}) async-start(), calls=%async_computation.22 | async-start | bytes 5242880 | tf_op jit(solution)/shard_map/all_gather | solution.py:232
  1886.2 338.9 %reduce-scatter.17.cloned.1.call-start = ((), (), s32[]{:S(2)}) async-start(), calls=%async_computation.16 | async-start | bytes 10485760 | tf_op jit(solution)/shard_map/reduce_scatter | solution.py:241
  2081.9 143.2 %copy-start.5 = (f32[256,2048]{1,0:T(8,128)S(1)}, f32[256,2048]{1,0:T(8,128)}, u32[]{:S(2)}) copy-start(f32[256,2048]{1,0:T(8,128)} %copy-done.4) | copy-start | bytes 6291460
  2081.9 229.3 %all-gather.17.cloned.1.call-start = ((), (), s32[]{:S(2)}) async-start(), calls=%async_computation.14 | async-start | bytes 5242880 | tf_op jit(solution)/shard_map/all_gather | solution.py:218
  2082.0 569.4 %copy-start.182 = (f32[256]{0:T(256)}, f32[256]{0:T(256)S(1)}, u32[]{:S(2)}) copy-start(f32[256]{0:T(256)S(1)} %fusion.421) | copy-start | bytes 3076
  2229.6 162.5 %all-gather.25.cloned.1.call-start = ((), (), s32[]{:S(2)}) async-start(), calls=%async_computation.23 | async-start | bytes 5242880 | tf_op jit(solution)/shard_map/all_gather | solution.py:232
  2230.4 340.6 %reduce-scatter.21.cloned.1.call-start = ((), (), s32[]{:S(2)}) async-start(), calls=%async_computation.19 | async-start | bytes 10485760 | tf_op jit(solution)/shard_map/reduce_scatter | solution.py:241
  2427.8 223.6 %reduce-scatter.15.cloned.1.call-start = ((), (), s32[]{:S(2)}) async-start(), calls=%async_computation.15 | async-start | bytes 5242880 | tf_op jit(solution)/shard_map/reduce_scatter | solution.py:225
  2438.8 299.6 %all-gather.19.cloned.1.call-start = ((), (), s32[]{:S(2)}) async-start(), calls=%async_computation.17 | async-start | bytes 5242880 | tf_op jit(solution)/shard_map/all_gather | solution.py:247
  2439.4 212.0 %copy-start.209 = (f32[256]{0:T(256)}, f32[256]{0:T(256)S(1)}, u32[]{:S(2)}) copy-start(f32[256]{0:T(256)S(1)} %multiply_multiply_fusion.11) | copy-start | bytes 3076
  2574.3 82.5 %copy-start.211 = (f32[256]{0:T(256)}, f32[256]{0:T(256)S(1)}, u32[]{:S(2)}) copy-start(f32[256]{0:T(256)S(1)} %multiply_multiply_fusion.9) | copy-start | bytes 3076
  2656.9 162.4 %all-gather.21.cloned.1.call-start = ((), (), s32[]{:S(2)}) async-start(), calls=%async_computation.20 | async-start | bytes 5242880 | tf_op jit(solution)/shard_map/all_gather | solution.py:247
  2657.6 2438.8 %reduce-scatter.23.cloned.1.call-start = ((), (), s32[]{:S(2)}) async-start(), calls=%async_computation.21 | async-start | bytes 5242880 | tf_op jit(solution)/shard_map/reduce_scatter | solution.py:258
  2840.3 18.4 copy-start.95
  2840.4 18.9 copy-start.97
  4767.2 92.1 %copy-start.192 = (f32[1024,4]{0,1:T(4,128)}, f32[1024,4]{0,1:T(4,128)S(1)}, u32[]{:S(2)}) copy-start(f32[1024,4]{0,1:T(4,128)S(1)} %fusion.403) | copy-start | bytes 49156
  4768.8 90.4 %copy-start.194 = (f32[1024,4]{0,1:T(4,128)}, f32[1024,4]{0,1:T(4,128)S(1)}, u32[]{:S(2)}) copy-start(f32[1024,4]{0,1:T(4,128)S(1)} %get-tuple-element.3733) | copy-start | bytes 49156
  4881.0 215.5 %reduce-scatter.19.cloned.1.call-start = ((), (), s32[]{:S(2)}) async-start(), calls=%async_computation.18 | async-start | bytes 5242880 | tf_op jit(solution)/shard_map/reduce_scatter | solution.py:258
  4881.9 17.5 copy-start.15
  4881.9 18.2 copy-start.61
  4927.8 216.3 %reduce-scatter.11.cloned.1.call-start = ((), (), s32[]{:S(2)}) async-start(), calls=%async_computation.11 | async-start | bytes 5242880 | tf_op jit(solution)/shard_map/reduce_scatter | solution.py:225
  4940.4 958.5 %all-reduce.85.cloned.1.call-start = ((), (), s32[]{:S(2)}) async-start(), calls=%async_computation.24 | async-start | bytes 136445952 | tf_op jit(solution)/shard_map/psum | solution.py:267
  5002.9 25.7 copy-start.86
  5070.9 25.6 copy-start.3
  5070.9 25.6 copy-start.130
  5070.9 25.6 copy-start.198
  5070.9 25.6 copy-start.200
  5096.4 42.4 copy-start.202
  5096.4 42.4 copy-start.204
  5096.4 42.4 copy-start.103
  5096.4 42.4 copy-start.183
  5096.4 42.4 copy-start.212
  (246 other events, 1438.6 us)
Sparse Core Ops, SparseCore 0:
  12.1 83.5 all-gather.14
  97.8 79.2 all-gather.10
  1016.3 143.0 reduce-scatter.12
  1734.6 142.6 reduce-scatter.8
  1884.1 81.4 all-gather.12
  1967.0 79.2 all-gather.22
  2082.1 143.0 reduce-scatter.16
  2229.7 81.4 all-gather.16
  2312.8 79.2 all-gather.24
  2427.9 143.0 reduce-scatter.20
  2573.9 77.4 reduce-scatter.14
  2657.0 81.2 all-gather.18
  2740.0 79.2 all-gather.20
  4881.2 75.2 reduce-scatter.22
  4959.2 77.2 reduce-scatter.18
  5039.3 77.2 reduce-scatter.10
  5121.8 777.0 all-reduce.84
where the time goes:
time: 6030 us; the launch traced here: 5990 us
  other arithmetic  1810 us (30%)
  waiting for transfers between devices  1730 us (29%)
  matrix products  1500 us (25%)
  local copies, waits for them, and re-layouts  848 us (14%)
  blocking collectives  63.8 us (1%)
    another operation x128, other arithmetic, advance(): lax.linalg.triangular_solve(system, target, left_side=True, lower=True)  1290 us
    psum x1, waiting for transfers between devices, body(): lax.psum((grad_proj, grad_out, grad_core[0], grad_core[1], grad_core[2],...  748 us
    reduce_scatter x2, waiting for transfers between devices, body(): lax.psum_scatter(contract_cols(gate_up_grad, ffn_both), 'tensor', scatter...  275 us
    dot_general x96, matrix products, advance(): key_state = jnp.einsum('ihd,hde->hie', k_blk, memory, precision=highest)  202 us
    dot_general x96, matrix products, advance(): query_state = jnp.einsum('ihd,hde->hie', q_blk, memory, precision=highest)  172 us
    another operation x96, matrix products, advance(): lax.linalg.triangular_solve(system, target, left_side=True, lower=True)  162 us
    dot_general x96, matrix products, advance(): query_key = jnp.einsum('ihd,jhd->hij', q_blk, k_blk, precision=highest)  149 us
    all_gather x2, waiting for transfers between devices, body(): lax.all_gather(ffn_input.astype(jnp.bfloat16), 'tensor', axis=0, tiled=True)  149 us
  transfers between devices with their start and end apart: 17, of which 13 were waited for; matrix products, arithmetic and copies ran while one was open for 18% of the time, Pallas kernels for 0%

commit v1 on v0

v1 whole, which is shorter than its diff:
```python
import functools
import jax
import jax.numpy as jnp
from jax import lax
from jax.experimental import pallas as pl
from jax.experimental.pallas import tpu as pltpu
from jax.sharding import PartitionSpec as P

SPAN = 64
LANES = 128
HALO = 8
DK = 128
DV = 256
LOW = jnp.bfloat16
F32 = jnp.float32


def mm(left, right):
    return jnp.dot(left.astype(LOW), right.astype(LOW), preferred_element_type=F32)


def mm_tb(left, right):
    return lax.dot_general(
        left.astype(LOW), right.astype(LOW), (((1,), (1,)), ((), ())), preferred_element_type=F32
    )


def mm_ta(left, right):
    return lax.dot_general(
        left.astype(LOW), right.astype(LOW), (((0,), (0,)), ((), ())), preferred_element_type=F32
    )


def mm_exact(left, right):
    return jnp.dot(left, right, precision=lax.Precision.HIGHEST, preferred_element_type=F32)


def grid_pair(rows, cols):
    return (
        lax.broadcasted_iota(jnp.int32, (rows, cols), 0),
        lax.broadcasted_iota(jnp.int32, (rows, cols), 1),
    )


def lower_inverses(strict_lowers):
    row, col = grid_pair(SPAN, SPAN)
    eye = (row == col).astype(F32)
    size = 1
    inverses = None
    while size < SPAN:
        fresh = (row // (2 * size) == col // (2 * size)) & (row // size != col // size)
        parts = [jnp.where(fresh, lower, 0.0) for lower in strict_lowers]
        if size == 1:
            inverses = [eye - part for part in parts]
        else:
            lows = [inverse.astype(LOW) for inverse in inverses]
            firsts = [mm(part, low) for part, low in zip(parts, lows)]
            inverses = [
                inverse - mm(low, first) for inverse, low, first in zip(inverses, lows, firsts)
            ]
        size *= 2
    return inverses


def gates(small, params):
    rate = small + params[1:2, :]
    soft = jnp.maximum(rate, 0.0) + jnp.log1p(jnp.exp(-jnp.abs(rate)))
    return rate, params[0:1, :] * soft, jax.nn.sigmoid(small)


def decay_tables(decay, aux):
    row, col = grid_pair(SPAN, SPAN)
    running = mm_exact((row >= col).astype(F32), decay)
    lane = lax.broadcasted_iota(jnp.int32, (SPAN, LANES), 1)
    flipped = jnp.transpose(jnp.where(lane == LANES - 1, aux[:, 0:1], running))
    growth = jnp.exp(running) * aux[:, 1:2]
    tail = jnp.exp(jnp.where(aux[:, 2:3] > 0.0, running[SPAN - 1 : SPAN, :] - running, -1e30))
    keep = (aux[:, 0:1] == flipped[LANES - 1 : LANES, :]) & (row >= col)
    return running, flipped, growth, tail, keep


def conv_in(window_ref, start, width, taps, aux):
    total = taps[0:1, start : start + width] * window_ref[HALO : HALO + SPAN, start : start + width]
    for offset in range(1, 4):
        shifted = window_ref[HALO - offset : HALO - offset + SPAN, start : start + width]
        total = total + taps[offset : offset + 1, start : start + width] * (
            shifted * aux[:, 2 + offset : 3 + offset]
        )
    return total


def unit(values):
    return values * lax.rsqrt(jnp.sum(values * values, axis=-1, keepdims=True) + 1e-06)


def forward_kernel(
    heads, proj_ref, halo_ref, aux_ref, taps_ref, params_ref, gain_ref,
    mixed_ref, delta_ref, solved_ref, inverse_ref, entry_ref, memory_ref, window_ref,
):
    qk_cols, v_cols = heads * DK, heads * DV
    gate_at = 2 * qk_cols + v_cols
    small_at = gate_at + v_cols

    @pl.when(pl.program_id(0) == 0)
    def _():
        memory_ref[...] = jnp.zeros_like(memory_ref)

    window_ref[0:HALO, :] = halo_ref[:, 0:gate_at]
    window_ref[HALO : HALO + SPAN, :] = proj_ref[:, 0:gate_at]
    aux = aux_ref[...]
    taps = taps_ref[...]
    _, decay, writes = gates(proj_ref[:, small_at : small_at + LANES], params_ref[...])
    running, flipped, growth, tail, keep = decay_tables(decay, aux)
    row, col = grid_pair(SPAN, SPAN)
    each = range(heads)
    queries = [
        unit(jax.nn.silu(conv_in(window_ref, h * DK, DK, taps, aux))) * DK ** (-0.5) for h in each
    ]
    keys = [
        unit(jax.nn.silu(conv_in(window_ref, qk_cols + h * DK, DK, taps, aux))) for h in each
    ]
    boths = [
        jnp.concatenate([query.astype(LOW), key.astype(LOW)], axis=0)
        for query, key in zip(queries, keys)
    ]
    scores = [mm_tb(both, both[SPAN:]) for both in boths]
    withins = [
        jnp.exp(jnp.where(keep, running[:, h : h + 1] - flipped[h : h + 1, :], -1e30))
        for h in each
    ]
    betas = [writes[:, heads + h : heads + h + 1] for h in each]
    grows = [growth[:, h : h + 1] for h in each]
    inverses = lower_inverses(
        [
            betas[h] * scores[h][SPAN:] * jnp.where(row > col, withins[h], 0.0)
            for h in each
        ]
    )
    inverses = [inverse.astype(LOW) for inverse in inverses]
    memories = [memory_ref[h] for h in each]
    lows = [memory.astype(LOW) for memory in memories]
    reads = [mm(both, low) for both, low in zip(boths, lows)]
    values = [
        jax.nn.silu(conv_in(window_ref, 2 * qk_cols + h * DV, DV, taps, aux)) for h in each
    ]
    targets = [betas[h] * (values[h] - grows[h] * reads[h][SPAN:]) for h in each]
    solveds = [mm(inverses[h], targets[h]).astype(LOW) for h in each]
    updates = [mm_ta(tail[:, h : h + 1] * keys[h], solveds[h]) for h in each]
    deltas = [
        grows[h] * reads[h][:SPAN] + mm(scores[h][:SPAN] * withins[h], solveds[h]) for h in each
    ]
    for h in each:
        entry_ref[0, h] = lows[h]
        inverse_ref[0, h] = inverses[h]
        memory_ref[h] = grows[h][SPAN - 1 : SPAN, :] * memories[h] + updates[h]
        cols = slice(h * DV, (h + 1) * DV)
        delta = deltas[h]
        solved_ref[:, cols] = solveds[h]
        delta_ref[:, cols] = delta
        scaled = delta * lax.rsqrt(jnp.mean(delta * delta, axis=-1, keepdims=True) + 1e-05)
        gate = proj_ref[:, gate_at + h * DV : gate_at + (h + 1) * DV]
        mixed_ref[:, cols] = (scaled * gain_ref[0:1, :] * jax.nn.silu(gate)).astype(LOW)


def silu_back(values, grad):
    sig = jax.nn.sigmoid(values)
    return grad * sig * (1.0 + values * (1.0 - sig))


def fold(values):
    total = values[0:8]
    for part in range(1, values.shape[0] // 8):
        total = total + values[8 * part : 8 * part + 8]
    return total


def backward_kernel(
    heads, proj_ref, halo_ref, aux_ref, taps_ref, params_ref, gain_ref,
    delta_ref, solved_ref, inverse_ref, entry_ref, grad_ref,
    dproj_ref, dtaps_ref, dsmall_ref, dgain_ref, dmemory_ref, window_ref, later_ref,
):
    qk_cols, v_cols = heads * DK, heads * DV
    gate_at = 2 * qk_cols + v_cols
    small_at = gate_at + v_cols

    @pl.when(pl.program_id(0) == 0)
    def _():
        dmemory_ref[...] = jnp.zeros_like(dmemory_ref)
        later_ref[...] = jnp.zeros_like(later_ref)
        dtaps_ref[...] = jnp.zeros_like(dtaps_ref)
        dsmall_ref[...] = jnp.zeros_like(dsmall_ref)
        dgain_ref[...] = jnp.zeros_like(dgain_ref)

    window_ref[0:HALO, :] = halo_ref[:, 0:gate_at]
    window_ref[HALO : HALO + SPAN, :] = proj_ref[:, 0:gate_at]
    later_ref[SPAN : SPAN + HALO, :] = later_ref[0:HALO, :]
    aux = aux_ref[...]
    taps = taps_ref[...]
    small = proj_ref[:, small_at : small_at + LANES]
    rate, decay, writes = gates(small, params_ref[...])
    running, flipped, growth, tail, keep = decay_tables(decay, aux)
    row, col = grid_pair(SPAN, SPAN)
    lane = lax.broadcasted_iota(jnp.int32, (SPAN, LANES), 1)
    upper = (row <= col).astype(F32)
    behind = (row > col).astype(F32)
    dbeta_all = jnp.zeros((SPAN, LANES), F32)
    arrive_all = jnp.zeros((SPAN, LANES), F32)
    leave_all = jnp.zeros((SPAN, LANES), F32)
    direct_all = jnp.zeros((SPAN, LANES), F32)

    def conv_back(pre, grad, start, width):
        dpre = silu_back(pre, grad)
        later_ref[0:SPAN, start : start + width] = dpre
        total = taps[0:1, start : start + width] * dpre
        base = window_ref[HALO : HALO + SPAN, start : start + width]
        dtaps_ref[0:8, start : start + width] += fold(dpre * base)
        for offset in range(1, 4):
            ahead = later_ref[offset : offset + SPAN, start : start + width]
            total = total + taps[offset : offset + 1, start : start + width] * (
                ahead * aux[:, 5 + offset : 6 + offset]
            )
            shifted = window_ref[HALO - offset : HALO - offset + SPAN, start : start + width]
            dtaps_ref[8 * offset : 8 * offset + 8, start : start + width] += fold(
                dpre * (shifted * aux[:, 2 + offset : 3 + offset])
            )
        dproj_ref[:, start : start + width] = total.astype(LOW)

    each = range(heads)
    values_at = [slice(h * DV, (h + 1) * DV) for h in each]
    ddeltas = []
    for h in each:
        delta = delta_ref[:, values_at[h]]
        scale = lax.rsqrt(jnp.mean(delta * delta, axis=-1, keepdims=True) + 1e-05)
        scaled = delta * scale
        gate = proj_ref[:, gate_at + h * DV : gate_at + (h + 1) * DV]
        gsig = jax.nn.sigmoid(gate)
        dmixed = grad_ref[:, values_at[h]]
        gain = gain_ref[0:1, :]
        dproj_ref[:, gate_at + h * DV : gate_at + (h + 1) * DV] = (
            dmixed * scaled * gain * gsig * (1.0 + gate * (1.0 - gsig))
        ).astype(LOW)
        dnormed = dmixed * (gate * gsig)
        dgain_ref[...] += fold(dnormed * scaled)
        dnormed = dnormed * gain
        ddelta = scale * (
            dnormed - scaled * jnp.mean(scaled * dnormed, axis=-1, keepdims=True)
        )
        ddeltas.append(ddelta.astype(LOW))
    q_pres = [conv_in(window_ref, h * DK, DK, taps, aux) for h in each]
    k_pres = [conv_in(window_ref, qk_cols + h * DK, DK, taps, aux) for h in each]
    q_acts = [jax.nn.silu(pre) for pre in q_pres]
    k_acts = [jax.nn.silu(pre) for pre in k_pres]
    q_scales = [
        lax.rsqrt(jnp.sum(act * act, axis=-1, keepdims=True) + 1e-06) for act in q_acts
    ]
    k_scales = [
        lax.rsqrt(jnp.sum(act * act, axis=-1, keepdims=True) + 1e-06) for act in k_acts
    ]
    q_units = [act * scale for act, scale in zip(q_acts, q_scales)]
    keys = [act * scale for act, scale in zip(k_acts, k_scales)]
    queries = [unit_row * DK ** (-0.5) for unit_row in q_units]
    betas = [writes[:, heads + h : heads + h + 1] for h in each]
    grows = [growth[:, h : h + 1] for h in each]
    fades = [tail[:, h : h + 1] for h in each]
    withins = [
        jnp.exp(jnp.where(keep, running[:, h : h + 1] - flipped[h : h + 1, :], -1e30))
        for h in each
    ]
    key_lows = [key.astype(LOW) for key in keys]
    boths = [
        jnp.concatenate([query.astype(LOW), low], axis=0) for query, low in zip(queries, key_lows)
    ]
    scores = [mm_tb(both, low) for both, low in zip(boths, key_lows)]
    solveds = [solved_ref[:, values_at[h]] for h in each]
    entries = [entry_ref[0, h] for h in each]
    dmemories = [dmemory_ref[h] for h in each]
    dmemory_lows = [dmemory.astype(LOW) for dmemory in dmemories]
    leaving = [mm(low, dlow) for low, dlow in zip(key_lows, dmemory_lows)]
    dsolveds = [
        mm_ta(scores[h][:SPAN] * withins[h], ddeltas[h]) + fades[h] * leaving[h] for h in each
    ]
    dtargets = [mm_ta(inverse_ref[0, h], dsolveds[h]) for h in each]
    pairs = [
        jnp.concatenate([ddeltas[h], dtargets[h].astype(LOW)], axis=0) for h in each
    ]
    factors = [
        jnp.concatenate(
            [
                (grows[h] * queries[h]).astype(LOW),
                (-(betas[h] * grows[h]) * keys[h]).astype(LOW),
            ],
            axis=0,
        )
        for h in each
    ]
    flows = [mm_ta(factor, pair) for factor, pair in zip(factors, pairs)]
    carries = []
    for h in each:
        last = grows[h][SPAN - 1 : SPAN, :]
        carries.append(
            last * jnp.sum(dmemories[h] * entries[h].astype(F32), keepdims=True)
        )
        dmemory_ref[h] = last * dmemories[h] + flows[h]
    on_solveds = [mm_tb(pair, solved) for pair, solved in zip(pairs, solveds)]
    on_entries = [mm_tb(pair, entry) for pair, entry in zip(pairs, entries)]
    dkey_leaves = [
        fades[h] * mm_tb(solveds[h], dmemory_lows[h]) for h in each
    ]
    dscores = [on_solveds[h][:SPAN] * withins[h] for h in each]
    dsystems = [
        -on_solveds[h][SPAN:] * jnp.where(row > col, withins[h], 0.0) for h in each
    ]
    dsystem_betas = [betas[h] * dsystems[h] for h in each]
    duos = [
        jnp.concatenate([dscores[h].astype(LOW), dsystem_betas[h].astype(LOW)], axis=0)
        for h in each
    ]
    forths = [mm(duo, low) for duo, low in zip(duos, key_lows)]
    backs = [mm_ta(duo, both) for duo, both in zip(duos, boths)]
    spreads = [
        mm(upper, dscores[h] * scores[h][:SPAN] + dsystem_betas[h] * scores[h][SPAN:])
        for h in each
    ]
    for h in each:
        q_at, k_at, v_at = h * DK, qk_cols + h * DK, 2 * qk_cols + h * DV
        key, query, beta = keys[h], queries[h], betas[h]
        dquery_far = grows[h] * on_entries[h][:SPAN]
        dkey_far = grows[h] * on_entries[h][SPAN:]
        dquery = dquery_far + forths[h][:SPAN]
        dkey = forths[h][SPAN:] + backs[h] - beta * dkey_far + dkey_leaves[h]
        v_pre = conv_in(window_ref, v_at, DV, taps, aux)
        value = jax.nn.silu(v_pre)
        key_far = jnp.sum(key * dkey_far, axis=-1, keepdims=True)
        dbeta = (
            jnp.sum(dtargets[h] * value, axis=-1, keepdims=True)
            - key_far
            + jnp.sum(dsystems[h] * scores[h][SPAN:], axis=-1, keepdims=True)
        )
        arrive = jnp.sum(query * dquery_far, axis=-1, keepdims=True) - beta * key_far
        leave = jnp.sum(key * dkey_leaves[h], axis=-1, keepdims=True)
        direct = jnp.sum(spreads[h] * behind, axis=-1, keepdims=True) + carries[h]
        dbeta_all = jnp.where(lane == heads + h, dbeta, dbeta_all)
        arrive_all = jnp.where(lane == h, arrive, arrive_all)
        leave_all = jnp.where(lane == h, leave, leave_all)
        direct_all = jnp.where(lane == h, direct, direct_all)
        dq_unit = dquery * DK ** (-0.5)
        dq_act = q_scales[h] * (
            dq_unit - q_units[h] * jnp.sum(q_units[h] * dq_unit, axis=-1, keepdims=True)
        )
        dk_act = k_scales[h] * (dkey - key * jnp.sum(key * dkey, axis=-1, keepdims=True))
        conv_back(q_pres[h], dq_act, q_at, DK)
        conv_back(k_pres[h], dk_act, k_at, DK)
        conv_back(v_pre, beta * dtargets[h], v_at, DV)

    ddecay = direct_all + mm_exact(upper, arrive_all) + mm_exact(behind, leave_all)
    drate = ddecay * params_ref[0:1, :] * jax.nn.sigmoid(rate)
    dsmall_ref[0:8, :] += fold(ddecay * decay)
    dsmall_ref[8:16, :] += fold(drate)
    dproj_ref[:, small_at : small_at + LANES] = (
        drate + dbeta_all * writes * (1.0 - writes)
    ).astype(LOW)


def whole(shape):
    return pl.BlockSpec(shape, lambda step: (0,) * len(shape))


def mixer_forward(projected, aux, taps, params, gain, heads):
    rows, width = projected.shape
    v_cols = heads * DV
    conv_cols = taps.shape[1]
    blocks = rows // SPAN
    tall = SPAN // HALO
    return pl.pallas_call(
        functools.partial(forward_kernel, heads),
        grid=(blocks,),
        in_specs=[
            pl.BlockSpec((SPAN, width), lambda c: (c, 0)),
            pl.BlockSpec((HALO, width), lambda c: (jnp.maximum(c * tall - 1, 0), 0)),
            pl.BlockSpec((SPAN, LANES), lambda c: (c, 0)),
            whole(taps.shape),
            whole(params.shape),
            whole((8, DV)),
        ],
        out_specs=[
            pl.BlockSpec((SPAN, v_cols), lambda c: (c, 0)),
            pl.BlockSpec((SPAN, v_cols), lambda c: (c, 0)),
            pl.BlockSpec((SPAN, v_cols), lambda c: (c, 0)),
            pl.BlockSpec((1, heads, SPAN, SPAN), lambda c: (c, 0, 0, 0)),
            pl.BlockSpec((1, heads, DK, DV), lambda c: (c, 0, 0, 0)),
        ],
        out_shape=[
            jax.ShapeDtypeStruct((rows, v_cols), LOW),
            jax.ShapeDtypeStruct((rows, v_cols), F32),
            jax.ShapeDtypeStruct((rows, v_cols), LOW),
            jax.ShapeDtypeStruct((blocks, heads, SPAN, SPAN), LOW),
            jax.ShapeDtypeStruct((blocks, heads, DK, DV), LOW),
        ],
        scratch_shapes=[
            pltpu.VMEM((heads, DK, DV), F32),
            pltpu.VMEM((SPAN + HALO, conv_cols), F32),
        ],
        compiler_params=pltpu.CompilerParams(vmem_limit_bytes=40 << 20),
        cost_estimate=pl.CostEstimate(
            flops=rows, bytes_accessed=rows, transcendentals=0
        ),
        name="mixer_forward",
    )(projected, projected, aux, taps, params, gain)


def mixer_backward(projected, aux, taps, params, gain, saved, grad, heads):
    delta, solved, inverse, entry = saved
    rows, width = projected.shape
    v_cols = heads * DV
    conv_cols = taps.shape[1]
    blocks = rows // SPAN
    tall = SPAN // HALO
    last = blocks - 1
    return pl.pallas_call(
        functools.partial(backward_kernel, heads),
        grid=(blocks,),
        in_specs=[
            pl.BlockSpec((SPAN, width), lambda c: (last - c, 0)),
            pl.BlockSpec((HALO, width), lambda c: (jnp.maximum((last - c) * tall - 1, 0), 0)),
            pl.BlockSpec((SPAN, LANES), lambda c: (last - c, 0)),
            whole(taps.shape),
            whole(params.shape),
            whole((8, DV)),
            pl.BlockSpec((SPAN, v_cols), lambda c: (last - c, 0)),
            pl.BlockSpec((SPAN, v_cols), lambda c: (last - c, 0)),
            pl.BlockSpec((1, heads, SPAN, SPAN), lambda c: (last - c, 0, 0, 0)),
            pl.BlockSpec((1, heads, DK, DV), lambda c: (last - c, 0, 0, 0)),
            pl.BlockSpec((SPAN, v_cols), lambda c: (last - c, 0)),
        ],
        out_specs=[
            pl.BlockSpec((SPAN, width), lambda c: (last - c, 0)),
            whole((32, conv_cols)),
            whole((16, LANES)),
            whole((8, DV)),
        ],
        out_shape=[
            jax.ShapeDtypeStruct((rows, width), LOW),
            jax.ShapeDtypeStruct((32, conv_cols), F32),
            jax.ShapeDtypeStruct((16, LANES), F32),
            jax.ShapeDtypeStruct((8, DV), F32),
        ],
        scratch_shapes=[
            pltpu.VMEM((heads, DK, DV), F32),
            pltpu.VMEM((SPAN + HALO, conv_cols), F32),
            pltpu.VMEM((SPAN + HALO, conv_cols), F32),
        ],
        compiler_params=pltpu.CompilerParams(vmem_limit_bytes=48 << 20),
        cost_estimate=pl.CostEstimate(
            flops=rows, bytes_accessed=rows, transcendentals=0
        ),
        name="mixer_backward",
    )(projected, projected, aux, taps, params, gain, delta, solved, inverse, entry, grad)


def token_tables(segments):
    rows = segments.shape[0]
    seg = segments.astype(F32)
    blocked = seg.reshape(rows // SPAN, SPAN)
    ends = blocked[:, SPAN - 1]
    before = jnp.concatenate([jnp.full((1,), -1.0, F32), ends[:-1]])
    columns = [
        seg,
        (blocked == before[:, None]).astype(F32).reshape(rows),
        (blocked == ends[:, None]).astype(F32).reshape(rows),
    ]
    links = [(seg[offset:] == seg[:-offset]).astype(F32) for offset in range(1, 4)]
    columns += [jnp.pad(link, (offset, 0)) for offset, link in enumerate(links, 1)]
    columns += [jnp.pad(link, (0, offset)) for offset, link in enumerate(links, 1)]
    return jnp.pad(jnp.stack(columns, axis=1), ((0, 0), (0, LANES - len(columns))))


def rms_forward(values, gain_vec):
    scale = lax.rsqrt(jnp.mean(values * values, axis=-1, keepdims=True) + 1e-05)
    return values * scale * gain_vec


def rms_backward(values, gain_vec, grad):
    scale = lax.rsqrt(jnp.mean(values * values, axis=-1, keepdims=True) + 1e-05)
    scaled = values * scale
    inner = grad * gain_vec
    back = scale * (inner - scaled * jnp.mean(scaled * inner, axis=-1, keepdims=True))
    return back, jnp.sum(grad * scaled, axis=0)


def dot(left, right):
    return jnp.dot(left, right, preferred_element_type=F32)


def contract_rows(left, right):
    return lax.dot_general(
        left, right, (((0,), (0,)), ((), ())), preferred_element_type=F32
    )


def contract_cols(left, right):
    return lax.dot_general(
        left, right, (((1,), (1,)), ((), ())), preferred_element_type=F32
    )


def gather(rows):
    return lax.all_gather(rows, "tensor", axis=0, tiled=True)


def scatter(rows):
    return lax.psum_scatter(
        rows.astype(LOW), "tensor", scatter_dimension=0, tiled=True
    ).astype(F32)


def after(values, first):
    return lax.optimization_barrier((values, first))[0]


def make_body(parts, replicas):
    near = parts // 2
    teams = [list(range(near)), list(range(near, parts))]
    swap = [(i, i ^ 1) for i in range(parts)]
    across = [(i, (i + near) % parts) for i in range(parts)]

    def team_exchange(rows):
        if near == 2:
            return lax.ppermute(rows, "tensor", swap)
        return lax.all_gather(rows, "tensor", axis=0, tiled=True, axis_index_groups=teams)

    def team_join(rows, others):
        return jnp.concatenate([rows, others], axis=0) if near == 2 else others

    def team_gather(rows):
        return team_join(rows, team_exchange(rows))

    def team_scatter(rows):
        if near == 2:
            half = rows.shape[0] // 2
            return rows[:half] + lax.ppermute(rows[half:].astype(LOW), "tensor", swap).astype(F32)
        return lax.psum_scatter(
            rows.astype(LOW), "tensor", scatter_dimension=0, tiled=True, axis_index_groups=teams
        ).astype(F32)

    def scatter_direct(rows):
        size = rows.shape[0] // parts
        place = lax.axis_index("tensor")

        def part(hop):
            index = lax.rem(place + hop, parts)
            return lax.dynamic_slice_in_dim(rows, index * size, size)

        total = part(0).astype(F32)
        for hop in range(1, parts):
            pairs = [(i, (i + hop) % parts) for i in range(parts)]
            total = total + lax.ppermute(part(hop).astype(LOW), "tensor", pairs).astype(F32)
        return total

    def own_piece(matrix):
        rows = matrix.shape[0] // replicas
        return lax.dynamic_slice_in_dim(matrix, lax.axis_index("dp") * rows, rows)

    def spread(piece):
        return lax.all_gather(piece, "dp", axis=0, tiled=True)

    def body(
        block_input,
        segment_ids,
        out_cotangent,
        norm1_gain,
        query_weight,
        key_weight,
        value_weight,
        gate_weight,
        decay_weight,
        conv_query,
        conv_key,
        conv_value,
        decay_log,
        decay_bias,
        output_gain,
        output_weight,
        norm2_gain,
        ffn_gate,
        ffn_up,
        ffn_down,
    ):
        batch_count, slice_rows, width = block_input.shape
        heads = decay_log.shape[0]
        qk_cols = query_weight.shape[1]
        v_cols = value_weight.shape[1]
        ffn_cols = ffn_gate.shape[1]
        batches = range(batch_count)
        x_rows = [block_input[b].astype(F32) for b in batches]
        cot_rows = [out_cotangent[b] for b in batches]
        first_rows = [rms_forward(x_rows[b], norm1_gain).astype(LOW) for b in batches]
        ffn_both = jnp.concatenate([ffn_gate, ffn_up], axis=1)
        proj_all = jnp.concatenate(
            [
                query_weight,
                key_weight,
                value_weight,
                gate_weight,
                decay_weight.reshape(width, 2 * heads),
                jnp.zeros((width, LANES - 2 * heads), LOW),
            ],
            axis=1,
        )
        taps = jnp.pad(
            jnp.concatenate([conv_query, conv_key, conv_value], axis=1), ((0, 4), (0, 0))
        )
        params = jnp.pad(
            jnp.stack([-jnp.exp(decay_log), decay_bias]), ((0, 6), (0, LANES - heads))
        )
        gain = jnp.broadcast_to(output_gain, (8, output_gain.shape[0]))
        aux = [token_tables(segment_ids[b]) for b in batches]

        normed, projs, mixeds, saveds, branches, cot_full = [], [], [], [], [], []
        pieces = [own_piece(ffn_both), own_piece(ffn_down)]
        far = None
        for b in batches:
            rows = first_rows[b]
            if b > 0:
                rows = after(rows, normed[b - 1])
            normed.append(gather(rows))
        pieces = [
            lax.ppermute(after(piece, proj_all), "tensor", across) for piece in pieces
        ]
        far = [spread(piece) for piece in pieces]
        cot_pairs = [team_exchange(after(rows, pieces)) for rows in cot_rows]
        cot_full = [team_join(cot_rows[b], cot_pairs[b]) for b in batches]
        for b in batches:
            rows = after(normed[b], branches[b - 1]) if b > 0 else normed[b]
            projected = dot(rows, proj_all)
            mixed, *saved = mixer_forward(projected, aux[b], taps, params, gain, heads)
            mixed = after(mixed, pieces if b == 0 else cot_pairs)
            projs.append(projected)
            mixeds.append(mixed)
            saveds.append(saved)
            branches.append(dot(mixed, output_weight).astype(LOW))
        last = branches[-1]
        branches = [scatter(rows) for rows in branches]

        near_weights, far_weights = (ffn_both, ffn_down), tuple(far)

        def ffn_half(rows, cot, weights):
            both, down = weights
            gate_up = dot(rows, both)
            gate_pre, up_pre = gate_up[:, :ffn_cols], gate_up[:, ffn_cols:]
            sig = jax.nn.sigmoid(gate_pre)
            hidden = (gate_pre * sig * up_pre).astype(LOW)
            dhidden = contract_cols(cot, down)
            dgate = dhidden * up_pre * sig * (1.0 + gate_pre * (1.0 - sig))
            dup = dhidden * (gate_pre * sig)
            return hidden, jnp.concatenate([dgate, dup], axis=1).astype(LOW)

        residuals = [None] * batch_count
        ffn_full = [None] * batch_count
        hiddens = [None] * batch_count
        dboths = [None] * batch_count
        partial_in = [None] * batch_count
        partial_out = [None] * batch_count
        dresiduals = [None] * batch_count
        dbranch = [None] * batch_count
        gain2 = []

        def enter(b, behind):
            residuals[b] = x_rows[b] + after(branches[b], behind)
            low_rows = rms_forward(residuals[b], norm2_gain).astype(LOW)
            ffn_full[b] = team_gather(low_rows)
            return low_rows

        def leave(b, behind):
            dffn = after(partial_in[b], behind)
            back, part = rms_backward(residuals[b], norm2_gain, dffn)
            gain2.append(part)
            dresiduals[b] = cot_rows[b].astype(F32) + back
            low_rows = dresiduals[b].astype(LOW)
            dbranch[b] = gather(low_rows)
            return low_rows

        def over_dp(matrix):
            return lax.psum_scatter(matrix, "dp", scatter_dimension=0, tiled=True)

        def joined(halves):
            return jnp.concatenate([jnp.concatenate(h, axis=1) for h in halves], axis=0)

        enter(0, last)
        behind = None
        for b in batches:
            rows = after(ffn_full[b], behind) if b > 0 else ffn_full[b]
            near_half = ffn_half(rows, cot_full[b], near_weights)
            if b + 1 < batch_count:
                behind = enter(b + 1, near_half)
            else:
                behind = leave(b - 1, near_half)
            far_half = ffn_half(after(ffn_full[b], behind), cot_full[b], far_weights)
            hiddens[b] = [near_half[0], far_half[0]]
            dboths[b] = [near_half[1], far_half[1]]
            if b == batch_count - 1:
                down_local = contract_rows(
                    after(jnp.concatenate(cot_full, axis=0), far_half), joined(hiddens)
                ).astype(LOW)
                near_half, far_half = after((near_half, far_half), down_local)
            dffn = contract_cols(near_half[1], ffn_both) + contract_cols(
                far_half[1], far_weights[0]
            )
            partial_in[b] = team_scatter(dffn)
            ffn_out = dot(near_half[0], ffn_down) + dot(far_half[0], far_weights[1])
            partial_out[b] = team_scatter(ffn_out)
            behind = (dffn.astype(LOW), ffn_out.astype(LOW))
        outputs = [(residuals[b] + partial_out[b]).astype(LOW) for b in batches]

        both_local = contract_rows(
            after(jnp.concatenate(ffn_full, axis=0), behind), joined(dboths)
        ).astype(LOW)
        leave(batch_count - 1, both_local)
        down_grad = over_dp(down_local)
        both_grad = over_dp(both_local)
        far_grads = [
            lax.ppermute(down_grad[:, ffn_cols:], "tensor", across),
            lax.ppermute(both_grad[:, 2 * ffn_cols :], "tensor", across),
        ]
        down_grad = spread(down_grad[:, :ffn_cols] + far_grads[0])
        both_grad = spread(both_grad[:, : 2 * ffn_cols] + far_grads[1])

        input_grads, gain1, dtaps, dsmall, dgain = [], [], [], [], []
        grads_out, grads_proj = [], []
        behind = both_local
        for b in batches:
            rows = after(dbranch[b], behind)
            dmixed = contract_cols(rows, output_weight)
            dproj, dt, ds, dg = mixer_backward(
                projs[b], aux[b], taps, params, gain, saveds[b], dmixed, heads
            )
            dtaps.append(dt)
            dsmall.append(ds)
            dgain.append(dg)
            if b == 0:
                pass
            else:
                dproj = after(dproj, dnormed)
            dnormed_low = contract_cols(dproj, proj_all).astype(LOW)
            behind = dnormed_low
            dnormed = scatter_direct(dnormed_low)
            back, part = rms_backward(x_rows[b], norm1_gain, dnormed)
            gain1.append(part)
            input_grads.append((dresiduals[b] + back).astype(LOW))
            grads_proj.append((normed[b], dproj))
            grads_out.append((mixeds[b], rows))
        total_out = sum(contract_rows(after(left, behind), right) for left, right in grads_out)
        total_proj = sum(contract_rows(after(left, behind), right) for left, right in grads_proj)
        total_proj = after(total_proj.astype(LOW), dnormed)
        sum_out, sum_proj = lax.psum((total_out.astype(LOW), total_proj), "dp")
        sum_taps = sum(dtaps).reshape(4, 8, -1).sum(axis=1)
        sum_small = sum(dsmall).reshape(2, 8, LANES).sum(axis=1)[:, :heads]
        sum_taps, sum_small = lax.psum((sum_taps, sum_small), "dp")
        gains = lax.psum((sum(gain1), sum(gain2), sum(dgain).sum(axis=0)), ("dp", "tensor"))
        grad_proj = sum_proj.astype(F32)
        grad_ffn = both_grad.astype(F32)
        small_at = 2 * qk_cols + 2 * v_cols
        return (
            jnp.stack(outputs, axis=0),
            jnp.stack(input_grads, axis=0),
            gains[0],
            grad_proj[:, :qk_cols],
            grad_proj[:, qk_cols : 2 * qk_cols],
            grad_proj[:, 2 * qk_cols : 2 * qk_cols + v_cols],
            grad_proj[:, 2 * qk_cols + v_cols : small_at],
            grad_proj[:, small_at : small_at + 2 * heads].reshape(width, 2, heads),
            sum_taps[:, :qk_cols],
            sum_taps[:, qk_cols : 2 * qk_cols],
            sum_taps[:, 2 * qk_cols :],
            sum_small[0],
            sum_small[1],
            gains[2],
            sum_out.astype(F32),
            gains[1],
            grad_ffn[:, :ffn_cols],
            grad_ffn[:, ffn_cols:],
            jnp.transpose(down_grad).astype(F32),
        )

    return body


def solution(mesh):
    in_specs = (
        P(None, ("dp", "tensor"), None),
        P(None, "dp"),
        P(None, ("dp", "tensor"), None),
        P(),
        P(None, "tensor"),
        P(None, "tensor"),
        P(None, "tensor"),
        P(None, "tensor"),
        P(None, None, "tensor"),
        P(None, "tensor"),
        P(None, "tensor"),
        P(None, "tensor"),
        P("tensor"),
        P("tensor"),
        P(),
        P("tensor", None),
        P(),
        P(None, "tensor"),
        P(None, "tensor"),
        P("tensor", None),
    )
    out_specs = (
        P(None, ("dp", "tensor"), None),
        P(None, ("dp", "tensor"), None),
        P(),
        P(None, "tensor"),
        P(None, "tensor"),
        P(None, "tensor"),
        P(None, "tensor"),
        P(None, None, "tensor"),
        P(None, "tensor"),
        P(None, "tensor"),
        P(None, "tensor"),
        P("tensor"),
        P("tensor"),
        P(),
        P("tensor", None),
        P(),
        P(None, "tensor"),
        P(None, "tensor"),
        P("tensor", None),
    )
    body = make_body(mesh.shape["tensor"], mesh.shape["dp"])
    return jax.shard_map(
        body, mesh=mesh, in_specs=in_specs, out_specs=out_specs, check_vma=False
    )
```

time: 6030 us -> 1350 us (0.22)
  other arithmetic: 1810 us -> 77.4 us
  waiting for transfers between devices: 1730 us -> 467 us
  matrix products: 1500 us -> 376 us
  local copies, waits for them, and re-layouts: 848 us -> 133 us
  Pallas kernels: 0 us -> 189 us
    another operation x228 -> x6, other arithmetic: 1340 us -> 11.1 us  [the longest x3 9.54 us: body(): jnp.stack(input_grads, axis=0)]
    dot_general x616 -> x12, matrix products: 1070 us -> 117 us  [dot(): return jnp.dot(left, right, preferred_element_type=F32)]
    psum x1, waiting for transfers between devices: 748 us -> 18 us  [body(): sum_out, sum_proj = lax.psum((total_out.astype(LOW), total_proj), 'dp')]
    reduce_scatter x8 -> x4, waiting for transfers between devices: 495 us -> 0.06 us  [the longest x2 0.04 us: over_dp(): return lax.psum_scatter(matrix, 'dp', scatter_dimension=0, tiled=True)]
    all_gather x8, waiting for transfers between devices: 485 us -> 187 us  [the longest x4 119 us: gather(): return lax.all_gather(rows, 'tensor', axis=0, tiled=True)]
    ppermute x0 -> x18, waiting for transfers between devices: none -> 260 us  [the longest x4 115 us: team_exchange(): return lax.ppermute(rows, 'tensor', swap)]
    reduce_sum x91 -> x9, other arithmetic: 252 us -> 9.94 us  [the longest x3 6.93 us: rms_backward(): return (back, jnp.sum(grad * scaled, axis=0))]
    pallas_call x0 -> x4, Pallas kernels: none -> 189 us  [the longest x2 107 us: mixer_backward(): pl.pallas_call(functools.partial(backward_kernel, heads), grid=(blocks,),...]
  transfers between devices with their start and end apart: 17 -> 31, of which waited for: 13 -> 10; matrix products, arithmetic and copies ran while one was open for 18% -> 39% of each run, Pallas kernels for 0% -> 14%
where the time goes in v1:
time: 1350 us; the launch traced here: 1340 us
  waiting for transfers between devices  467 us (35%)
  matrix products  376 us (28%)
  Pallas kernels  189 us (14%)
  local copies, waits for them, and re-layouts  133 us (10%)
  other arithmetic  77.4 us (6%)
  blocking collectives  65.2 us (5%)
  starting transfers between devices  19 us (1%)
  between operations  17.5 us (1%)
    dot_general x12, matrix products, contract_cols(): lax.dot_general(left, right, (((1,), (1,)), ((), ())), preferred_element_...  138 us
    dot_general x6, matrix products, contract_rows(): lax.dot_general(left, right, (((0,), (0,)), ((), ())), preferred_element_...  121 us
    all_gather x4, waiting for transfers between devices, gather(): return lax.all_gather(rows, 'tensor', axis=0, tiled=True)  119 us
    dot_general x12, matrix products, dot(): return jnp.dot(left, right, preferred_element_type=F32)  117 us
    ppermute x4, waiting for transfers between devices, team_exchange(): return lax.ppermute(rows, 'tensor', swap)  115 us
    pallas_call x2, Pallas kernels, mixer_backward(): pl.pallas_call(functools.partial(backward_kernel, heads), grid=(blocks,),...  107 us
    pallas_call x2, Pallas kernels, mixer_forward(): pl.pallas_call(functools.partial(forward_kernel, heads), grid=(blocks,),...  82.4 us
    all_gather x4, waiting for transfers between devices, spread(): return lax.all_gather(piece, 'dp', axis=0, tiled=True)  67.7 us
  transfers between devices with their start and end apart: 31, of which 10 were waited for; matrix products, arithmetic and copies ran while one was open for 39% of the time, Pallas kernels for 14%

profile of v1, /device:TPU:0, one launch (start us, length us, event | category | flops | bytes accessed | tf_op | source)
XLA Modules:
  0.0 1344.5 jit_solution(1025458532252404806)
XLA Ops:
  14.5 19.1 %concatenate.71 = bf16[2048,3200]{1,0:T(8,128)(2,1)} concatenate(bf16[2048,512]{1,0:T(8,128)(2,1)S(1)} %copy-done.54, bf16[2048,512]{1,0:T(8,128)(2,1)} %param.25, bf16[2048,1024]{1,0:T(8,128)(2,1)} %param.26, bf16[2048,1024]{1,0:T(8,128)(2,1)} %param.27, bf16[2048,8]{1,0:T(8,128)(2,1)S(1)} %copy.75, bf16[2048,120]{1,0:T(8,128)(2,1)S(1)} %broadcast_in_dim.4), dimensions={1} | concatenate | bytes 26214400 | tf_op jit(solution)/shard_map/concatenate | solution.py:598
  35.6 4.1 collective-permute-start.1
  39.6 3.2 constant_dynamic-update-slice_fusion.1
  44.9 4.4 copy-done.42
  51.5 118.8 %all-gather.9.cloned.1.call-done = bf16[1024,2048]{1,0:T(8,128)(2,1)} async-done(((bf16[256,2048]{1,0:T(8,128)(2,1)}), bf16[1024,2048]{1,0:T(8,128)(2,1)}) %all-gather.9.cloned.1.call-update) | async-done | bytes 4194320 | tf_op jit(solution)/shard_map/all_gather | solution.py:507
  172.2 22.1 %fusion.90.proj_ref.halo_ref = f32[1024,3200]{1,0:T(8,128)} fusion(bf16[1024,2048]{1,0:T(8,128)(2,1)} %all-gather.9.cloned.1.call-done, bf16[2048,3200]{1,0:T(8,128)(2,1)} %concatenate.71), kind=kOutput, calls=%fused_computation.204 | convolution fusion | flops 13421772800 | bytes 30408704 | tf_op jit(solution)/shard_map/dot_general | solution.py:491
  194.4 41.1 %mixer_forward.2 = (bf16[1024,1024]{1,0:T(8,128)(2,1)S(1)}, f32[1024,1024]{1,0:T(8,128)S(1)}, bf16[1024,1024]{1,0:T(8,128)(2,1)S(1)}, bf16[16,4,64,64]{3,2,1,0:T(8,128)(2,1)S(1)}, bf16[16,4,128,256]{3,2,1,0:T(8,128)(2,1)S(1)}) custom-call(f32[1024,3200]{1,0:T(8,128)} %fusion.90.proj_ref.halo_ref, f32[1024,3200]{1,0:T(8,128)} %fusion.90.proj_ref.halo_ref, ...), custom_call_target="tpu_custom_call" | custom-call | flops 1024 | bytes 1024 | tf_op jit(solution)/shard_map/mixer_forward/pallas_call | solution.py:374
  241.9 9.6 convolution_convert_fusion.5
  252.4 3.3 slice_bitcast_fusion
  257.7 22.0 %fusion.91.proj_ref.halo_ref = f32[1024,3200]{1,0:T(8,128)} fusion(bf16[1024,2048]{1,0:T(8,128)(2,1)} %all-gather.11.cloned.1.call-done, bf16[2048,3200]{1,0:T(8,128)(2,1)} %concatenate.71), kind=kOutput, calls=%fused_computation.205 | convolution fusion | flops 13421772800 | bytes 30408704 | tf_op jit(solution)/shard_map/dot_general | solution.py:491
  279.7 41.2 %mixer_forward.3 = (bf16[1024,1024]{1,0:T(8,128)(2,1)S(1)}, f32[1024,1024]{1,0:T(8,128)S(1)}, bf16[1024,1024]{1,0:T(8,128)(2,1)S(1)}, bf16[16,4,64,64]{3,2,1,0:T(8,128)(2,1)S(1)}, bf16[16,4,128,256]{3,2,1,0:T(8,128)(2,1)S(1)}) custom-call(f32[1024,3200]{1,0:T(8,128)} %fusion.91.proj_ref.halo_ref, f32[1024,3200]{1,0:T(8,128)} %fusion.91.proj_ref.halo_ref, ...), custom_call_target="tpu_custom_call" | custom-call | flops 1024 | bytes 1024 | tf_op jit(solution)/shard_map/mixer_forward/pallas_call | solution.py:374
  327.4 42.9 %collective-permute-done.3 = bf16[256,2048]{1,0:T(8,128)(2,1)} collective-permute-done((bf16[256,2048]{1,0:T(8,128)(2,1)}, bf16[256,2048]{1,0:T(8,128)(2,1)}, u32[]{:S(2)}, u32[]{:S(2)}) %collective-permute-start.3) | collective-permute-done | bytes 1048608 | tf_op jit(solution)/shard_map/ppermute | solution.py:528
  370.3 6.1 convolution_convert_fusion.4
  382.1 5.7 pad_maximum_fusion
  387.7 72.4 %collective-permute-done.4 = bf16[256,2048]{1,0:T(8,128)(2,1)S(1)} collective-permute-done((bf16[256,2048]{1,0:T(8,128)(2,1)S(1)}, bf16[256,2048]{1,0:T(8,128)(2,1)S(1)}, u32[]{:S(2)}, u32[]{:S(2)}) %collective-permute-start.4) | collective-permute-done | bytes 1048608 | tf_op jit(solution)/shard_map/ppermute | solution.py:528
  461.8 9.0 fusion.76
  470.8 10.7 multiply_convert_fusion.10
  483.2 7.7 fusion.77
  495.8 12.7 fusion.93
  508.5 11.4 multiply_convert_fusion.4
  519.9 11.9 convolution_add_fusion.3
  536.6 6.9 pad_maximum_fusion.1
  545.2 8.1 fusion.94
  553.3 10.5 multiply_convert_fusion.6
  573.7 10.8 fusion.95
  584.5 8.9 multiply_convert_fusion.1
  597.7 18.1 %convolution_convert_fusion.1 = bf16[2048,2816]{1,0:T(8,128)(2,1)} fusion(bf16[1024,2048]{1,0:T(8,128)(2,1)S(1)} %copy-done.43, bf16[512,1408]{1,0:T(8,128)(2,1)} %get-tuple-element.81, bf16[512,1408]{1,0:T(8,128)(2,1)} %get-tuple-element.80, bf16[512,1408]{1,0:T(8,128)(2,1)} %get-tuple-element.206, bf16[512,1408]{1,0:T(8,128)(2,1)} %get-tuple-element.208), kind=kOutput, calls=%fused_computation.18 | convolution fusion | flops 11839995904 | bytes 21495808 | tf_op jit(solution)/shard_map/dot_general | solution.py:495
  615.8 10.0 fusion.98
  625.8 9.1 convolution_add_fusion.2
  638.0 42.3 %convolution_convert_fusion = bf16[2048,5632]{1,0:T(8,128)(2,1)} fusion(bf16[1024,2048]{1,0:T(8,128)(2,1)} %pad_maximum_fusion.1, bf16[512,1408]{1,0:T(8,128)(2,1)} %copy-done.59, bf16[512,1408]{1,0:T(8,128)(2,1)} %copy-done.58, bf16[512,1408]{1,0:T(8,128)(2,1)} %copy-done.57, bf16[512,1408]{1,0:T(8,128)(2,1)} %copy-done.56, ...), kind=kOutput, calls=%fused_computation.1 | convolution fusion | flops 23726129152 | bytes 38797312 | tf_op jit(solution)/shard_map/dot_general | solution.py:495
  688.4 10.1 fusion.97.grad_ref
  698.5 53.6 %mixer_backward.2 = (bf16[1024,3200]{1,0:T(8,128)(2,1)}, f32[32,2048]{1,0:T(8,128)S(1)}, f32[16,128]{1,0:T(8,128)S(1)}, f32[8,256]{1,0:T(8,128)S(1)}) custom-call(f32[1024,3200]{1,0:T(8,128)} %fusion.90.proj_ref.halo_ref, f32[1024,3200]{1,0:T(8,128)} %fusion.90.proj_ref.halo_ref, f32[1024,128]{1,0:T(8,128)S(1)} %copy-done.1, ...), custom_call_target="tpu_custom_call" | custom-call | flops 1024 | bytes 1024 | tf_op jit(solution)/shard_map/mixer_backward/pallas_call | solution.py:419
  752.0 18.9 %convolution_convert_fusion.3 = bf16[1024,2048]{1,0:T(8,128)(2,1)S(1)} fusion(bf16[1024,3200]{1,0:T(8,128)(2,1)} %get-tuple-element.87, bf16[2048,3200]{1,0:T(8,128)(2,1)} %concatenate.71), kind=kOutput, calls=%fused_computation.30 | convolution fusion | flops 13423869952 | bytes 23855104 | tf_op jit(solution)/shard_map/dot_general | solution.py:501
  778.1 10.1 fusion.99.grad_ref
  788.3 53.3 %mixer_backward.3 = (bf16[1024,3200]{1,0:T(8,128)(2,1)}, f32[32,2048]{1,0:T(8,128)S(1)}, f32[16,128]{1,0:T(8,128)S(1)}, f32[8,256]{1,0:T(8,128)S(1)}) custom-call(f32[1024,3200]{1,0:T(8,128)} %fusion.91.proj_ref.halo_ref, f32[1024,3200]{1,0:T(8,128)} %fusion.91.proj_ref.halo_ref, f32[1024,128]{1,0:T(8,128)S(1)} %copy-done.3, ...), custom_call_target="tpu_custom_call" | custom-call | flops 1024 | bytes 1024 | tf_op jit(solution)/shard_map/mixer_backward/pallas_call | solution.py:419
  841.6 21.3 %collective-permute-done.10 = bf16[256,2048]{1,0:T(8,128)(2,1)} collective-permute-done((bf16[256,2048]{1,0:T(8,128)(2,1)}, bf16[256,2048]{1,0:T(8,128)(2,1)}, u32[]{:S(2)}, u32[]{:S(2)}) %collective-permute-start.10) | collective-permute-done | bytes 1048608 | tf_op jit(solution)/shard_map/ppermute | solution.py:556
  862.9 4.5 convert_add_fusion.3
  867.5 19.0 %convolution_convert_fusion.2 = bf16[1024,2048]{1,0:T(8,128)(2,1)S(1)} fusion(bf16[1024,3200]{1,0:T(8,128)(2,1)} %get-tuple-element.97, bf16[2048,3200]{1,0:T(8,128)(2,1)} %concatenate.71), kind=kOutput, calls=%fused_computation.29 | convolution fusion | flops 13423869952 | bytes 23855104 | tf_op jit(solution)/shard_map/dot_general | solution.py:501
  890.1 4.0 collective-permute-start.15
  894.1 6.8 fusion.101
  901.0 21.4 %fusion.100 = f32[2048,3200]{1,0:T(8,128)} fusion(bf16[1024,2048]{1,0:T(8,128)(2,1)} %all-gather.9.cloned.1.call-done, bf16[1024,3200]{1,0:T(8,128)(2,1)S(1)} %bitcast.175), kind=kOutput, calls=%fused_computation.214 | convolution fusion | flops 13421772800 | bytes 36962304 | tf_op jit(solution)/shard_map/dot_general | solution.py:495
  922.4 23.4 %add_convert_fusion = bf16[2048,3200]{1,0:T(8,128)(2,1)} fusion(f32[2048,3200]{1,0:T(8,128)} %fusion.100, bf16[1024,2048]{1,0:T(8,128)(2,1)} %all-gather.11.cloned.1.call-done, bf16[1024,3200]{1,0:T(8,128)(2,1)S(1)} %bitcast.177), kind=kOutput, calls=%fused_computation | convolution fusion | flops 13434880000 | bytes 50069504 | tf_op jit(solution)/shard_map/dot_general | solution.py:495
  945.8 8.6 add_convert_fusion.1
  954.4 27.0 %collective-permute-done.14 = bf16[256,2048]{1,0:T(8,128)(2,1)} collective-permute-done((bf16[256,2048]{1,0:T(8,128)(2,1)}, bf16[256,2048]{1,0:T(8,128)(2,1)}, u32[]{:S(2)}, u32[]{:S(2)}) %collective-permute-start.14) | collective-permute-done | bytes 1048608 | tf_op jit(solution)/shard_map/ppermute | solution.py:556
  981.4 4.6 fusion.43
  987.3 31.3 %collective-permute-done.17 = bf16[256,1408]{1,0:T(8,128)(2,1)S(1)} collective-permute-done((bf16[256,1408]{1,0:T(8,128)(2,1)S(1)}, bf16[256,1408]{1,0:T(8,128)(2,1)S(1)}, u32[]{:S(2)}, u32[]{:S(2)}) %collective-permute-start.17) | collective-permute-done | bytes 720928 | tf_op jit(solution)/shard_map/ppermute | solution.py:721
  1022.6 65.1 %collective-permute-done.16 = bf16[256,2816]{1,0:T(8,128)(2,1)S(1)} collective-permute-done((bf16[256,2816]{1,0:T(8,128)(2,1)S(1)}, bf16[256,2816]{1,0:T(8,128)(2,1)S(1)}, u32[]{:S(2)}, u32[]{:S(2)}) %collective-permute-start.16) | collective-permute-done | bytes 1441824 | tf_op jit(solution)/shard_map/ppermute | solution.py:722
  1089.0 6.3 fusion.92
  1095.5 3.4 convolution_add_fusion.1
  1101.2 3.4 fusion.96
  1104.7 3.4 convolution_add_fusion
  1110.7 25.5 %all-reduce.17 = (f32[4,2048]{1,0:T(4,128)S(1)}, f32[2,4]{1,0:T(2,128)S(1)}) all-reduce(f32[4,2048]{1,0:T(4,128)S(1)} %bitcast_reduce_fusion, f32[2,4]{1,0:T(2,128)S(1)} %bitcast.168), channel_id=1, replica_groups=mesh['dp'=8,'tensor'=4] {'dp'}, use_global_device_ids=true, to_apply=%region_15.16 | all-reduce | flops 8200 | bytes 65600 | tf_op jit(solution)/shard_map/psum | solution.py:757
  1137.9 39.8 %all-reduce.16 = (f32[2048]{0:T(1024)}, f32[256]{0:T(256)}, f32[2048]{0:T(1024)}) all-reduce(f32[2048]{0:T(1024)S(1)} %add.284, f32[256]{0:T(256)S(1)} %add_reduce_fusion, f32[2048]{0:T(1024)S(1)} %add.290), channel_id=1, replica_groups=mesh['dp'=8,'tensor'=4] {'dp','tensor'}, use_global_device_ids=true, to_apply=%region_12.13 | all-reduce | flops 4352 | bytes 34816 | tf_op jit(solution)/shard_map/psum | solution.py:758
  1177.8 4.8 fusion.64
  1185.5 3.3 fusion.63
  1191.8 18.0 %all-reduce.21.cloned.1.call-done = (bf16[2048,3200]{1,0:T(8,128)(2,1)}, bf16[1024,2048]{1,0:T(8,128)(2,1)}) async-done(((bf16[2048,3200]{1,0:T(8,128)(2,1)}, bf16[1024,2048]{1,0:T(8,128)(2,1)}), (bf16[2048,3200]{1,0:T(8,128)(2,1)}, bf16[1024,2048]{1,0:T(8,128)(2,1)})) %all-reduce.21.cloned.1.call-update) | async-done | bytes 17301520 | tf_op jit(solution)/shard_map/psum | solution.py:754
  1211.8 6.7 convert_element_type.371
  1218.5 7.2 fusion.81
  1225.7 11.9 fusion.80
  1237.6 17.9 %all-gather.23.cloned.1.call-done = bf16[2048,1408]{1,0:T(8,128)(2,1)} async-done(((bf16[256,1408]{1,0:T(8,128)(2,1)}), bf16[2048,1408]{1,0:T(8,128)(2,1)}) %all-gather.23.cloned.1.call-update) | async-done | bytes 5767184 | tf_op jit(solution)/shard_map/all_gather | solution.py:564
  1255.5 7.8 convert_bitcast_fusion
  1263.3 12.3 copy.83
  1275.6 49.8 %all-gather.21.cloned.1.call-done = bf16[2048,2816]{1,0:T(8,128)(2,1)} async-done(((bf16[256,2816]{1,0:T(8,128)(2,1)}), bf16[2048,2816]{1,0:T(8,128)(2,1)}) %all-gather.21.cloned.1.call-update) | async-done | bytes 11534352 | tf_op jit(solution)/shard_map/all_gather | solution.py:564
  1325.4 11.1 fusion.82
  (386 shorter events, 107.2 us)
Async XLA Ops:
  8.0 162.3 %all-gather.9.cloned.1.call-start = ((), (), s32[]{:S(2)}) async-start(), calls=%async_computation.4 | async-start | bytes 5242880 | tf_op jit(solution)/shard_map/all_gather | solution.py:507
  12.9 244.8 %all-gather.11.cloned.1.call-start = ((), (), s32[]{:S(2)}) async-start(), calls=%async_computation.6 | async-start | bytes 5242880 | tf_op jit(solution)/shard_map/all_gather | solution.py:507
  35.6 206.3 %collective-permute-start.1 = (bf16[176,2048]{1,0:T(8,128)(2,1)}, bf16[176,2048]{1,0:T(8,128)(2,1)S(1)}, u32[]{:S(2)}, u32[]{:S(2)}) collective-permute-start(bf16[176,2048]{1,0:T(8,128)(2,1)} %constant_dynamic-slice_fusion.6), channel_id=1, source_target_pairs={{0,2},{1,3},{2,0},{3,1},{4,6},{5,7},{6,4},{7,5},{8,10},{9,11},{10,... | collective-permute-start | bytes 2162696 | tf_op jit(solution)/shard_map/ppermute | solution.py:627
  49.3 122.8 %copy-start.89 = (f32[4]{0:T(128)S(1)}, f32[4]{0:T(128)}, u32[]{:S(2)}) copy-start(f32[4]{0:T(128)} %param.32) | copy-start | bytes 52
  49.3 122.8 %copy-start.85 = (f32[4]{0:T(128)S(1)}, f32[4]{0:T(128)}, u32[]{:S(2)}) copy-start(f32[4]{0:T(128)} %param.33) | copy-start | bytes 52
  49.3 122.8 %copy-start.73 = (f32[4,1024]{1,0:T(4,128)S(1)}, f32[4,1024]{1,0:T(4,128)}, u32[]{:S(2)}) copy-start(f32[4,1024]{1,0:T(4,128)} %param.31) | copy-start | bytes 49156
  49.3 122.8 %copy-start.82 = (f32[4,512]{1,0:T(4,128)S(1)}, f32[4,512]{1,0:T(4,128)}, u32[]{:S(2)}) copy-start(f32[4,512]{1,0:T(4,128)} %param.30) | copy-start | bytes 24580
  49.4 122.8 %copy-start.83 = (f32[4,512]{1,0:T(4,128)S(1)}, f32[4,512]{1,0:T(4,128)}, u32[]{:S(2)}) copy-start(f32[4,512]{1,0:T(4,128)} %param.29) | copy-start | bytes 24580
  50.6 191.3 %collective-permute-start = (bf16[256,2816]{1,0:T(8,128)(2,1)}, bf16[256,2816]{1,0:T(8,128)(2,1)}, u32[]{:S(2)}, u32[]{:S(2)}) collective-permute-start(bf16[256,2816]{1,0:T(8,128)(2,1)} %constant_dynamic-slice_fusion.7), channel_id=1, source_target_pairs={{0,2},{1,3},{2,0},{3,1},{4,6},{5,7},{6,4},{7,5},{8,10},{9,11},{10,... | collective-permute-start | bytes 4325384 | tf_op jit(solution)/shard_map/ppermute | solution.py:627
  170.4 207.7 %reduce-scatter.5.cloned.1.call-start = ((), (), s32[]{:S(2)}) async-start(), calls=%async_computation.5 | async-start | bytes 5242880 | tf_op jit(solution)/shard_map/reduce_scatter | solution.py:511
  172.1 22.3 %copy-start = (f32[1024,128]{1,0:T(8,128)}, f32[1024,128]{1,0:T(8,128)S(1)}, u32[]{:S(2)}) copy-start(f32[1024,128]{1,0:T(8,128)S(1)} %pad.63.aux_ref) | copy-start | bytes 1572868
  172.2 107.5 %copy-start.16 = (f32[8,128]{1,0:T(8,128)}, f32[8,128]{1,0:T(8,128)S(1)}, u32[]{:S(2)}) copy-start(f32[8,128]{1,0:T(8,128)S(1)} %select_maximum_fusion.2.params_ref) | copy-start | bytes 12292
  172.2 22.2 %copy-start.84 = (f32[256]{0:T(256)S(1)}, f32[256]{0:T(256)}, u32[]{:S(2)}) copy-start(f32[256]{0:T(256)} %param.34) | copy-start | bytes 3076
  194.4 85.3 %copy-start.14 = (f32[8,256]{1,0:T(8,128)}, f32[8,256]{1,0:T(8,128)S(1)}, u32[]{:S(2)}) copy-start(f32[8,256]{1,0:T(8,128)S(1)} %broadcast_in_dim.5.gain_ref) | copy-start | bytes 24580
  251.5 239.4 %reduce-scatter.7.cloned.1.call-start = ((), (), s32[]{:S(2)}) async-start(), calls=%async_computation.7 | async-start | bytes 5242880 | tf_op jit(solution)/shard_map/reduce_scatter | solution.py:511
  252.4 27.3 %copy-start.2 = (f32[1024,128]{1,0:T(8,128)}, f32[1024,128]{1,0:T(8,128)S(1)}, u32[]{:S(2)}) copy-start(f32[1024,128]{1,0:T(8,128)S(1)} %pad.72.aux_ref) | copy-start | bytes 1572868
  255.7 71.7 %collective-permute-start.2 = (bf16[256,2048]{1,0:T(8,128)(2,1)}, bf16[256,2048]{1,0:T(8,128)(2,1)}, u32[]{:S(2)}, u32[]{:S(2)}) collective-permute-start(bf16[256,2048]{1,0:T(8,128)(2,1)} %get-tuple-element.71), channel_id=1, source_target_pairs={{0,1},{1,0},{2,3},{3,2},{4,5},{5,4},{6,7},{7,6},{8,9},{9,8},{10,11... | collective-permute-start | bytes 3145736 | tf_op jit(solution)/shard_map/ppermute | solution.py:528
  255.7 114.6 %collective-permute-start.3 = (bf16[256,2048]{1,0:T(8,128)(2,1)}, bf16[256,2048]{1,0:T(8,128)(2,1)}, u32[]{:S(2)}, u32[]{:S(2)}) collective-permute-start(bf16[256,2048]{1,0:T(8,128)(2,1)} %get-tuple-element.72), channel_id=1, source_target_pairs={{0,1},{1,0},{2,3},{3,2},{4,5},{5,4},{6,7},{7,6},{8,9},{9,8},{10,11... | collective-permute-start | bytes 3145736 | tf_op jit(solution)/shard_map/ppermute | solution.py:528
  279.7 90.5 %copy-start.86 = (bf16[1024,2048]{1,0:T(8,128)(2,1)S(1)}, bf16[1024,2048]{1,0:T(8,128)(2,1)}, u32[]{:S(2)}) copy-start(bf16[1024,2048]{1,0:T(8,128)(2,1)} %param.35) | copy-start | bytes 12582916
  327.4 42.9 %copy-start.20 = (bf16[1024,1024]{1,0:T(8,128)(2,1)}, bf16[1024,1024]{1,0:T(8,128)(2,1)S(1)}, u32[]{:S(2)}) copy-start(bf16[1024,1024]{1,0:T(8,128)(2,1)S(1)} %get-tuple-element.108) | copy-start | bytes 6291460
  376.4 119.4 %all-gather.13.cloned.1.call-start = ((), (), s32[]{:S(2)}) async-start(), calls=%async_computation.8 | async-start | bytes 12976128 | tf_op jit(solution)/shard_map/all_gather | solution.py:564
  376.9 131.5 %all-gather.15.cloned.1.call-start = ((), (), s32[]{:S(2)}) async-start(), calls=%async_computation.9 | async-start | bytes 6488064 | tf_op jit(solution)/shard_map/all_gather | solution.py:564
  377.5 310.8 %all-gather.17.cloned.1.call-start = ((), (), s32[]{:S(2)}) async-start(), calls=%async_computation.10 | async-start | bytes 5242880 | tf_op jit(solution)/shard_map/all_gather | solution.py:507
  380.0 81.8 %slice-start.2 = ((s8[11534336]{0:T(1024)(128)(4,1)}), s8[4194304]{0:T(1024)(128)(4,1)S(1)}, s32[]{:S(2)}) async-start(s8[11534336]{0:T(1024)(128)(4,1)} %bitcast.144), calls=%async_computation.19 | async-start | bytes 8388608
  380.4 190.5 %copy-start.68 = (f32[256]{0:T(256)}, f32[256]{0:T(256)S(1)}, u32[]{:S(2)}) copy-start(f32[256]{0:T(256)S(1)} %add_rsqrt_fusion.1) | copy-start | bytes 3076
  381.7 80.1 %slice-start.3 = ((s8[11534336]{0:T(1024)(128)(4,1)}), s8[4194304]{0:T(1024)(128)(4,1)S(1)}, s32[]{:S(2)}) async-start(s8[11534336]{0:T(1024)(128)(4,1)} %bitcast.144), calls=%async_computation.20 | async-start | bytes 8388608
  382.0 79.8 %copy-start.39 = (bf16[256,2048]{1,0:T(8,128)(2,1)}, bf16[256,2048]{1,0:T(8,128)(2,1)S(1)}, u32[]{:S(2)}) copy-start(bf16[256,2048]{1,0:T(8,128)(2,1)S(1)} %multiply_convert_fusion.13) | copy-start | bytes 3145732
  382.0 79.8 %slice-start.4 = ((s8[11534336]{0:T(1024)(128)(4,1)}), s8[3145728]{0:T(1024)(128)(4,1)S(1)}, s32[]{:S(2)}) async-start(s8[11534336]{0:T(1024)(128)(4,1)} %bitcast.144), calls=%async_computation.21 | async-start | bytes 6291456
  382.0 78.2 %collective-permute-start.4 = (bf16[256,2048]{1,0:T(8,128)(2,1)S(1)}, bf16[256,2048]{1,0:T(8,128)(2,1)S(1)}, u32[]{:S(2)}, u32[]{:S(2)}) collective-permute-start(bf16[256,2048]{1,0:T(8,128)(2,1)S(1)} %multiply_convert_fusion.13), channel_id=1, source_target_pairs={{0,1},{1,0},{2,3},{3,2},{4,5},{5,4},{6,7},{7,6},{8,9},{9,8},{10,11... | collective-permute-start | bytes 3145736 | tf_op jit(solution)/shard_map/ppermute | solution.py:528
  495.8 40.8 %collective-permute-start.6 = (bf16[256,2048]{1,0:T(8,128)(2,1)}, bf16[256,2048]{1,0:T(8,128)(2,1)}, u32[]{:S(2)}, u32[]{:S(2)}) collective-permute-start(bf16[256,2048]{1,0:T(8,128)(2,1)} %multiply_convert_fusion.12), channel_id=1, source_target_pairs={{0,1},{1,0},{2,3},{3,2},{4,5},{5,4},{6,7},{7,6},{8,9},{9,8},{10,11... | collective-permute-start | bytes 3145736 | tf_op jit(solution)/shard_map/ppermute | solution.py:528
  508.5 36.7 %slice-start.5 = ((s8[11534336]{0:T(1024)(128)(4,1)}), s8[4194304]{0:T(1024)(128)(4,1)S(1)}, s32[]{:S(2)}) async-start(s8[11534336]{0:T(1024)(128)(4,1)} %bitcast.146), calls=%async_computation.22 | async-start | bytes 8388608
  508.5 36.7 %slice-start.6 = ((s8[11534336]{0:T(1024)(128)(4,1)}), s8[4194304]{0:T(1024)(128)(4,1)S(1)}, s32[]{:S(2)}) async-start(s8[11534336]{0:T(1024)(128)(4,1)} %bitcast.146), calls=%async_computation.23 | async-start | bytes 8388608
  519.9 25.2 %slice-start.7 = ((s8[11534336]{0:T(1024)(128)(4,1)}), s8[3145728]{0:T(1024)(128)(4,1)S(1)}, s32[]{:S(2)}) async-start(s8[11534336]{0:T(1024)(128)(4,1)} %bitcast.146), calls=%async_computation.24 | async-start | bytes 6291456
  534.6 32.1 %collective-permute-start.7 = (bf16[256,2048]{1,0:T(8,128)(2,1)}, bf16[256,2048]{1,0:T(8,128)(2,1)}, u32[]{:S(2)}, u32[]{:S(2)}) collective-permute-start(bf16[256,2048]{1,0:T(8,128)(2,1)} %slice.406), channel_id=1, source_target_pairs={{0,1},{1,0},{2,3},{3,2},{4,5},{5,4},{6,7},{7,6},{8,9},{9,8},{10,11... | collective-permute-start | bytes 3145736 | tf_op jit(solution)/shard_map/ppermute | solution.py:540
  573.6 204.5 %all-gather.19.cloned.1.call-start = ((), (), s32[]{:S(2)}) async-start(), calls=%async_computation.11 | async-start | bytes 5242880 | tf_op jit(solution)/shard_map/all_gather | solution.py:507
  638.0 42.4 %collective-permute-start.12 = (bf16[256,2048]{1,0:T(8,128)(2,1)}, bf16[256,2048]{1,0:T(8,128)(2,1)}, u32[]{:S(2)}, u32[]{:S(2)}) collective-permute-start(bf16[256,2048]{1,0:T(8,128)(2,1)} %slice.404), channel_id=1, source_target_pairs={{0,1},{1,0},{2,3},{3,2},{4,5},{5,4},{6,7},{7,6},{8,9},{9,8},{10,11... | collective-permute-start | bytes 3145736 | tf_op jit(solution)/shard_map/ppermute | solution.py:540
  686.9 299.2 %reduce-scatter.11.cloned.1.call-start = ((), (), s32[]{:S(2)}) async-start(), calls=%async_computation.14 | async-start | bytes 12976128 | tf_op jit(solution)/shard_map/reduce_scatter | solution.py:683
  687.5 333.4 %reduce-scatter.9.cloned.1.call-start = ((), (), s32[]{:S(2)}) async-start(), calls=%async_computation.12 | async-start | bytes 25952256 | tf_op jit(solution)/shard_map/reduce_scatter | solution.py:683
  688.2 521.6 %all-reduce.21.cloned.1.call-start = ((), (), s32[]{:S(2)}) async-start(), calls=%async_computation.16 | async-start | bytes 34603008 | tf_op jit(solution)/shard_map/psum | solution.py:754
  773.9 67.7 %collective-permute-start.9 = (bf16[256,2048]{1,0:T(8,128)(2,1)}, bf16[256,2048]{1,0:T(8,128)(2,1)}, u32[]{:S(2)}, u32[]{:S(2)}) collective-permute-start(bf16[256,2048]{1,0:T(8,128)(2,1)} %get-tuple-element.213), channel_id=1, source_target_pairs={{0,1},{1,2},{2,3},{3,0},{4,5},{5,6},{6,7},{7,4},{8,9},{9,10},{10,1... | collective-permute-start | bytes 3145736 | tf_op jit(solution)/shard_map/ppermute | solution.py:556
  775.7 65.9 %collective-permute-start.11 = (bf16[256,2048]{1,0:T(8,128)(2,1)}, bf16[256,2048]{1,0:T(8,128)(2,1)}, u32[]{:S(2)}, u32[]{:S(2)}) collective-permute-start(bf16[256,2048]{1,0:T(8,128)(2,1)} %get-tuple-element.214), channel_id=1, source_target_pairs={{0,3},{1,0},{2,1},{3,2},{4,7},{5,4},{6,5},{7,6},{8,11},{9,8},{10,9... | collective-permute-start | bytes 3145736 | tf_op jit(solution)/shard_map/ppermute | solution.py:556
  778.1 84.8 %collective-permute-start.10 = (bf16[256,2048]{1,0:T(8,128)(2,1)}, bf16[256,2048]{1,0:T(8,128)(2,1)}, u32[]{:S(2)}, u32[]{:S(2)}) collective-permute-start(bf16[256,2048]{1,0:T(8,128)(2,1)} %get-tuple-element.215), channel_id=1, source_target_pairs={{0,2},{1,3},{2,0},{3,1},{4,6},{5,7},{6,4},{7,5},{8,10},{9,11},{10,... | collective-permute-start | bytes 3145736 | tf_op jit(solution)/shard_map/ppermute | solution.py:556
  890.1 64.2 %collective-permute-start.13 = (bf16[256,2048]{1,0:T(8,128)(2,1)}, bf16[256,2048]{1,0:T(8,128)(2,1)}, u32[]{:S(2)}, u32[]{:S(2)}) collective-permute-start(bf16[256,2048]{1,0:T(8,128)(2,1)} %get-tuple-element.210), channel_id=1, source_target_pairs={{0,1},{1,2},{2,3},{3,0},{4,5},{5,6},{6,7},{7,4},{8,9},{9,10},{10,1... | collective-permute-start | bytes 3145736 | tf_op jit(solution)/shard_map/ppermute | solution.py:556
  890.1 64.2 %collective-permute-start.15 = (bf16[256,2048]{1,0:T(8,128)(2,1)}, bf16[256,2048]{1,0:T(8,128)(2,1)}, u32[]{:S(2)}, u32[]{:S(2)}) collective-permute-start(bf16[256,2048]{1,0:T(8,128)(2,1)} %get-tuple-element.211), channel_id=1, source_target_pairs={{0,3},{1,0},{2,1},{3,2},{4,7},{5,4},{6,5},{7,6},{8,11},{9,8},{10,9... | collective-permute-start | bytes 3145736 | tf_op jit(solution)/shard_map/ppermute | solution.py:556
  894.1 87.3 %collective-permute-start.14 = (bf16[256,2048]{1,0:T(8,128)(2,1)}, bf16[256,2048]{1,0:T(8,128)(2,1)}, u32[]{:S(2)}, u32[]{:S(2)}) collective-permute-start(bf16[256,2048]{1,0:T(8,128)(2,1)} %get-tuple-element.212), channel_id=1, source_target_pairs={{0,2},{1,3},{2,0},{3,1},{4,6},{5,7},{6,4},{7,5},{8,10},{9,11},{10,... | collective-permute-start | bytes 3145736 | tf_op jit(solution)/shard_map/ppermute | solution.py:556
  894.1 28.2 %slice-start.12 = ((s8[6553600]{0:T(1024)(128)(4,1)}), s8[4194304]{0:T(1024)(128)(4,1)S(1)}, s32[]{:S(2)}) async-start(s8[6553600]{0:T(1024)(128)(4,1)} %bitcast.176), calls=%async_computation.29 | async-start | bytes 8388608
  901.0 21.4 %slice-start.13 = ((s8[6553600]{0:T(1024)(128)(4,1)}), s8[2359296]{0:T(1024)(128)(4,1)S(1)}, s32[]{:S(2)}) async-start(s8[6553600]{0:T(1024)(128)(4,1)} %bitcast.176), calls=%async_computation.30 | async-start | bytes 4718592
  922.4 23.4 %copy-start.21 = (bf16[1024,1024]{1,0:T(8,128)(2,1)S(1)}, bf16[1024,1024]{1,0:T(8,128)(2,1)}, u32[]{:S(2)}) copy-start(bf16[1024,1024]{1,0:T(8,128)(2,1)} %copy-done.20) | copy-start | bytes 6291460
  922.4 23.4 %copy-start.88 = (bf16[1024,2048]{1,0:T(8,128)(2,1)S(1)}, bf16[1024,2048]{1,0:T(8,128)(2,1)}, u32[]{:S(2)}) copy-start(bf16[1024,2048]{1,0:T(8,128)(2,1)} %all-gather.19.cloned.1.call-done) | copy-start | bytes 12582916
  945.8 35.6 %copy-start.31 = (bf16[2,256,2048]{2,1,0:T(8,128)(2,1)S(1)}, bf16[2,256,2048]{2,1,0:T(8,128)(2,1)}, u32[]{:S(2)}) copy-start(bf16[2,256,2048]{2,1,0:T(8,128)(2,1)} %param.20) | copy-start | bytes 6291460
  945.8 35.6 %copy-start.63 = (f32[2048]{0:T(1024)S(1)}, f32[2048]{0:T(1024)}, u32[]{:S(2)}) copy-start(f32[2048]{0:T(1024)} %param.23) | copy-start | bytes 24580
  945.8 35.6 %copy-start.75 = (f32[256]{0:T(256)S(1)}, f32[256]{0:T(256)}, u32[]{:S(2)}) copy-start(f32[256]{0:T(256)} %copy-done.74) | copy-start | bytes 3076
  945.8 35.6 %copy-start.77 = (f32[256]{0:T(256)S(1)}, f32[256]{0:T(256)}, u32[]{:S(2)}) copy-start(f32[256]{0:T(256)} %copy-done.76) | copy-start | bytes 3076
  986.0 269.5 %all-gather.23.cloned.1.call-start = ((), (), s32[]{:S(2)}) async-start(), calls=%async_computation.15 | async-start | bytes 6488064 | tf_op jit(solution)/shard_map/all_gather | solution.py:564
  987.3 31.4 %collective-permute-start.17 = (bf16[256,1408]{1,0:T(8,128)(2,1)S(1)}, bf16[256,1408]{1,0:T(8,128)(2,1)S(1)}, u32[]{:S(2)}, u32[]{:S(2)}) collective-permute-start(bf16[256,1408]{1,0:T(8,128)(2,1)S(1)} %slice.291), channel_id=1, source_target_pairs={{0,2},{1,3},{2,0},{3,1},{4,6},{5,7},{6,4},{7,5},{8,10},{9,11},{10,... | collective-permute-start | bytes 2162696 | tf_op jit(solution)/shard_map/ppermute | solution.py:721
  1020.8 304.6 %all-gather.21.cloned.1.call-start = ((), (), s32[]{:S(2)}) async-start(), calls=%async_computation.13 | async-start | bytes 12976128 | tf_op jit(solution)/shard_map/all_gather | solution.py:564
  1020.8 66.9 %copy-start.48 = (bf16[256,5632]{1,0:T(8,128)(2,1)S(1)}, bf16[256,5632]{1,0:T(8,128)(2,1)}, u32[]{:S(2)}) copy-start(bf16[256,5632]{1,0:T(8,128)(2,1)} %reduce-scatter.9.cloned.1.call-done) | copy-start | bytes 8650756
  1022.5 65.2 %collective-permute-start.16 = (bf16[256,2816]{1,0:T(8,128)(2,1)S(1)}, bf16[256,2816]{1,0:T(8,128)(2,1)S(1)}, u32[]{:S(2)}, u32[]{:S(2)}) collective-permute-start(bf16[256,2816]{1,0:T(8,128)(2,1)S(1)} %slice.287), channel_id=1, source_target_pairs={{0,2},{1,3},{2,0},{3,1},{4,6},{5,7},{6,4},{7,5},{8,10},{9,11},{10,... | collective-permute-start | bytes 4325384 | tf_op jit(solution)/shard_map/ppermute | solution.py:722
  1100.2 77.6 %collective-permute-start.5 = (bf16[256,2048]{1,0:T(8,128)(2,1)}, bf16[256,2048]{1,0:T(8,128)(2,1)}, u32[]{:S(2)}, u32[]{:S(2)}) collective-permute-start(bf16[256,2048]{1,0:T(8,128)(2,1)} %slice.407), channel_id=1, source_target_pairs={{0,1},{1,0},{2,3},{3,2},{4,5},{5,4},{6,7},{7,6},{8,9},{9,8},{10,11... | collective-permute-start | bytes 3145736 | tf_op jit(solution)/shard_map/ppermute | solution.py:540
  1108.1 69.7 %copy-start.24 = (f32[256,2048]{1,0:T(8,128)S(1)}, f32[256,2048]{1,0:T(8,128)}, u32[]{:S(2)}) copy-start(f32[256,2048]{1,0:T(8,128)} %copy-done.22) | copy-start | bytes 6291460
  1108.1 69.7 %copy-start.62 = (f32[2048]{0:T(1024)S(1)}, f32[2048]{0:T(1024)}, u32[]{:S(2)}) copy-start(f32[2048]{0:T(1024)} %param.36) | copy-start | bytes 24580
  1108.1 69.7 %copy-start.69 = (f32[256]{0:T(256)S(1)}, f32[256]{0:T(256)}, u32[]{:S(2)}) copy-start(f32[256]{0:T(256)} %copy-done.68) | copy-start | bytes 3076
  1108.1 69.7 %copy-start.79 = (f32[256]{0:T(256)S(1)}, f32[256]{0:T(256)}, u32[]{:S(2)}) copy-start(f32[256]{0:T(256)} %copy-done.78) | copy-start | bytes 3076
  1109.3 73.3 %collective-permute-start.8 = (bf16[256,2048]{1,0:T(8,128)(2,1)}, bf16[256,2048]{1,0:T(8,128)(2,1)}, u32[]{:S(2)}, u32[]{:S(2)}) collective-permute-start(bf16[256,2048]{1,0:T(8,128)(2,1)} %slice.405), channel_id=1, source_target_pairs={{0,1},{1,0},{2,3},{3,2},{4,5},{5,4},{6,7},{7,6},{8,9},{9,8},{10,11... | collective-permute-start | bytes 3145736 | tf_op jit(solution)/shard_map/ppermute | solution.py:540
  (78 other events, 393.5 us)
Sparse Core Ops, SparseCore 0:
  13.0 157.3 all-gather.8
  172.5 84.1 all-gather.10
  259.6 109.7 reduce-scatter.4
  376.5 97.3 reduce-scatter.6
  573.7 87.8 all-gather.16
  687.0 80.3 all-gather.18
Sparse Core Ops, SparseCore 1:
  378.7 65.6 all-gather.12
  446.2 43.1 all-gather.14
  691.4 86.2 reduce-scatter.10
  781.3 145.7 reduce-scatter.8
  986.1 223.6 all-reduce.20
  1212.3 43.2 all-gather.22
  1257.8 67.5 all-gather.20

commit v2 on v1

--- a/solution.py
+++ b/solution.py
@@ -717,12 +717,7 @@
         leave(batch_count - 1, both_local)
         down_grad = over_dp(down_local)
         both_grad = over_dp(both_local)
-        far_grads = [
-            lax.ppermute(down_grad[:, ffn_cols:], "tensor", across),
-            lax.ppermute(both_grad[:, 2 * ffn_cols :], "tensor", across),
-        ]
-        down_grad = spread(down_grad[:, :ffn_cols] + far_grads[0])
-        both_grad = spread(both_grad[:, : 2 * ffn_cols] + far_grads[1])
+        down_other = lax.ppermute(down_grad[:, ffn_cols:], "tensor", across)
 
         input_grads, gain1, dtaps, dsmall, dgain = [], [], [], [], []
         grads_out, grads_proj = [], []
@@ -736,10 +731,7 @@
             dtaps.append(dt)
             dsmall.append(ds)
             dgain.append(dg)
-            if b == 0:
-                pass
-            else:
-                dproj = after(dproj, dnormed)
+            dproj = after(dproj, down_other if b == 0 else dnormed)
             dnormed_low = contract_cols(dproj, proj_all).astype(LOW)
             behind = dnormed_low
             dnormed = scatter_direct(dnormed_low)
@@ -751,6 +743,11 @@
         total_out = sum(contract_rows(after(left, behind), right) for left, right in grads_out)
         total_proj = sum(contract_rows(after(left, behind), right) for left, right in grads_proj)
         total_proj = after(total_proj.astype(LOW), dnormed)
+        both_other = lax.ppermute(
+            both_grad[:, 2 * ffn_cols :], "tensor", across
+        )
+        down_grad = spread(down_grad[:, :ffn_cols] + down_other)
+        both_grad = spread(both_grad[:, : 2 * ffn_cols] + both_other)
         sum_out, sum_proj = lax.psum((total_out.astype(LOW), total_proj), "dp")
         sum_taps = sum(dtaps).reshape(4, 8, -1).sum(axis=1)
         sum_small = sum(dsmall).reshape(2, 8, LANES).sum(axis=1)[:, :heads]

time: 1350 us -> 1330 us (0.985)
  waiting for transfers between devices: 467 us -> 448 us
    all_gather x4, waiting for transfers between devices: 67.7 us -> 42.1 us  [spread(): return lax.all_gather(piece, 'dp', axis=0, tiled=True)]
    ppermute x2, waiting for transfers between devices: 96.5 us -> 71.9 us  [the longest x1 61.6 us: body(): both_other = lax.ppermute(both_grad[:, 2 * ffn_cols:], 'tensor', across)]
    psum x1, waiting for transfers between devices: 18 us -> 35.6 us  [body(): sum_out, sum_proj = lax.psum((total_out.astype(LOW), total_proj), 'dp')]
  transfers between devices with their start and end apart: 31 -> 31, of which waited for: 10 -> 11; matrix products, arithmetic and copies ran while one was open for 39% -> 40% of each run, Pallas kernels for 14% -> 14%
where the time goes in v2:
time: 1330 us
  waiting for transfers between devices  448 us (34%)
  matrix products  377 us (28%)
  Pallas kernels  189 us (14%)
  local copies, waits for them, and re-layouts  134 us (10%)
  other arithmetic  74 us (6%)
  blocking collectives  65.6 us (5%)
  starting transfers between devices  21.5 us (2%)
  between operations  17.5 us (1%)
    dot_general x12, matrix products, contract_cols(): lax.dot_general(left, right, (((1,), (1,)), ((), ())), preferred_element_...  140 us
    all_gather x4, waiting for transfers between devices, gather(): return lax.all_gather(rows, 'tensor', axis=0, tiled=True)  122 us
    dot_general x6, matrix products, contract_rows(): lax.dot_general(left, right, (((0,), (0,)), ((), ())), preferred_element_...  120 us
    dot_general x12, matrix products, dot(): return jnp.dot(left, right, preferred_element_type=F32)  117 us
    ppermute x4, waiting for transfers between devices, team_exchange(): return lax.ppermute(rows, 'tensor', swap)  115 us
    pallas_call x2, Pallas kernels, mixer_backward(): pl.pallas_call(functools.partial(backward_kernel, heads), grid=(blocks,),...  107 us
    pallas_call x2, Pallas kernels, mixer_forward(): pl.pallas_call(functools.partial(forward_kernel, heads), grid=(blocks,),...  82.4 us
    ppermute x1, waiting for transfers between devices, body(): both_other = lax.ppermute(both_grad[:, 2 * ffn_cols:], 'tensor', across)  61.6 us
  transfers between devices with their start and end apart: 31, of which 11 were waited for; matrix products, arithmetic and copies ran while one was open for 40% of the time, Pallas kernels for 14%

profile of v2, /device:TPU:0, one launch (start us, length us, event | category | flops | bytes accessed | tf_op | source)
XLA Modules:
  0.0 1325.6 jit_solution(8611650716027149487)
XLA Ops:
  14.5 19.1 %concatenate.71 = bf16[2048,3200]{1,0:T(8,128)(2,1)} concatenate(bf16[2048,512]{1,0:T(8,128)(2,1)S(1)} %copy-done.50, bf16[2048,512]{1,0:T(8,128)(2,1)} %param.25, bf16[2048,1024]{1,0:T(8,128)(2,1)} %param.26, bf16[2048,1024]{1,0:T(8,128)(2,1)} %param.27, bf16[2048,8]{1,0:T(8,128)(2,1)S(1)} %copy.75, bf16[2048,120]{1,0:T(8,128)(2,1)S(1)} %broadcast_in_dim.4), dimensions={1} | concatenate | bytes 26214400 | tf_op jit(solution)/shard_map/concatenate | solution.py:598
  35.6 4.1 collective-permute-start.1
  44.9 4.4 copy-done.39
  51.5 118.8 %all-gather.9.cloned.1.call-done = bf16[1024,2048]{1,0:T(8,128)(2,1)} async-done(((bf16[256,2048]{1,0:T(8,128)(2,1)}), bf16[1024,2048]{1,0:T(8,128)(2,1)}) %all-gather.9.cloned.1.call-update) | async-done | bytes 4194320 | tf_op jit(solution)/shard_map/all_gather | solution.py:507
  172.2 22.2 %fusion.90.proj_ref.halo_ref = f32[1024,3200]{1,0:T(8,128)} fusion(bf16[1024,2048]{1,0:T(8,128)(2,1)} %all-gather.9.cloned.1.call-done, bf16[2048,3200]{1,0:T(8,128)(2,1)} %concatenate.71), kind=kOutput, calls=%fused_computation.204 | convolution fusion | flops 13421772800 | bytes 30408704 | tf_op jit(solution)/shard_map/dot_general | solution.py:491
  194.4 41.2 %mixer_forward.2 = (bf16[1024,1024]{1,0:T(8,128)(2,1)S(1)}, f32[1024,1024]{1,0:T(8,128)S(1)}, bf16[1024,1024]{1,0:T(8,128)(2,1)S(1)}, bf16[16,4,64,64]{3,2,1,0:T(8,128)(2,1)S(1)}, bf16[16,4,128,256]{3,2,1,0:T(8,128)(2,1)S(1)}) custom-call(f32[1024,3200]{1,0:T(8,128)} %fusion.90.proj_ref.halo_ref, f32[1024,3200]{1,0:T(8,128)} %fusion.90.proj_ref.halo_ref, ...), custom_call_target="tpu_custom_call" | custom-call | flops 1024 | bytes 1024 | tf_op jit(solution)/shard_map/mixer_forward/pallas_call | solution.py:374
  241.9 9.6 convolution_convert_fusion.5
  257.6 21.9 %fusion.91.proj_ref.halo_ref = f32[1024,3200]{1,0:T(8,128)} fusion(bf16[1024,2048]{1,0:T(8,128)(2,1)} %all-gather.11.cloned.1.call-done, bf16[2048,3200]{1,0:T(8,128)(2,1)} %concatenate.71), kind=kOutput, calls=%fused_computation.205 | convolution fusion | flops 13421772800 | bytes 30408704 | tf_op jit(solution)/shard_map/dot_general | solution.py:491
  279.6 41.2 %mixer_forward.3 = (bf16[1024,1024]{1,0:T(8,128)(2,1)S(1)}, f32[1024,1024]{1,0:T(8,128)S(1)}, bf16[1024,1024]{1,0:T(8,128)(2,1)S(1)}, bf16[16,4,64,64]{3,2,1,0:T(8,128)(2,1)S(1)}, bf16[16,4,128,256]{3,2,1,0:T(8,128)(2,1)S(1)}) custom-call(f32[1024,3200]{1,0:T(8,128)} %fusion.91.proj_ref.halo_ref, f32[1024,3200]{1,0:T(8,128)} %fusion.91.proj_ref.halo_ref, ...), custom_call_target="tpu_custom_call" | custom-call | flops 1024 | bytes 1024 | tf_op jit(solution)/shard_map/mixer_forward/pallas_call | solution.py:374
  327.2 43.0 %collective-permute-done.3 = bf16[256,2048]{1,0:T(8,128)(2,1)} collective-permute-done((bf16[256,2048]{1,0:T(8,128)(2,1)}, bf16[256,2048]{1,0:T(8,128)(2,1)}, u32[]{:S(2)}, u32[]{:S(2)}) %collective-permute-start.3) | collective-permute-done | bytes 1048608 | tf_op jit(solution)/shard_map/ppermute | solution.py:528
  370.2 6.1 convolution_convert_fusion.4
  381.9 5.7 pad_maximum_fusion
  387.6 72.4 %collective-permute-done.4 = bf16[256,2048]{1,0:T(8,128)(2,1)S(1)} collective-permute-done((bf16[256,2048]{1,0:T(8,128)(2,1)S(1)}, bf16[256,2048]{1,0:T(8,128)(2,1)S(1)}, u32[]{:S(2)}, u32[]{:S(2)}) %collective-permute-start.4) | collective-permute-done | bytes 1048608 | tf_op jit(solution)/shard_map/ppermute | solution.py:528
  461.6 8.9 fusion.76
  470.6 10.9 multiply_convert_fusion.10
  483.1 7.7 fusion.77
  495.6 12.7 fusion.93
  508.3 10.9 multiply_convert_fusion.4
  519.2 11.9 convolution_add_fusion.3
  537.5 7.9 fusion.94
  545.5 10.4 multiply_convert_fusion.6
  565.7 10.8 fusion.95
  576.6 8.8 multiply_convert_fusion.1
  589.7 18.1 %convolution_convert_fusion.1 = bf16[2048,2816]{1,0:T(8,128)(2,1)} fusion(bf16[1024,2048]{1,0:T(8,128)(2,1)S(1)} %copy-done.40, bf16[512,1408]{1,0:T(8,128)(2,1)} %get-tuple-element.82, bf16[512,1408]{1,0:T(8,128)(2,1)} %get-tuple-element.81, bf16[512,1408]{1,0:T(8,128)(2,1)} %get-tuple-element.208, bf16[512,1408]{1,0:T(8,128)(2,1)} %get-tuple-element.210), kind=kOutput, calls=%fused_computation.18 | convolution fusion | flops 11839995904 | bytes 21495808 | tf_op jit(solution)/shard_map/dot_general | solution.py:495
  607.9 4.4 pad_maximum_fusion.1
  612.3 10.1 fusion.98
  622.4 9.5 convolution_add_fusion.2
  635.2 42.3 %convolution_convert_fusion = bf16[2048,5632]{1,0:T(8,128)(2,1)} fusion(bf16[1024,2048]{1,0:T(8,128)(2,1)} %pad_maximum_fusion.1, bf16[512,1408]{1,0:T(8,128)(2,1)} %copy-done.56, bf16[512,1408]{1,0:T(8,128)(2,1)} %copy-done.55, bf16[512,1408]{1,0:T(8,128)(2,1)} %copy-done.54, bf16[512,1408]{1,0:T(8,128)(2,1)} %copy-done.53, ...), kind=kOutput, calls=%fused_computation.1 | convolution fusion | flops 23726129152 | bytes 38797312 | tf_op jit(solution)/shard_map/dot_general | solution.py:495
  684.9 7.8 reduce-scatter.9.cloned.1.call-done
  696.5 10.6 fusion.97.grad_ref
  707.1 53.5 %mixer_backward.2 = (bf16[1024,3200]{1,0:T(8,128)(2,1)}, f32[32,2048]{1,0:T(8,128)S(1)}, f32[16,128]{1,0:T(8,128)S(1)}, f32[8,256]{1,0:T(8,128)S(1)}) custom-call(f32[1024,3200]{1,0:T(8,128)} %fusion.90.proj_ref.halo_ref, f32[1024,3200]{1,0:T(8,128)} %fusion.90.proj_ref.halo_ref, f32[1024,128]{1,0:T(8,128)S(1)} %copy-done.1, ...), custom_call_target="tpu_custom_call" | custom-call | flops 1024 | bytes 1024 | tf_op jit(solution)/shard_map/mixer_backward/pallas_call | solution.py:419
  760.6 10.3 collective-permute-done.9
  771.8 19.9 %convolution_convert_fusion.3 = bf16[1024,2048]{1,0:T(8,128)(2,1)} fusion(bf16[1024,3200]{1,0:T(8,128)(2,1)} %get-tuple-element.89, bf16[2048,3200]{1,0:T(8,128)(2,1)} %concatenate.71), kind=kOutput, calls=%fused_computation.30 | convolution fusion | flops 13423869952 | bytes 23855104 | tf_op jit(solution)/shard_map/dot_general | solution.py:501
  791.7 3.3 all-gather.19.cloned.1.call-done
  794.9 3.7 constant_dynamic-slice_fusion.5
  798.6 3.8 collective-permute-start.12
  803.9 10.2 fusion.99.grad_ref
  814.1 53.2 %mixer_backward.3 = (bf16[1024,3200]{1,0:T(8,128)(2,1)}, f32[32,2048]{1,0:T(8,128)S(1)}, f32[16,128]{1,0:T(8,128)S(1)}, f32[8,256]{1,0:T(8,128)S(1)}) custom-call(f32[1024,3200]{1,0:T(8,128)} %fusion.91.proj_ref.halo_ref, f32[1024,3200]{1,0:T(8,128)} %fusion.91.proj_ref.halo_ref, f32[1024,128]{1,0:T(8,128)S(1)} %pad.72.aux_ref, ...), custom_call_target="tpu_custom_call" | custom-call | flops 1024 | bytes 1024 | tf_op jit(solution)/shard_map/mixer_backward/pallas_call | solution.py:419
  867.3 23.3 %collective-permute-done.11 = bf16[256,2048]{1,0:T(8,128)(2,1)} collective-permute-done((bf16[256,2048]{1,0:T(8,128)(2,1)}, bf16[256,2048]{1,0:T(8,128)(2,1)}, u32[]{:S(2)}, u32[]{:S(2)}) %collective-permute-start.11) | collective-permute-done | bytes 1048608 | tf_op jit(solution)/shard_map/ppermute | solution.py:556
  890.6 4.2 convert_add_fusion.3
  894.8 18.8 %convolution_convert_fusion.2 = bf16[1024,2048]{1,0:T(8,128)(2,1)S(1)} fusion(bf16[1024,3200]{1,0:T(8,128)(2,1)} %get-tuple-element.99, bf16[2048,3200]{1,0:T(8,128)(2,1)} %concatenate.71), kind=kOutput, calls=%fused_computation.29 | convolution fusion | flops 13423869952 | bytes 23855104 | tf_op jit(solution)/shard_map/dot_general | solution.py:501
  917.2 4.0 collective-permute-start.16
  921.2 6.8 fusion.101
  928.0 21.4 %fusion.100 = f32[2048,3200]{1,0:T(8,128)} fusion(bf16[1024,2048]{1,0:T(8,128)(2,1)} %all-gather.11.cloned.1.call-done, bf16[1024,3200]{1,0:T(8,128)(2,1)S(1)} %bitcast.177), kind=kOutput, calls=%fused_computation.214 | convolution fusion | flops 13421772800 | bytes 36962304 | tf_op jit(solution)/shard_map/dot_general | solution.py:495
  949.4 23.3 %add_convert_fusion = bf16[2048,3200]{1,0:T(8,128)(2,1)} fusion(f32[2048,3200]{1,0:T(8,128)} %fusion.100, bf16[1024,2048]{1,0:T(8,128)(2,1)} %all-gather.9.cloned.1.call-done, bf16[1024,3200]{1,0:T(8,128)(2,1)S(1)} %bitcast.175), kind=kOutput, calls=%fused_computation | convolution fusion | flops 13434880000 | bytes 50069504 | tf_op jit(solution)/shard_map/dot_general | solution.py:495
  972.7 8.6 add_convert_fusion.1
  981.3 27.2 %collective-permute-done.15 = bf16[256,2048]{1,0:T(8,128)(2,1)} collective-permute-done((bf16[256,2048]{1,0:T(8,128)(2,1)}, bf16[256,2048]{1,0:T(8,128)(2,1)}, u32[]{:S(2)}, u32[]{:S(2)}) %collective-permute-start.15) | collective-permute-done | bytes 1048608 | tf_op jit(solution)/shard_map/ppermute | solution.py:556
  1008.6 4.6 fusion.43
  1015.0 61.6 %collective-permute-done.17 = bf16[256,2816]{1,0:T(8,128)(2,1)S(1)} collective-permute-done((bf16[256,2816]{1,0:T(8,128)(2,1)S(1)}, bf16[256,2816]{1,0:T(8,128)(2,1)S(1)}, u32[]{:S(2)}, u32[]{:S(2)}) %collective-permute-start.17) | collective-permute-done | bytes 1441824 | tf_op jit(solution)/shard_map/ppermute | solution.py:746
  1077.9 6.4 fusion.92
  1084.3 3.4 convolution_add_fusion.1
  1090.1 3.4 fusion.96
  1093.5 3.4 convolution_add_fusion
  1099.5 26.2 %all-reduce.17 = (f32[4,2048]{1,0:T(4,128)S(1)}, f32[2,4]{1,0:T(2,128)S(1)}) all-reduce(f32[4,2048]{1,0:T(4,128)S(1)} %bitcast_reduce_fusion, f32[2,4]{1,0:T(2,128)S(1)} %bitcast.168), channel_id=1, replica_groups=mesh['dp'=8,'tensor'=4] {'dp'}, use_global_device_ids=true, to_apply=%region_16.17 | all-reduce | flops 8200 | bytes 65600 | tf_op jit(solution)/shard_map/psum | solution.py:754
  1127.4 39.5 %all-reduce.16 = (f32[2048]{0:T(1024)}, f32[256]{0:T(256)}, f32[2048]{0:T(1024)}) all-reduce(f32[2048]{0:T(1024)S(1)} %add.284, f32[256]{0:T(256)S(1)} %add_reduce_fusion, f32[2048]{0:T(1024)S(1)} %add.290), channel_id=1, replica_groups=mesh['dp'=8,'tensor'=4] {'dp','tensor'}, use_global_device_ids=true, to_apply=%region_13.14 | all-reduce | flops 4352 | bytes 34816 | tf_op jit(solution)/shard_map/psum | solution.py:755
  1167.0 4.8 fusion.64
  1180.3 8.4 convert_bitcast_fusion
  1188.7 12.1 copy.83
  1200.8 35.6 %all-reduce.21.cloned.1.call-done = (bf16[2048,3200]{1,0:T(8,128)(2,1)}, bf16[1024,2048]{1,0:T(8,128)(2,1)}) async-done(((bf16[2048,3200]{1,0:T(8,128)(2,1)}, bf16[1024,2048]{1,0:T(8,128)(2,1)}), (bf16[2048,3200]{1,0:T(8,128)(2,1)}, bf16[1024,2048]{1,0:T(8,128)(2,1)})) %all-reduce.21.cloned.1.call-update) | async-done | bytes 17301520 | tf_op jit(solution)/shard_map/psum | solution.py:751
  1238.5 6.7 convert_element_type.371
  1245.1 7.5 fusion.81
  1252.6 11.8 fusion.80
  1264.4 42.1 %all-gather.21.cloned.1.call-done = bf16[2048,2816]{1,0:T(8,128)(2,1)} async-done(((bf16[256,2816]{1,0:T(8,128)(2,1)}), bf16[2048,2816]{1,0:T(8,128)(2,1)}) %all-gather.21.cloned.1.call-update) | async-done | bytes 11534352 | tf_op jit(solution)/shard_map/all_gather | solution.py:564
  1306.5 11.1 fusion.82
  (386 shorter events, 110.9 us)
Async XLA Ops:
  8.0 162.3 %all-gather.9.cloned.1.call-start = ((), (), s32[]{:S(2)}) async-start(), calls=%async_computation.4 | async-start | bytes 5242880 | tf_op jit(solution)/shard_map/all_gather | solution.py:507
  12.9 244.7 %all-gather.11.cloned.1.call-start = ((), (), s32[]{:S(2)}) async-start(), calls=%async_computation.6 | async-start | bytes 5242880 | tf_op jit(solution)/shard_map/all_gather | solution.py:507
  35.6 206.4 %collective-permute-start.1 = (bf16[176,2048]{1,0:T(8,128)(2,1)}, bf16[176,2048]{1,0:T(8,128)(2,1)S(1)}, u32[]{:S(2)}, u32[]{:S(2)}) collective-permute-start(bf16[176,2048]{1,0:T(8,128)(2,1)} %constant_dynamic-slice_fusion.6), channel_id=1, source_target_pairs={{0,2},{1,3},{2,0},{3,1},{4,6},{5,7},{6,4},{7,5},{8,10},{9,11},{10,... | collective-permute-start | bytes 2162696 | tf_op jit(solution)/shard_map/ppermute | solution.py:627
  49.3 122.8 %copy-start.88 = (f32[4]{0:T(128)S(1)}, f32[4]{0:T(128)}, u32[]{:S(2)}) copy-start(f32[4]{0:T(128)} %param.32) | copy-start | bytes 52
  49.3 122.8 %copy-start.84 = (f32[4]{0:T(128)S(1)}, f32[4]{0:T(128)}, u32[]{:S(2)}) copy-start(f32[4]{0:T(128)} %param.33) | copy-start | bytes 52
  49.3 122.8 %copy-start.72 = (f32[4,1024]{1,0:T(4,128)S(1)}, f32[4,1024]{1,0:T(4,128)}, u32[]{:S(2)}) copy-start(f32[4,1024]{1,0:T(4,128)} %param.31) | copy-start | bytes 49156
  49.3 122.8 %copy-start.81 = (f32[4,512]{1,0:T(4,128)S(1)}, f32[4,512]{1,0:T(4,128)}, u32[]{:S(2)}) copy-start(f32[4,512]{1,0:T(4,128)} %param.30) | copy-start | bytes 24580
  49.4 122.8 %copy-start.82 = (f32[4,512]{1,0:T(4,128)S(1)}, f32[4,512]{1,0:T(4,128)}, u32[]{:S(2)}) copy-start(f32[4,512]{1,0:T(4,128)} %param.29) | copy-start | bytes 24580
  50.6 191.4 %collective-permute-start = (bf16[256,2816]{1,0:T(8,128)(2,1)}, bf16[256,2816]{1,0:T(8,128)(2,1)}, u32[]{:S(2)}, u32[]{:S(2)}) collective-permute-start(bf16[256,2816]{1,0:T(8,128)(2,1)} %constant_dynamic-slice_fusion.7), channel_id=1, source_target_pairs={{0,2},{1,3},{2,0},{3,1},{4,6},{5,7},{6,4},{7,5},{8,10},{9,11},{10,... | collective-permute-start | bytes 4325384 | tf_op jit(solution)/shard_map/ppermute | solution.py:627
  170.4 207.6 %reduce-scatter.5.cloned.1.call-start = ((), (), s32[]{:S(2)}) async-start(), calls=%async_computation.5 | async-start | bytes 5242880 | tf_op jit(solution)/shard_map/reduce_scatter | solution.py:511
  172.1 22.3 %copy-start = (f32[1024,128]{1,0:T(8,128)}, f32[1024,128]{1,0:T(8,128)S(1)}, u32[]{:S(2)}) copy-start(f32[1024,128]{1,0:T(8,128)S(1)} %pad.63.aux_ref) | copy-start | bytes 1572868
  172.2 107.4 %copy-start.14 = (f32[8,128]{1,0:T(8,128)}, f32[8,128]{1,0:T(8,128)S(1)}, u32[]{:S(2)}) copy-start(f32[8,128]{1,0:T(8,128)S(1)} %select_maximum_fusion.2.params_ref) | copy-start | bytes 12292
  172.2 22.2 %copy-start.83 = (f32[256]{0:T(256)S(1)}, f32[256]{0:T(256)}, u32[]{:S(2)}) copy-start(f32[256]{0:T(256)} %param.34) | copy-start | bytes 3076
  194.4 85.1 %copy-start.12 = (f32[8,256]{1,0:T(8,128)}, f32[8,256]{1,0:T(8,128)S(1)}, u32[]{:S(2)}) copy-start(f32[8,256]{1,0:T(8,128)S(1)} %broadcast_in_dim.5.gain_ref) | copy-start | bytes 24580
  251.6 239.2 %reduce-scatter.7.cloned.1.call-start = ((), (), s32[]{:S(2)}) async-start(), calls=%async_computation.7 | async-start | bytes 5242880 | tf_op jit(solution)/shard_map/reduce_scatter | solution.py:511
  255.6 71.6 %collective-permute-start.2 = (bf16[256,2048]{1,0:T(8,128)(2,1)}, bf16[256,2048]{1,0:T(8,128)(2,1)}, u32[]{:S(2)}, u32[]{:S(2)}) collective-permute-start(bf16[256,2048]{1,0:T(8,128)(2,1)} %get-tuple-element.72), channel_id=1, source_target_pairs={{0,1},{1,0},{2,3},{3,2},{4,5},{5,4},{6,7},{7,6},{8,9},{9,8},{10,11... | collective-permute-start | bytes 3145736 | tf_op jit(solution)/shard_map/ppermute | solution.py:528
  255.6 114.6 %collective-permute-start.3 = (bf16[256,2048]{1,0:T(8,128)(2,1)}, bf16[256,2048]{1,0:T(8,128)(2,1)}, u32[]{:S(2)}, u32[]{:S(2)}) collective-permute-start(bf16[256,2048]{1,0:T(8,128)(2,1)} %get-tuple-element.73), channel_id=1, source_target_pairs={{0,1},{1,0},{2,3},{3,2},{4,5},{5,4},{6,7},{7,6},{8,9},{9,8},{10,11... | collective-permute-start | bytes 3145736 | tf_op jit(solution)/shard_map/ppermute | solution.py:528
  279.6 90.6 %copy-start.85 = (bf16[1024,2048]{1,0:T(8,128)(2,1)S(1)}, bf16[1024,2048]{1,0:T(8,128)(2,1)}, u32[]{:S(2)}) copy-start(bf16[1024,2048]{1,0:T(8,128)(2,1)} %param.35) | copy-start | bytes 12582916
  327.2 43.0 %copy-start.18 = (bf16[1024,1024]{1,0:T(8,128)(2,1)}, bf16[1024,1024]{1,0:T(8,128)(2,1)S(1)}, u32[]{:S(2)}) copy-start(bf16[1024,1024]{1,0:T(8,128)(2,1)S(1)} %get-tuple-element.110) | copy-start | bytes 6291460
  376.3 119.3 %all-gather.13.cloned.1.call-start = ((), (), s32[]{:S(2)}) async-start(), calls=%async_computation.8 | async-start | bytes 12976128 | tf_op jit(solution)/shard_map/all_gather | solution.py:564
  376.8 131.4 %all-gather.15.cloned.1.call-start = ((), (), s32[]{:S(2)}) async-start(), calls=%async_computation.9 | async-start | bytes 6488064 | tf_op jit(solution)/shard_map/all_gather | solution.py:564
  377.4 307.5 %all-gather.17.cloned.1.call-start = ((), (), s32[]{:S(2)}) async-start(), calls=%async_computation.10 | async-start | bytes 5242880 | tf_op jit(solution)/shard_map/all_gather | solution.py:507
  379.9 81.7 %slice-start.2 = ((s8[11534336]{0:T(1024)(128)(4,1)}), s8[4194304]{0:T(1024)(128)(4,1)S(1)}, s32[]{:S(2)}) async-start(s8[11534336]{0:T(1024)(128)(4,1)} %bitcast.144), calls=%async_computation.19 | async-start | bytes 8388608
  380.3 182.7 %copy-start.67 = (f32[256]{0:T(256)}, f32[256]{0:T(256)S(1)}, u32[]{:S(2)}) copy-start(f32[256]{0:T(256)S(1)} %add_rsqrt_fusion.1) | copy-start | bytes 3076
  381.5 80.1 %slice-start.3 = ((s8[11534336]{0:T(1024)(128)(4,1)}), s8[4194304]{0:T(1024)(128)(4,1)S(1)}, s32[]{:S(2)}) async-start(s8[11534336]{0:T(1024)(128)(4,1)} %bitcast.144), calls=%async_computation.20 | async-start | bytes 8388608
  381.8 79.8 %copy-start.37 = (bf16[256,2048]{1,0:T(8,128)(2,1)}, bf16[256,2048]{1,0:T(8,128)(2,1)S(1)}, u32[]{:S(2)}) copy-start(bf16[256,2048]{1,0:T(8,128)(2,1)S(1)} %multiply_convert_fusion.13) | copy-start | bytes 3145732
  381.8 79.8 %slice-start.4 = ((s8[11534336]{0:T(1024)(128)(4,1)}), s8[3145728]{0:T(1024)(128)(4,1)S(1)}, s32[]{:S(2)}) async-start(s8[11534336]{0:T(1024)(128)(4,1)} %bitcast.144), calls=%async_computation.21 | async-start | bytes 6291456
  381.8 78.2 %collective-permute-start.4 = (bf16[256,2048]{1,0:T(8,128)(2,1)S(1)}, bf16[256,2048]{1,0:T(8,128)(2,1)S(1)}, u32[]{:S(2)}, u32[]{:S(2)}) collective-permute-start(bf16[256,2048]{1,0:T(8,128)(2,1)S(1)} %multiply_convert_fusion.13), channel_id=1, source_target_pairs={{0,1},{1,0},{2,3},{3,2},{4,5},{5,4},{6,7},{7,6},{8,9},{9,8},{10,11... | collective-permute-start | bytes 3145736 | tf_op jit(solution)/shard_map/ppermute | solution.py:528
  495.6 40.2 %collective-permute-start.6 = (bf16[256,2048]{1,0:T(8,128)(2,1)}, bf16[256,2048]{1,0:T(8,128)(2,1)}, u32[]{:S(2)}, u32[]{:S(2)}) collective-permute-start(bf16[256,2048]{1,0:T(8,128)(2,1)} %multiply_convert_fusion.12), channel_id=1, source_target_pairs={{0,1},{1,0},{2,3},{3,2},{4,5},{5,4},{6,7},{7,6},{8,9},{9,8},{10,11... | collective-permute-start | bytes 3145736 | tf_op jit(solution)/shard_map/ppermute | solution.py:528
  519.2 18.3 %slice-start.5 = ((s8[11534336]{0:T(1024)(128)(4,1)}), s8[4194304]{0:T(1024)(128)(4,1)S(1)}, s32[]{:S(2)}) async-start(s8[11534336]{0:T(1024)(128)(4,1)} %bitcast.146), calls=%async_computation.22 | async-start | bytes 8388608
  519.2 18.4 %slice-start.6 = ((s8[11534336]{0:T(1024)(128)(4,1)}), s8[4194304]{0:T(1024)(128)(4,1)S(1)}, s32[]{:S(2)}) async-start(s8[11534336]{0:T(1024)(128)(4,1)} %bitcast.146), calls=%async_computation.23 | async-start | bytes 8388608
  519.2 18.4 %slice-start.7 = ((s8[11534336]{0:T(1024)(128)(4,1)}), s8[3145728]{0:T(1024)(128)(4,1)S(1)}, s32[]{:S(2)}) async-start(s8[11534336]{0:T(1024)(128)(4,1)} %bitcast.146), calls=%async_computation.24 | async-start | bytes 6291456
  533.8 25.0 %collective-permute-start.7 = (bf16[256,2048]{1,0:T(8,128)(2,1)}, bf16[256,2048]{1,0:T(8,128)(2,1)}, u32[]{:S(2)}, u32[]{:S(2)}) collective-permute-start(bf16[256,2048]{1,0:T(8,128)(2,1)} %slice.406), channel_id=1, source_target_pairs={{0,1},{1,0},{2,3},{3,2},{4,5},{5,4},{6,7},{7,6},{8,9},{9,8},{10,11... | collective-permute-start | bytes 3145736 | tf_op jit(solution)/shard_map/ppermute | solution.py:540
  565.7 127.0 %reduce-scatter.9.cloned.1.call-start = ((), (), s32[]{:S(2)}) async-start(), calls=%async_computation.11 | async-start | bytes 12976128 | tf_op jit(solution)/shard_map/reduce_scatter | solution.py:683
  607.8 187.1 %all-gather.19.cloned.1.call-start = ((), (), s32[]{:S(2)}) async-start(), calls=%async_computation.12 | async-start | bytes 5242880 | tf_op jit(solution)/shard_map/all_gather | solution.py:507
  635.1 42.4 %collective-permute-start.13 = (bf16[256,2048]{1,0:T(8,128)(2,1)}, bf16[256,2048]{1,0:T(8,128)(2,1)}, u32[]{:S(2)}, u32[]{:S(2)}) collective-permute-start(bf16[256,2048]{1,0:T(8,128)(2,1)} %slice.404), channel_id=1, source_target_pairs={{0,1},{1,0},{2,3},{3,2},{4,5},{5,4},{6,7},{7,6},{8,9},{9,8},{10,11... | collective-permute-start | bytes 3145736 | tf_op jit(solution)/shard_map/ppermute | solution.py:540
  684.1 329.2 %reduce-scatter.11.cloned.1.call-start = ((), (), s32[]{:S(2)}) async-start(), calls=%async_computation.13 | async-start | bytes 25952256 | tf_op jit(solution)/shard_map/reduce_scatter | solution.py:683
  684.8 495.5 %all-gather.23.cloned.1.call-start = ((), (), s32[]{:S(2)}) async-start(), calls=%async_computation.15 | async-start | bytes 6488064 | tf_op jit(solution)/shard_map/all_gather | solution.py:564
  694.0 13.1 copy-start.1
  694.0 76.9 %collective-permute-start.9 = (bf16[256,1408]{1,0:T(8,128)(2,1)S(1)}, bf16[256,1408]{1,0:T(8,128)(2,1)S(1)}, u32[]{:S(2)}, u32[]{:S(2)}) collective-permute-start(bf16[256,1408]{1,0:T(8,128)(2,1)S(1)} %slice.276), channel_id=1, source_target_pairs={{0,2},{1,3},{2,0},{3,1},{4,6},{5,7},{6,4},{7,5},{8,10},{9,11},{10,... | collective-permute-start | bytes 2162696 | tf_op jit(solution)/shard_map/ppermute | solution.py:720
  798.6 68.6 %collective-permute-start.10 = (bf16[256,2048]{1,0:T(8,128)(2,1)}, bf16[256,2048]{1,0:T(8,128)(2,1)}, u32[]{:S(2)}, u32[]{:S(2)}) collective-permute-start(bf16[256,2048]{1,0:T(8,128)(2,1)} %get-tuple-element.215), channel_id=1, source_target_pairs={{0,1},{1,2},{2,3},{3,0},{4,5},{5,6},{6,7},{7,4},{8,9},{9,10},{10,1... | collective-permute-start | bytes 3145736 | tf_op jit(solution)/shard_map/ppermute | solution.py:556
  798.6 68.6 %collective-permute-start.12 = (bf16[256,2048]{1,0:T(8,128)(2,1)}, bf16[256,2048]{1,0:T(8,128)(2,1)}, u32[]{:S(2)}, u32[]{:S(2)}) collective-permute-start(bf16[256,2048]{1,0:T(8,128)(2,1)} %get-tuple-element.216), channel_id=1, source_target_pairs={{0,3},{1,0},{2,1},{3,2},{4,7},{5,4},{6,5},{7,6},{8,11},{9,8},{10,9... | collective-permute-start | bytes 3145736 | tf_op jit(solution)/shard_map/ppermute | solution.py:556
  802.4 88.2 %collective-permute-start.11 = (bf16[256,2048]{1,0:T(8,128)(2,1)}, bf16[256,2048]{1,0:T(8,128)(2,1)}, u32[]{:S(2)}, u32[]{:S(2)}) collective-permute-start(bf16[256,2048]{1,0:T(8,128)(2,1)} %get-tuple-element.217), channel_id=1, source_target_pairs={{0,2},{1,3},{2,0},{3,1},{4,6},{5,7},{6,4},{7,5},{8,10},{9,11},{10,... | collective-permute-start | bytes 3145736 | tf_op jit(solution)/shard_map/ppermute | solution.py:556
  803.4 432.9 %all-reduce.21.cloned.1.call-start = ((), (), s32[]{:S(2)}) async-start(), calls=%async_computation.16 | async-start | bytes 34603008 | tf_op jit(solution)/shard_map/psum | solution.py:751
  917.2 64.1 %collective-permute-start.14 = (bf16[256,2048]{1,0:T(8,128)(2,1)}, bf16[256,2048]{1,0:T(8,128)(2,1)}, u32[]{:S(2)}, u32[]{:S(2)}) collective-permute-start(bf16[256,2048]{1,0:T(8,128)(2,1)} %get-tuple-element.212), channel_id=1, source_target_pairs={{0,1},{1,2},{2,3},{3,0},{4,5},{5,6},{6,7},{7,4},{8,9},{9,10},{10,1... | collective-permute-start | bytes 3145736 | tf_op jit(solution)/shard_map/ppermute | solution.py:556
  917.2 64.1 %collective-permute-start.16 = (bf16[256,2048]{1,0:T(8,128)(2,1)}, bf16[256,2048]{1,0:T(8,128)(2,1)}, u32[]{:S(2)}, u32[]{:S(2)}) collective-permute-start(bf16[256,2048]{1,0:T(8,128)(2,1)} %get-tuple-element.213), channel_id=1, source_target_pairs={{0,3},{1,0},{2,1},{3,2},{4,7},{5,4},{6,5},{7,6},{8,11},{9,8},{10,9... | collective-permute-start | bytes 3145736 | tf_op jit(solution)/shard_map/ppermute | solution.py:556
  921.2 87.4 %collective-permute-start.15 = (bf16[256,2048]{1,0:T(8,128)(2,1)}, bf16[256,2048]{1,0:T(8,128)(2,1)}, u32[]{:S(2)}, u32[]{:S(2)}) collective-permute-start(bf16[256,2048]{1,0:T(8,128)(2,1)} %get-tuple-element.214), channel_id=1, source_target_pairs={{0,2},{1,3},{2,0},{3,1},{4,6},{5,7},{6,4},{7,5},{8,10},{9,11},{10,... | collective-permute-start | bytes 3145736 | tf_op jit(solution)/shard_map/ppermute | solution.py:556
  921.2 28.2 %slice-start.10 = ((s8[6553600]{0:T(1024)(128)(4,1)}), s8[4194304]{0:T(1024)(128)(4,1)S(1)}, s32[]{:S(2)}) async-start(s8[6553600]{0:T(1024)(128)(4,1)} %bitcast.174), calls=%async_computation.27 | async-start | bytes 8388608
  928.0 21.4 %slice-start.11 = ((s8[6553600]{0:T(1024)(128)(4,1)}), s8[2359296]{0:T(1024)(128)(4,1)S(1)}, s32[]{:S(2)}) async-start(s8[6553600]{0:T(1024)(128)(4,1)} %bitcast.174), calls=%async_computation.28 | async-start | bytes 4718592
  949.4 23.3 %copy-start.19 = (bf16[1024,1024]{1,0:T(8,128)(2,1)S(1)}, bf16[1024,1024]{1,0:T(8,128)(2,1)}, u32[]{:S(2)}) copy-start(bf16[1024,1024]{1,0:T(8,128)(2,1)} %copy-done.18) | copy-start | bytes 6291460
  949.4 23.3 %copy-start.87 = (bf16[1024,2048]{1,0:T(8,128)(2,1)S(1)}, bf16[1024,2048]{1,0:T(8,128)(2,1)}, u32[]{:S(2)}) copy-start(bf16[1024,2048]{1,0:T(8,128)(2,1)} %all-gather.19.cloned.1.call-done) | copy-start | bytes 12582916
  972.7 35.9 %copy-start.29 = (bf16[2,256,2048]{2,1,0:T(8,128)(2,1)S(1)}, bf16[2,256,2048]{2,1,0:T(8,128)(2,1)}, u32[]{:S(2)}) copy-start(bf16[2,256,2048]{2,1,0:T(8,128)(2,1)} %param.20) | copy-start | bytes 6291460
  972.7 35.9 %copy-start.62 = (f32[2048]{0:T(1024)S(1)}, f32[2048]{0:T(1024)}, u32[]{:S(2)}) copy-start(f32[2048]{0:T(1024)} %param.23) | copy-start | bytes 24580
  972.7 35.8 %copy-start.74 = (f32[256]{0:T(256)S(1)}, f32[256]{0:T(256)}, u32[]{:S(2)}) copy-start(f32[256]{0:T(256)} %copy-done.73) | copy-start | bytes 3076
  972.7 35.8 %copy-start.76 = (f32[256]{0:T(256)S(1)}, f32[256]{0:T(256)}, u32[]{:S(2)}) copy-start(f32[256]{0:T(256)} %copy-done.75) | copy-start | bytes 3076
  1013.2 293.3 %all-gather.21.cloned.1.call-start = ((), (), s32[]{:S(2)}) async-start(), calls=%async_computation.14 | async-start | bytes 12976128 | tf_op jit(solution)/shard_map/all_gather | solution.py:564
  1013.3 63.3 %copy-start.43 = (bf16[256,5632]{1,0:T(8,128)(2,1)S(1)}, bf16[256,5632]{1,0:T(8,128)(2,1)}, u32[]{:S(2)}) copy-start(bf16[256,5632]{1,0:T(8,128)(2,1)} %reduce-scatter.11.cloned.1.call-done) | copy-start | bytes 8650756
  1014.9 61.6 %collective-permute-start.17 = (bf16[256,2816]{1,0:T(8,128)(2,1)S(1)}, bf16[256,2816]{1,0:T(8,128)(2,1)S(1)}, u32[]{:S(2)}, u32[]{:S(2)}) collective-permute-start(bf16[256,2816]{1,0:T(8,128)(2,1)S(1)} %slice.288), channel_id=1, source_target_pairs={{0,2},{1,3},{2,0},{3,1},{4,6},{5,7},{6,4},{7,5},{8,10},{9,11},{10,... | collective-permute-start | bytes 4325384 | tf_op jit(solution)/shard_map/ppermute | solution.py:746
  1089.0 77.9 %collective-permute-start.5 = (bf16[256,2048]{1,0:T(8,128)(2,1)}, bf16[256,2048]{1,0:T(8,128)(2,1)}, u32[]{:S(2)}, u32[]{:S(2)}) collective-permute-start(bf16[256,2048]{1,0:T(8,128)(2,1)} %slice.407), channel_id=1, source_target_pairs={{0,1},{1,0},{2,3},{3,2},{4,5},{5,4},{6,7},{7,6},{8,9},{9,8},{10,11... | collective-permute-start | bytes 3145736 | tf_op jit(solution)/shard_map/ppermute | solution.py:540
  1097.0 70.0 %copy-start.22 = (f32[256,2048]{1,0:T(8,128)S(1)}, f32[256,2048]{1,0:T(8,128)}, u32[]{:S(2)}) copy-start(f32[256,2048]{1,0:T(8,128)} %copy-done.20) | copy-start | bytes 6291460
  1097.0 70.0 %copy-start.61 = (f32[2048]{0:T(1024)S(1)}, f32[2048]{0:T(1024)}, u32[]{:S(2)}) copy-start(f32[2048]{0:T(1024)} %param.36) | copy-start | bytes 24580
  1097.0 70.0 %copy-start.68 = (f32[256]{0:T(256)S(1)}, f32[256]{0:T(256)}, u32[]{:S(2)}) copy-start(f32[256]{0:T(256)} %copy-done.67) | copy-start | bytes 3076
  1097.0 70.0 %copy-start.78 = (f32[256]{0:T(256)S(1)}, f32[256]{0:T(256)}, u32[]{:S(2)}) copy-start(f32[256]{0:T(256)} %copy-done.77) | copy-start | bytes 3076
  1098.1 73.6 %collective-permute-start.8 = (bf16[256,2048]{1,0:T(8,128)(2,1)}, bf16[256,2048]{1,0:T(8,128)(2,1)}, u32[]{:S(2)}, u32[]{:S(2)}) collective-permute-start(bf16[256,2048]{1,0:T(8,128)(2,1)} %slice.405), channel_id=1, source_target_pairs={{0,1},{1,0},{2,3},{3,2},{4,5},{5,4},{6,7},{7,6},{8,9},{9,8},{10,11... | collective-permute-start | bytes 3145736 | tf_op jit(solution)/shard_map/ppermute | solution.py:540
  (78 other events, 363.6 us)
Sparse Core Ops, SparseCore 0:
  13.0 157.3 all-gather.8
  172.5 84.1 all-gather.10
  259.6 109.5 reduce-scatter.4
  376.4 97.3 reduce-scatter.6
  565.8 83.4 all-gather.16
  684.2 110.6 all-gather.18
Sparse Core Ops, SparseCore 1:
  378.6 65.6 all-gather.12
  446.1 43.1 all-gather.14
  607.9 84.8 reduce-scatter.8
  696.4 145.7 reduce-scatter.10
  844.0 43.1 all-gather.22
  1013.3 223.0 all-reduce.20
  1238.7 67.7 all-gather.20

commit v3 on v2

--- a/solution.py
+++ b/solution.py
@@ -742,10 +742,10 @@
             grads_out.append((mixeds[b], rows))
         total_out = sum(contract_rows(after(left, behind), right) for left, right in grads_out)
         total_proj = sum(contract_rows(after(left, behind), right) for left, right in grads_proj)
-        total_proj = after(total_proj.astype(LOW), dnormed)
         both_other = lax.ppermute(
             both_grad[:, 2 * ffn_cols :], "tensor", across
         )
+        total_proj = after(total_proj.astype(LOW), both_other)
         down_grad = spread(down_grad[:, :ffn_cols] + down_other)
         both_grad = spread(both_grad[:, : 2 * ffn_cols] + both_other)
         sum_out, sum_proj = lax.psum((total_out.astype(LOW), total_proj), "dp")

time: 1330 us -> 1340 us (level)
    ppermute x6, waiting for transfers between devices: 50.6 us -> 79.2 us  [scatter_direct(): lax.ppermute(part(hop).astype(LOW), 'tensor', pairs).astype(F32)]
    unnamed x228 -> x222, local copies, waits for them, and re-layouts: 56.1 us -> 55.8 us
  transfers between devices with their start and end apart: 31 -> 31, of which waited for: 11 -> 13; matrix products, arithmetic and copies ran while one was open for 40% -> 39% of each run, Pallas kernels for 14% -> 14%
where the time goes in v3:
time: 1340 us
  waiting for transfers between devices  459 us (34%)
  matrix products  375 us (28%)
  Pallas kernels  189 us (14%)
  local copies, waits for them, and re-layouts  134 us (10%)
  other arithmetic  77.2 us (6%)
  blocking collectives  65.7 us (5%)
  starting transfers between devices  22.1 us (2%)
  between operations  17.3 us (1%)
    dot_general x12, matrix products, contract_cols(): lax.dot_general(left, right, (((1,), (1,)), ((), ())), preferred_element_...  141 us
    all_gather x4, waiting for transfers between devices, gather(): return lax.all_gather(rows, 'tensor', axis=0, tiled=True)  122 us
    dot_general x6, matrix products, contract_rows(): lax.dot_general(left, right, (((0,), (0,)), ((), ())), preferred_element_...  118 us
    dot_general x12, matrix products, dot(): return jnp.dot(left, right, preferred_element_type=F32)  116 us
    ppermute x4, waiting for transfers between devices, team_exchange(): return lax.ppermute(rows, 'tensor', swap)  115 us
    pallas_call x2, Pallas kernels, mixer_backward(): pl.pallas_call(functools.partial(backward_kernel, heads), grid=(blocks,),...  107 us
    pallas_call x2, Pallas kernels, mixer_forward(): pl.pallas_call(functools.partial(forward_kernel, heads), grid=(blocks,),...  82.4 us
    ppermute x6, waiting for transfers between devices, scatter_direct(): lax.ppermute(part(hop).astype(LOW), 'tensor', pairs).astype(F32)  79.2 us
  transfers between devices with their start and end apart: 31, of which 13 were waited for; matrix products, arithmetic and copies ran while one was open for 39% of the time, Pallas kernels for 14%

profile of v3, /device:TPU:0, one launch (start us, length us, event | category | flops | bytes accessed | tf_op | source)
XLA Modules:
  0.0 1339.4 jit_solution(472622740758439626)
XLA Ops:
  14.5 19.0 %concatenate.71 = bf16[2048,3200]{1,0:T(8,128)(2,1)} concatenate(bf16[2048,512]{1,0:T(8,128)(2,1)S(1)} %copy-done.48, bf16[2048,512]{1,0:T(8,128)(2,1)} %param.25, bf16[2048,1024]{1,0:T(8,128)(2,1)} %param.26, bf16[2048,1024]{1,0:T(8,128)(2,1)} %param.27, bf16[2048,8]{1,0:T(8,128)(2,1)S(1)} %copy.75, bf16[2048,120]{1,0:T(8,128)(2,1)S(1)} %broadcast_in_dim.4), dimensions={1} | concatenate | bytes 26214400 | tf_op jit(solution)/shard_map/concatenate | solution.py:598
  35.5 4.1 collective-permute-start.1
  44.9 4.4 copy-done.38
  51.5 118.8 %all-gather.9.cloned.1.call-done = bf16[1024,2048]{1,0:T(8,128)(2,1)} async-done(((bf16[256,2048]{1,0:T(8,128)(2,1)}), bf16[1024,2048]{1,0:T(8,128)(2,1)}) %all-gather.9.cloned.1.call-update) | async-done | bytes 4194320 | tf_op jit(solution)/shard_map/all_gather | solution.py:507
  172.2 22.2 %fusion.90.proj_ref.halo_ref = f32[1024,3200]{1,0:T(8,128)} fusion(bf16[1024,2048]{1,0:T(8,128)(2,1)} %all-gather.9.cloned.1.call-done, bf16[2048,3200]{1,0:T(8,128)(2,1)} %concatenate.71), kind=kOutput, calls=%fused_computation.204 | convolution fusion | flops 13421772800 | bytes 30408704 | tf_op jit(solution)/shard_map/dot_general | solution.py:491
  194.4 41.2 %mixer_forward.2 = (bf16[1024,1024]{1,0:T(8,128)(2,1)S(1)}, f32[1024,1024]{1,0:T(8,128)S(1)}, bf16[1024,1024]{1,0:T(8,128)(2,1)S(1)}, bf16[16,4,64,64]{3,2,1,0:T(8,128)(2,1)S(1)}, bf16[16,4,128,256]{3,2,1,0:T(8,128)(2,1)S(1)}) custom-call(f32[1024,3200]{1,0:T(8,128)} %fusion.90.proj_ref.halo_ref, f32[1024,3200]{1,0:T(8,128)} %fusion.90.proj_ref.halo_ref, ...), custom_call_target="tpu_custom_call" | custom-call | flops 1024 | bytes 1024 | tf_op jit(solution)/shard_map/mixer_forward/pallas_call | solution.py:374
  242.0 9.6 convolution_convert_fusion.5
  257.6 22.0 %fusion.91.proj_ref.halo_ref = f32[1024,3200]{1,0:T(8,128)} fusion(bf16[1024,2048]{1,0:T(8,128)(2,1)} %all-gather.11.cloned.1.call-done, bf16[2048,3200]{1,0:T(8,128)(2,1)} %concatenate.71), kind=kOutput, calls=%fused_computation.205 | convolution fusion | flops 13421772800 | bytes 30408704 | tf_op jit(solution)/shard_map/dot_general | solution.py:491
  279.6 41.2 %mixer_forward.3 = (bf16[1024,1024]{1,0:T(8,128)(2,1)S(1)}, f32[1024,1024]{1,0:T(8,128)S(1)}, bf16[1024,1024]{1,0:T(8,128)(2,1)S(1)}, bf16[16,4,64,64]{3,2,1,0:T(8,128)(2,1)S(1)}, bf16[16,4,128,256]{3,2,1,0:T(8,128)(2,1)S(1)}) custom-call(f32[1024,3200]{1,0:T(8,128)} %fusion.91.proj_ref.halo_ref, f32[1024,3200]{1,0:T(8,128)} %fusion.91.proj_ref.halo_ref, ...), custom_call_target="tpu_custom_call" | custom-call | flops 1024 | bytes 1024 | tf_op jit(solution)/shard_map/mixer_forward/pallas_call | solution.py:374
  327.1 43.0 %collective-permute-done.3 = bf16[256,2048]{1,0:T(8,128)(2,1)} collective-permute-done((bf16[256,2048]{1,0:T(8,128)(2,1)}, bf16[256,2048]{1,0:T(8,128)(2,1)}, u32[]{:S(2)}, u32[]{:S(2)}) %collective-permute-start.3) | collective-permute-done | bytes 1048608 | tf_op jit(solution)/shard_map/ppermute | solution.py:528
  370.1 6.1 convolution_convert_fusion.4
  382.0 5.7 pad_maximum_fusion
  387.7 72.4 %collective-permute-done.4 = bf16[256,2048]{1,0:T(8,128)(2,1)S(1)} collective-permute-done((bf16[256,2048]{1,0:T(8,128)(2,1)S(1)}, bf16[256,2048]{1,0:T(8,128)(2,1)S(1)}, u32[]{:S(2)}, u32[]{:S(2)}) %collective-permute-start.4) | collective-permute-done | bytes 1048608 | tf_op jit(solution)/shard_map/ppermute | solution.py:528
  461.7 9.0 fusion.76
  470.7 10.8 multiply_convert_fusion.10
  483.1 7.7 fusion.77
  495.5 12.7 fusion.93
  508.2 11.0 multiply_convert_fusion.4
  519.2 11.9 convolution_add_fusion.3
  537.5 7.9 fusion.94
  545.5 10.4 multiply_convert_fusion.6
  565.8 10.6 fusion.95
  576.4 8.9 multiply_convert_fusion.1
  589.6 18.1 %convolution_convert_fusion.1 = bf16[2048,2816]{1,0:T(8,128)(2,1)} fusion(bf16[1024,2048]{1,0:T(8,128)(2,1)S(1)} %copy-done.39, bf16[512,1408]{1,0:T(8,128)(2,1)} %get-tuple-element.82, bf16[512,1408]{1,0:T(8,128)(2,1)} %get-tuple-element.81, bf16[512,1408]{1,0:T(8,128)(2,1)} %get-tuple-element.208, bf16[512,1408]{1,0:T(8,128)(2,1)} %get-tuple-element.210), kind=kOutput, calls=%fused_computation.18 | convolution fusion | flops 11839995904 | bytes 21495808 | tf_op jit(solution)/shard_map/dot_general | solution.py:495
  607.7 4.4 pad_maximum_fusion.1
  612.1 10.1 fusion.98
  622.2 9.5 convolution_add_fusion.2
  635.1 42.2 %convolution_convert_fusion = bf16[2048,5632]{1,0:T(8,128)(2,1)} fusion(bf16[1024,2048]{1,0:T(8,128)(2,1)} %pad_maximum_fusion.1, bf16[512,1408]{1,0:T(8,128)(2,1)} %copy-done.54, bf16[512,1408]{1,0:T(8,128)(2,1)} %copy-done.53, bf16[512,1408]{1,0:T(8,128)(2,1)} %copy-done.52, bf16[512,1408]{1,0:T(8,128)(2,1)} %copy-done.51, ...), kind=kOutput, calls=%fused_computation.1 | convolution fusion | flops 23726129152 | bytes 38797312 | tf_op jit(solution)/shard_map/dot_general | solution.py:495
  684.7 7.8 reduce-scatter.9.cloned.1.call-done
  696.3 10.6 fusion.97.grad_ref
  707.0 53.5 %mixer_backward.2 = (bf16[1024,3200]{1,0:T(8,128)(2,1)}, f32[32,2048]{1,0:T(8,128)S(1)}, f32[16,128]{1,0:T(8,128)S(1)}, f32[8,256]{1,0:T(8,128)S(1)}) custom-call(f32[1024,3200]{1,0:T(8,128)} %fusion.90.proj_ref.halo_ref, f32[1024,3200]{1,0:T(8,128)} %fusion.90.proj_ref.halo_ref, f32[1024,128]{1,0:T(8,128)S(1)} %copy-done.1, ...), custom_call_target="tpu_custom_call" | custom-call | flops 1024 | bytes 1024 | tf_op jit(solution)/shard_map/mixer_backward/pallas_call | solution.py:419
  760.4 10.2 collective-permute-done.9
  771.5 19.9 %convolution_convert_fusion.3 = bf16[1024,2048]{1,0:T(8,128)(2,1)} fusion(bf16[1024,3200]{1,0:T(8,128)(2,1)} %get-tuple-element.89, bf16[2048,3200]{1,0:T(8,128)(2,1)} %concatenate.71), kind=kOutput, calls=%fused_computation.30 | convolution fusion | flops 13423869952 | bytes 23855104 | tf_op jit(solution)/shard_map/dot_general | solution.py:501
  794.7 3.7 constant_dynamic-slice_fusion.5
  798.5 3.8 collective-permute-start.12
  803.8 10.2 fusion.99.grad_ref
  814.0 53.2 %mixer_backward.3 = (bf16[1024,3200]{1,0:T(8,128)(2,1)}, f32[32,2048]{1,0:T(8,128)S(1)}, f32[16,128]{1,0:T(8,128)S(1)}, f32[8,256]{1,0:T(8,128)S(1)}) custom-call(f32[1024,3200]{1,0:T(8,128)} %fusion.91.proj_ref.halo_ref, f32[1024,3200]{1,0:T(8,128)} %fusion.91.proj_ref.halo_ref, f32[1024,128]{1,0:T(8,128)S(1)} %pad.72.aux_ref, ...), custom_call_target="tpu_custom_call" | custom-call | flops 1024 | bytes 1024 | tf_op jit(solution)/shard_map/mixer_backward/pallas_call | solution.py:419
  867.3 23.2 %collective-permute-done.11 = bf16[256,2048]{1,0:T(8,128)(2,1)} collective-permute-done((bf16[256,2048]{1,0:T(8,128)(2,1)}, bf16[256,2048]{1,0:T(8,128)(2,1)}, u32[]{:S(2)}, u32[]{:S(2)}) %collective-permute-start.11) | collective-permute-done | bytes 1048608 | tf_op jit(solution)/shard_map/ppermute | solution.py:556
  890.4 4.3 convert_add_fusion.3
  894.8 19.8 %convolution_convert_fusion.2 = bf16[1024,2048]{1,0:T(8,128)(2,1)} fusion(bf16[1024,3200]{1,0:T(8,128)(2,1)} %get-tuple-element.99, bf16[2048,3200]{1,0:T(8,128)(2,1)} %concatenate.71), kind=kOutput, calls=%fused_computation.29 | convolution fusion | flops 13423869952 | bytes 23855104 | tf_op jit(solution)/shard_map/dot_general | solution.py:501
  914.6 21.5 %fusion.100 = f32[2048,3200]{1,0:T(8,128)} fusion(bf16[1024,2048]{1,0:T(8,128)(2,1)} %all-gather.11.cloned.1.call-done, bf16[1024,3200]{1,0:T(8,128)(2,1)S(1)} %bitcast.177), kind=kOutput, calls=%fused_computation.214 | convolution fusion | flops 13421772800 | bytes 36962304 | tf_op jit(solution)/shard_map/dot_general | solution.py:495
  936.2 23.0 %add_convert_fusion = bf16[2048,3200]{1,0:T(8,128)(2,1)} fusion(f32[2048,3200]{1,0:T(8,128)} %fusion.100, bf16[1024,2048]{1,0:T(8,128)(2,1)} %all-gather.9.cloned.1.call-done, bf16[1024,3200]{1,0:T(8,128)(2,1)S(1)} %bitcast.175), kind=kOutput, calls=%fused_computation | convolution fusion | flops 13434880000 | bytes 50069504 | tf_op jit(solution)/shard_map/dot_general | solution.py:495
  961.8 6.8 fusion.101
  968.6 6.1 add_convert_fusion.1
  974.8 49.9 %collective-permute-done.17 = bf16[256,2816]{1,0:T(8,128)(2,1)} collective-permute-done((bf16[256,2816]{1,0:T(8,128)(2,1)}, bf16[256,2816]{1,0:T(8,128)(2,1)}, u32[]{:S(2)}, u32[]{:S(2)}) %collective-permute-start.17) | collective-permute-done | bytes 1441824 | tf_op jit(solution)/shard_map/ppermute | solution.py:745
  1028.0 6.0 fusion.92
  1034.1 3.4 convolution_add_fusion.1
  1040.6 3.4 fusion.96
  1051.4 3.4 convolution_add_fusion
  1057.2 26.4 %all-reduce.17 = (f32[4,2048]{1,0:T(4,128)S(1)}, f32[2,4]{1,0:T(2,128)S(1)}) all-reduce(f32[4,2048]{1,0:T(4,128)S(1)} %bitcast_reduce_fusion, f32[2,4]{1,0:T(2,128)S(1)} %bitcast.168), channel_id=1, replica_groups=mesh['dp'=8,'tensor'=4] {'dp'}, use_global_device_ids=true, to_apply=%region_17.18 | all-reduce | flops 8200 | bytes 65600 | tf_op jit(solution)/shard_map/psum | solution.py:754
  1085.3 4.8 collective-permute-done.14
  1090.1 37.2 %collective-permute-done.16 = bf16[256,2048]{1,0:T(8,128)(2,1)} collective-permute-done((bf16[256,2048]{1,0:T(8,128)(2,1)}, bf16[256,2048]{1,0:T(8,128)(2,1)}, u32[]{:S(2)}, u32[]{:S(2)}) %collective-permute-start.16) | collective-permute-done | bytes 1048608 | tf_op jit(solution)/shard_map/ppermute | solution.py:556
  1127.3 14.0 %collective-permute-done.15 = bf16[256,2048]{1,0:T(8,128)(2,1)} collective-permute-done((bf16[256,2048]{1,0:T(8,128)(2,1)}, bf16[256,2048]{1,0:T(8,128)(2,1)}, u32[]{:S(2)}, u32[]{:S(2)}) %collective-permute-start.15) | collective-permute-done | bytes 1048608 | tf_op jit(solution)/shard_map/ppermute | solution.py:556
  1141.3 5.8 fusion.43
  1147.1 39.3 %all-reduce.16 = (f32[2048]{0:T(1024)}, f32[256]{0:T(256)}, f32[2048]{0:T(1024)}) all-reduce(f32[2048]{0:T(1024)S(1)} %add.284, f32[256]{0:T(256)S(1)} %add_reduce_fusion, f32[2048]{0:T(1024)S(1)} %add.290), channel_id=1, replica_groups=mesh['dp'=8,'tensor'=4] {'dp','tensor'}, use_global_device_ids=true, to_apply=%region_13.14 | all-reduce | flops 4352 | bytes 34816 | tf_op jit(solution)/shard_map/psum | solution.py:755
  1186.5 4.9 fusion.64
  1199.9 8.3 convert_bitcast_fusion
  1208.2 12.0 copy.83
  1220.2 30.2 %all-reduce.21.cloned.1.call-done = (bf16[2048,3200]{1,0:T(8,128)(2,1)}, bf16[1024,2048]{1,0:T(8,128)(2,1)}) async-done(((bf16[2048,3200]{1,0:T(8,128)(2,1)}, bf16[1024,2048]{1,0:T(8,128)(2,1)}), (bf16[2048,3200]{1,0:T(8,128)(2,1)}, bf16[1024,2048]{1,0:T(8,128)(2,1)})) %all-reduce.21.cloned.1.call-update) | async-done | bytes 17301520 | tf_op jit(solution)/shard_map/psum | solution.py:751
  1252.5 6.7 convert_element_type.371
  1259.2 7.5 fusion.81
  1266.7 11.8 fusion.80
  1278.5 41.9 %all-gather.21.cloned.1.call-done = bf16[2048,2816]{1,0:T(8,128)(2,1)} async-done(((bf16[256,2816]{1,0:T(8,128)(2,1)}), bf16[2048,2816]{1,0:T(8,128)(2,1)}) %all-gather.21.cloned.1.call-update) | async-done | bytes 11534352 | tf_op jit(solution)/shard_map/all_gather | solution.py:564
  1320.4 11.1 fusion.82
  (380 shorter events, 121.5 us)
Async XLA Ops:
  8.0 162.3 %all-gather.9.cloned.1.call-start = ((), (), s32[]{:S(2)}) async-start(), calls=%async_computation.4 | async-start | bytes 5242880 | tf_op jit(solution)/shard_map/all_gather | solution.py:507
  12.9 244.7 %all-gather.11.cloned.1.call-start = ((), (), s32[]{:S(2)}) async-start(), calls=%async_computation.6 | async-start | bytes 5242880 | tf_op jit(solution)/shard_map/all_gather | solution.py:507
  35.5 206.5 %collective-permute-start.1 = (bf16[176,2048]{1,0:T(8,128)(2,1)}, bf16[176,2048]{1,0:T(8,128)(2,1)S(1)}, u32[]{:S(2)}, u32[]{:S(2)}) collective-permute-start(bf16[176,2048]{1,0:T(8,128)(2,1)} %constant_dynamic-slice_fusion.6), channel_id=1, source_target_pairs={{0,2},{1,3},{2,0},{3,1},{4,6},{5,7},{6,4},{7,5},{8,10},{9,11},{10,... | collective-permute-start | bytes 2162696 | tf_op jit(solution)/shard_map/ppermute | solution.py:627
  49.3 122.8 %copy-start.85 = (f32[4]{0:T(128)S(1)}, f32[4]{0:T(128)}, u32[]{:S(2)}) copy-start(f32[4]{0:T(128)} %param.32) | copy-start | bytes 52
  49.3 122.8 %copy-start.82 = (f32[4]{0:T(128)S(1)}, f32[4]{0:T(128)}, u32[]{:S(2)}) copy-start(f32[4]{0:T(128)} %param.33) | copy-start | bytes 52
  49.3 122.8 %copy-start.70 = (f32[4,1024]{1,0:T(4,128)S(1)}, f32[4,1024]{1,0:T(4,128)}, u32[]{:S(2)}) copy-start(f32[4,1024]{1,0:T(4,128)} %param.31) | copy-start | bytes 49156
  49.4 122.8 %copy-start.79 = (f32[4,512]{1,0:T(4,128)S(1)}, f32[4,512]{1,0:T(4,128)}, u32[]{:S(2)}) copy-start(f32[4,512]{1,0:T(4,128)} %param.30) | copy-start | bytes 24580
  49.4 122.8 %copy-start.80 = (f32[4,512]{1,0:T(4,128)S(1)}, f32[4,512]{1,0:T(4,128)}, u32[]{:S(2)}) copy-start(f32[4,512]{1,0:T(4,128)} %param.29) | copy-start | bytes 24580
  50.6 191.4 %collective-permute-start = (bf16[256,2816]{1,0:T(8,128)(2,1)}, bf16[256,2816]{1,0:T(8,128)(2,1)}, u32[]{:S(2)}, u32[]{:S(2)}) collective-permute-start(bf16[256,2816]{1,0:T(8,128)(2,1)} %constant_dynamic-slice_fusion.7), channel_id=1, source_target_pairs={{0,2},{1,3},{2,0},{3,1},{4,6},{5,7},{6,4},{7,5},{8,10},{9,11},{10,... | collective-permute-start | bytes 4325384 | tf_op jit(solution)/shard_map/ppermute | solution.py:627
  170.4 207.5 %reduce-scatter.5.cloned.1.call-start = ((), (), s32[]{:S(2)}) async-start(), calls=%async_computation.5 | async-start | bytes 5242880 | tf_op jit(solution)/shard_map/reduce_scatter | solution.py:511
  172.1 22.3 %copy-start = (f32[1024,128]{1,0:T(8,128)}, f32[1024,128]{1,0:T(8,128)S(1)}, u32[]{:S(2)}) copy-start(f32[1024,128]{1,0:T(8,128)S(1)} %pad.63.aux_ref) | copy-start | bytes 1572868
  172.2 107.4 %copy-start.14 = (f32[8,128]{1,0:T(8,128)}, f32[8,128]{1,0:T(8,128)S(1)}, u32[]{:S(2)}) copy-start(f32[8,128]{1,0:T(8,128)S(1)} %select_maximum_fusion.2.params_ref) | copy-start | bytes 12292
  172.2 22.2 %copy-start.81 = (f32[256]{0:T(256)S(1)}, f32[256]{0:T(256)}, u32[]{:S(2)}) copy-start(f32[256]{0:T(256)} %param.34) | copy-start | bytes 3076
  194.4 85.2 %copy-start.12 = (f32[8,256]{1,0:T(8,128)}, f32[8,256]{1,0:T(8,128)S(1)}, u32[]{:S(2)}) copy-start(f32[8,256]{1,0:T(8,128)S(1)} %broadcast_in_dim.5.gain_ref) | copy-start | bytes 24580
  251.6 239.1 %reduce-scatter.7.cloned.1.call-start = ((), (), s32[]{:S(2)}) async-start(), calls=%async_computation.7 | async-start | bytes 5242880 | tf_op jit(solution)/shard_map/reduce_scatter | solution.py:511
  255.6 71.5 %collective-permute-start.2 = (bf16[256,2048]{1,0:T(8,128)(2,1)}, bf16[256,2048]{1,0:T(8,128)(2,1)}, u32[]{:S(2)}, u32[]{:S(2)}) collective-permute-start(bf16[256,2048]{1,0:T(8,128)(2,1)} %get-tuple-element.72), channel_id=1, source_target_pairs={{0,1},{1,0},{2,3},{3,2},{4,5},{5,4},{6,7},{7,6},{8,9},{9,8},{10,11... | collective-permute-start | bytes 3145736 | tf_op jit(solution)/shard_map/ppermute | solution.py:528
  255.6 114.5 %collective-permute-start.3 = (bf16[256,2048]{1,0:T(8,128)(2,1)}, bf16[256,2048]{1,0:T(8,128)(2,1)}, u32[]{:S(2)}, u32[]{:S(2)}) collective-permute-start(bf16[256,2048]{1,0:T(8,128)(2,1)} %get-tuple-element.73), channel_id=1, source_target_pairs={{0,1},{1,0},{2,3},{3,2},{4,5},{5,4},{6,7},{7,6},{8,9},{9,8},{10,11... | collective-permute-start | bytes 3145736 | tf_op jit(solution)/shard_map/ppermute | solution.py:528
  279.6 90.6 %copy-start.83 = (bf16[1024,2048]{1,0:T(8,128)(2,1)S(1)}, bf16[1024,2048]{1,0:T(8,128)(2,1)}, u32[]{:S(2)}) copy-start(bf16[1024,2048]{1,0:T(8,128)(2,1)} %param.35) | copy-start | bytes 12582916
  327.1 43.0 %copy-start.18 = (bf16[1024,1024]{1,0:T(8,128)(2,1)}, bf16[1024,1024]{1,0:T(8,128)(2,1)S(1)}, u32[]{:S(2)}) copy-start(bf16[1024,1024]{1,0:T(8,128)(2,1)S(1)} %get-tuple-element.110) | copy-start | bytes 6291460
  376.2 119.3 %all-gather.13.cloned.1.call-start = ((), (), s32[]{:S(2)}) async-start(), calls=%async_computation.8 | async-start | bytes 12976128 | tf_op jit(solution)/shard_map/all_gather | solution.py:564
  376.8 131.4 %all-gather.15.cloned.1.call-start = ((), (), s32[]{:S(2)}) async-start(), calls=%async_computation.9 | async-start | bytes 6488064 | tf_op jit(solution)/shard_map/all_gather | solution.py:564
  377.4 307.3 %all-gather.17.cloned.1.call-start = ((), (), s32[]{:S(2)}) async-start(), calls=%async_computation.10 | async-start | bytes 5242880 | tf_op jit(solution)/shard_map/all_gather | solution.py:507
  379.9 81.8 %slice-start.2 = ((s8[11534336]{0:T(1024)(128)(4,1)}), s8[4194304]{0:T(1024)(128)(4,1)S(1)}, s32[]{:S(2)}) async-start(s8[11534336]{0:T(1024)(128)(4,1)} %bitcast.144), calls=%async_computation.19 | async-start | bytes 8388608
  380.2 182.7 %copy-start.65 = (f32[256]{0:T(256)}, f32[256]{0:T(256)S(1)}, u32[]{:S(2)}) copy-start(f32[256]{0:T(256)S(1)} %add_rsqrt_fusion.1) | copy-start | bytes 3076
  381.7 80.0 %slice-start.3 = ((s8[11534336]{0:T(1024)(128)(4,1)}), s8[4194304]{0:T(1024)(128)(4,1)S(1)}, s32[]{:S(2)}) async-start(s8[11534336]{0:T(1024)(128)(4,1)} %bitcast.144), calls=%async_computation.20 | async-start | bytes 8388608
  381.9 79.7 %copy-start.36 = (bf16[256,2048]{1,0:T(8,128)(2,1)}, bf16[256,2048]{1,0:T(8,128)(2,1)S(1)}, u32[]{:S(2)}) copy-start(bf16[256,2048]{1,0:T(8,128)(2,1)S(1)} %multiply_convert_fusion.13) | copy-start | bytes 3145732
  381.9 79.7 %slice-start.4 = ((s8[11534336]{0:T(1024)(128)(4,1)}), s8[3145728]{0:T(1024)(128)(4,1)S(1)}, s32[]{:S(2)}) async-start(s8[11534336]{0:T(1024)(128)(4,1)} %bitcast.144), calls=%async_computation.21 | async-start | bytes 6291456
  381.9 78.1 %collective-permute-start.4 = (bf16[256,2048]{1,0:T(8,128)(2,1)S(1)}, bf16[256,2048]{1,0:T(8,128)(2,1)S(1)}, u32[]{:S(2)}, u32[]{:S(2)}) collective-permute-start(bf16[256,2048]{1,0:T(8,128)(2,1)S(1)} %multiply_convert_fusion.13), channel_id=1, source_target_pairs={{0,1},{1,0},{2,3},{3,2},{4,5},{5,4},{6,7},{7,6},{8,9},{9,8},{10,11... | collective-permute-start | bytes 3145736 | tf_op jit(solution)/shard_map/ppermute | solution.py:528
  495.5 40.3 %collective-permute-start.6 = (bf16[256,2048]{1,0:T(8,128)(2,1)}, bf16[256,2048]{1,0:T(8,128)(2,1)}, u32[]{:S(2)}, u32[]{:S(2)}) collective-permute-start(bf16[256,2048]{1,0:T(8,128)(2,1)} %multiply_convert_fusion.12), channel_id=1, source_target_pairs={{0,1},{1,0},{2,3},{3,2},{4,5},{5,4},{6,7},{7,6},{8,9},{9,8},{10,11... | collective-permute-start | bytes 3145736 | tf_op jit(solution)/shard_map/ppermute | solution.py:528
  519.1 18.3 %slice-start.5 = ((s8[11534336]{0:T(1024)(128)(4,1)}), s8[4194304]{0:T(1024)(128)(4,1)S(1)}, s32[]{:S(2)}) async-start(s8[11534336]{0:T(1024)(128)(4,1)} %bitcast.146), calls=%async_computation.22 | async-start | bytes 8388608
  519.2 18.4 %slice-start.6 = ((s8[11534336]{0:T(1024)(128)(4,1)}), s8[4194304]{0:T(1024)(128)(4,1)S(1)}, s32[]{:S(2)}) async-start(s8[11534336]{0:T(1024)(128)(4,1)} %bitcast.146), calls=%async_computation.23 | async-start | bytes 8388608
  519.2 18.4 %slice-start.7 = ((s8[11534336]{0:T(1024)(128)(4,1)}), s8[3145728]{0:T(1024)(128)(4,1)S(1)}, s32[]{:S(2)}) async-start(s8[11534336]{0:T(1024)(128)(4,1)} %bitcast.146), calls=%async_computation.24 | async-start | bytes 6291456
  533.8 25.0 %collective-permute-start.7 = (bf16[256,2048]{1,0:T(8,128)(2,1)}, bf16[256,2048]{1,0:T(8,128)(2,1)}, u32[]{:S(2)}, u32[]{:S(2)}) collective-permute-start(bf16[256,2048]{1,0:T(8,128)(2,1)} %slice.406), channel_id=1, source_target_pairs={{0,1},{1,0},{2,3},{3,2},{4,5},{5,4},{6,7},{7,6},{8,9},{9,8},{10,11... | collective-permute-start | bytes 3145736 | tf_op jit(solution)/shard_map/ppermute | solution.py:540
  565.7 126.8 %reduce-scatter.9.cloned.1.call-start = ((), (), s32[]{:S(2)}) async-start(), calls=%async_computation.11 | async-start | bytes 12976128 | tf_op jit(solution)/shard_map/reduce_scatter | solution.py:683
  607.7 187.0 %all-gather.19.cloned.1.call-start = ((), (), s32[]{:S(2)}) async-start(), calls=%async_computation.12 | async-start | bytes 5242880 | tf_op jit(solution)/shard_map/all_gather | solution.py:507
  635.0 42.4 %collective-permute-start.13 = (bf16[256,2048]{1,0:T(8,128)(2,1)}, bf16[256,2048]{1,0:T(8,128)(2,1)}, u32[]{:S(2)}, u32[]{:S(2)}) collective-permute-start(bf16[256,2048]{1,0:T(8,128)(2,1)} %slice.404), channel_id=1, source_target_pairs={{0,1},{1,0},{2,3},{3,2},{4,5},{5,4},{6,7},{7,6},{8,9},{9,8},{10,11... | collective-permute-start | bytes 3145736 | tf_op jit(solution)/shard_map/ppermute | solution.py:540
  683.9 275.2 %reduce-scatter.11.cloned.1.call-start = ((), (), s32[]{:S(2)}) async-start(), calls=%async_computation.13 | async-start | bytes 25952256 | tf_op jit(solution)/shard_map/reduce_scatter | solution.py:683
  684.6 515.3 %all-gather.23.cloned.1.call-start = ((), (), s32[]{:S(2)}) async-start(), calls=%async_computation.15 | async-start | bytes 6488064 | tf_op jit(solution)/shard_map/all_gather | solution.py:564
  693.8 13.1 copy-start.1
  693.8 13.1 copy-start.9
  693.8 13.1 copy-start.13
  693.8 76.8 %collective-permute-start.9 = (bf16[256,1408]{1,0:T(8,128)(2,1)S(1)}, bf16[256,1408]{1,0:T(8,128)(2,1)S(1)}, u32[]{:S(2)}, u32[]{:S(2)}) collective-permute-start(bf16[256,1408]{1,0:T(8,128)(2,1)S(1)} %slice.276), channel_id=1, source_target_pairs={{0,2},{1,3},{2,0},{3,1},{4,6},{5,7},{6,4},{7,5},{8,10},{9,11},{10,... | collective-permute-start | bytes 2162696 | tf_op jit(solution)/shard_map/ppermute | solution.py:720
  798.5 68.8 %collective-permute-start.10 = (bf16[256,2048]{1,0:T(8,128)(2,1)}, bf16[256,2048]{1,0:T(8,128)(2,1)}, u32[]{:S(2)}, u32[]{:S(2)}) collective-permute-start(bf16[256,2048]{1,0:T(8,128)(2,1)} %get-tuple-element.215), channel_id=1, source_target_pairs={{0,1},{1,2},{2,3},{3,0},{4,5},{5,6},{6,7},{7,4},{8,9},{9,10},{10,1... | collective-permute-start | bytes 3145736 | tf_op jit(solution)/shard_map/ppermute | solution.py:556
  798.5 68.8 %collective-permute-start.12 = (bf16[256,2048]{1,0:T(8,128)(2,1)}, bf16[256,2048]{1,0:T(8,128)(2,1)}, u32[]{:S(2)}, u32[]{:S(2)}) collective-permute-start(bf16[256,2048]{1,0:T(8,128)(2,1)} %get-tuple-element.216), channel_id=1, source_target_pairs={{0,3},{1,0},{2,1},{3,2},{4,7},{5,4},{6,5},{7,6},{8,11},{9,8},{10,9... | collective-permute-start | bytes 3145736 | tf_op jit(solution)/shard_map/ppermute | solution.py:556
  802.3 88.1 %collective-permute-start.11 = (bf16[256,2048]{1,0:T(8,128)(2,1)}, bf16[256,2048]{1,0:T(8,128)(2,1)}, u32[]{:S(2)}, u32[]{:S(2)}) collective-permute-start(bf16[256,2048]{1,0:T(8,128)(2,1)} %get-tuple-element.217), channel_id=1, source_target_pairs={{0,2},{1,3},{2,0},{3,1},{4,6},{5,7},{6,4},{7,5},{8,10},{9,11},{10,... | collective-permute-start | bytes 3145736 | tf_op jit(solution)/shard_map/ppermute | solution.py:556
  803.3 447.1 %all-reduce.21.cloned.1.call-start = ((), (), s32[]{:S(2)}) async-start(), calls=%async_computation.16 | async-start | bytes 34603008 | tf_op jit(solution)/shard_map/psum | solution.py:751
  890.4 24.2 %slice-start.12 = ((s8[6553600]{0:T(1024)(128)(4,1)}), s8[4194304]{0:T(1024)(128)(4,1)S(1)}, s32[]{:S(2)}) async-start(s8[6553600]{0:T(1024)(128)(4,1)} %bitcast.176), calls=%async_computation.29 | async-start | bytes 8388608
  894.8 19.9 %slice-start.13 = ((s8[6553600]{0:T(1024)(128)(4,1)}), s8[2359296]{0:T(1024)(128)(4,1)S(1)}, s32[]{:S(2)}) async-start(s8[6553600]{0:T(1024)(128)(4,1)} %bitcast.176), calls=%async_computation.30 | async-start | bytes 4718592
  894.8 41.4 %slice-start.10 = ((s8[6553600]{0:T(1024)(128)(4,1)}), s8[4194304]{0:T(1024)(128)(4,1)S(1)}, s32[]{:S(2)}) async-start(s8[6553600]{0:T(1024)(128)(4,1)} %bitcast.174), calls=%async_computation.27 | async-start | bytes 8388608
  914.6 21.5 %slice-start.11 = ((s8[6553600]{0:T(1024)(128)(4,1)}), s8[2359296]{0:T(1024)(128)(4,1)S(1)}, s32[]{:S(2)}) async-start(s8[6553600]{0:T(1024)(128)(4,1)} %bitcast.174), calls=%async_computation.28 | async-start | bytes 4718592
  961.8 62.8 %collective-permute-start.17 = (bf16[256,2816]{1,0:T(8,128)(2,1)}, bf16[256,2816]{1,0:T(8,128)(2,1)}, u32[]{:S(2)}, u32[]{:S(2)}) collective-permute-start(bf16[256,2816]{1,0:T(8,128)(2,1)} %slice.279), channel_id=1, source_target_pairs={{0,2},{1,3},{2,0},{3,1},{4,6},{5,7},{6,4},{7,5},{8,10},{9,11},{10,... | collective-permute-start | bytes 4325384 | tf_op jit(solution)/shard_map/ppermute | solution.py:745
  1024.7 295.7 %all-gather.21.cloned.1.call-start = ((), (), s32[]{:S(2)}) async-start(), calls=%async_computation.14 | async-start | bytes 12976128 | tf_op jit(solution)/shard_map/all_gather | solution.py:564
  1040.6 145.9 %collective-permute-start.5 = (bf16[256,2048]{1,0:T(8,128)(2,1)}, bf16[256,2048]{1,0:T(8,128)(2,1)}, u32[]{:S(2)}, u32[]{:S(2)}) collective-permute-start(bf16[256,2048]{1,0:T(8,128)(2,1)} %slice.407), channel_id=1, source_target_pairs={{0,1},{1,0},{2,3},{3,2},{4,5},{5,4},{6,7},{7,6},{8,9},{9,8},{10,11... | collective-permute-start | bytes 3145736 | tf_op jit(solution)/shard_map/ppermute | solution.py:540
  1045.9 44.2 %collective-permute-start.14 = (bf16[256,2048]{1,0:T(8,128)(2,1)}, bf16[256,2048]{1,0:T(8,128)(2,1)}, u32[]{:S(2)}, u32[]{:S(2)}) collective-permute-start(bf16[256,2048]{1,0:T(8,128)(2,1)} %get-tuple-element.212), channel_id=1, source_target_pairs={{0,1},{1,2},{2,3},{3,0},{4,5},{5,6},{6,7},{7,4},{8,9},{9,10},{10,1... | collective-permute-start | bytes 3145736 | tf_op jit(solution)/shard_map/ppermute | solution.py:556
  1047.9 79.4 %collective-permute-start.16 = (bf16[256,2048]{1,0:T(8,128)(2,1)}, bf16[256,2048]{1,0:T(8,128)(2,1)}, u32[]{:S(2)}, u32[]{:S(2)}) collective-permute-start(bf16[256,2048]{1,0:T(8,128)(2,1)} %get-tuple-element.213), channel_id=1, source_target_pairs={{0,3},{1,0},{2,1},{3,2},{4,7},{5,4},{6,5},{7,6},{8,11},{9,8},{10,9... | collective-permute-start | bytes 3145736 | tf_op jit(solution)/shard_map/ppermute | solution.py:556
  1049.9 91.4 %copy-start.60 = (f32[2048]{0:T(1024)S(1)}, f32[2048]{0:T(1024)}, u32[]{:S(2)}) copy-start(f32[2048]{0:T(1024)} %param.23) | copy-start | bytes 24580
  1049.9 91.4 %copy-start.72 = (f32[256]{0:T(256)S(1)}, f32[256]{0:T(256)}, u32[]{:S(2)}) copy-start(f32[256]{0:T(256)} %copy-done.71) | copy-start | bytes 3076
  1049.9 91.4 %copy-start.74 = (f32[256]{0:T(256)S(1)}, f32[256]{0:T(256)}, u32[]{:S(2)}) copy-start(f32[256]{0:T(256)} %copy-done.73) | copy-start | bytes 3076
  1049.9 91.3 %collective-permute-start.15 = (bf16[256,2048]{1,0:T(8,128)(2,1)}, bf16[256,2048]{1,0:T(8,128)(2,1)}, u32[]{:S(2)}, u32[]{:S(2)}) collective-permute-start(bf16[256,2048]{1,0:T(8,128)(2,1)} %get-tuple-element.214), channel_id=1, source_target_pairs={{0,2},{1,3},{2,0},{3,1},{4,6},{5,7},{6,4},{7,5},{8,10},{9,11},{10,... | collective-permute-start | bytes 3145736 | tf_op jit(solution)/shard_map/ppermute | solution.py:556
  1056.1 135.3 %collective-permute-start.8 = (bf16[256,2048]{1,0:T(8,128)(2,1)}, bf16[256,2048]{1,0:T(8,128)(2,1)}, u32[]{:S(2)}, u32[]{:S(2)}) collective-permute-start(bf16[256,2048]{1,0:T(8,128)(2,1)} %slice.405), channel_id=1, source_target_pairs={{0,1},{1,0},{2,3},{3,2},{4,5},{5,4},{6,7},{7,6},{8,9},{9,8},{10,11... | collective-permute-start | bytes 3145736 | tf_op jit(solution)/shard_map/ppermute | solution.py:540
  1085.3 101.2 %copy-start.22 = (f32[256,2048]{1,0:T(8,128)S(1)}, f32[256,2048]{1,0:T(8,128)}, u32[]{:S(2)}) copy-start(f32[256,2048]{1,0:T(8,128)} %copy-done.20) | copy-start | bytes 6291460
  1085.3 101.3 %copy-start.59 = (f32[2048]{0:T(1024)S(1)}, f32[2048]{0:T(1024)}, u32[]{:S(2)}) copy-start(f32[2048]{0:T(1024)} %param.36) | copy-start | bytes 24580
  1085.3 101.3 %copy-start.66 = (f32[256]{0:T(256)S(1)}, f32[256]{0:T(256)}, u32[]{:S(2)}) copy-start(f32[256]{0:T(256)} %copy-done.65) | copy-start | bytes 3076
  1085.3 101.3 %copy-start.76 = (f32[256]{0:T(256)S(1)}, f32[256]{0:T(256)}, u32[]{:S(2)}) copy-start(f32[256]{0:T(256)} %copy-done.75) | copy-start | bytes 3076
  (75 other events, 332.1 us)
Sparse Core Ops, SparseCore 0:
  13.0 157.3 all-gather.8
  172.5 84.1 all-gather.10
  259.6 109.5 reduce-scatter.4
  376.4 97.3 reduce-scatter.6
  565.8 83.4 all-gather.16
  684.0 110.6 all-gather.18
Sparse Core Ops, SparseCore 1:
  378.6 65.6 all-gather.12
  446.1 43.1 all-gather.14
  607.8 84.7 reduce-scatter.8
  696.2 145.7 reduce-scatter.10
  843.8 43.1 all-gather.22
  1024.8 225.6 all-reduce.20
  1252.8 67.6 all-gather.20
